TPU v7x, 32 devices: a whole 2x2x4 slice. The times are simulated.
32 devices in a mesh: stream: 2 (over x), dp: 16 (over z, y, core).
Axes of the slice: x: 2, y: 2, z: 4, core: 2. Of those that a mesh axis runs over, the one named last changes fastest.
Arguments:
- text_states: bfloat16 [8192, 768], P(('stream', 'dp')), may hold values from -6 to 6
- image_states: bfloat16 [2304, 1024], P(('stream', 'dp')), may hold values from -6 to 6
- caption_lengths: int32 [64], P(('stream', 'dp')), may hold values from 8 to 128, as said below
- text_query: bfloat16 [768, 1024], replicated, may hold values from -0.21875 to 0.21875
- text_keyval: bfloat16 [768, 2048], replicated, may hold values from -0.21875 to 0.21875
- text_attend: bfloat16 [1024, 768], replicated, may hold values from -0.75 to 0.75
- text_up: bfloat16 [768, 3072], replicated, may hold values from -0.21875 to 0.21875
- text_down: bfloat16 [3072, 768], replicated, may hold values from -0.109375 to 0.109375
- text_qkv: bfloat16 [768, 2304], replicated, may hold values from -0.21875 to 0.21875
- text_output: bfloat16 [768, 768], replicated, may hold values from -0.875 to 0.875
- text_gains: float32 [3, 768], replicated, may hold values from 0.5 to 1.5
- image_query: bfloat16 [1024, 1024], replicated, may hold values from -0.1875 to 0.1875
- image_keyval: bfloat16 [1024, 2048], replicated, may hold values from -0.1875 to 0.1875
- image_attend: bfloat16 [1024, 1024], replicated, may hold values from -0.75 to 0.75
- image_up: bfloat16 [1024, 1024], replicated, may hold values from -0.1875 to 0.1875
- image_down: bfloat16 [1024, 1024], replicated, may hold values from -0.1875 to 0.1875
- image_qkv: bfloat16 [1024, 3072], replicated, may hold values from -0.1875 to 0.1875
- image_output: bfloat16 [1024, 1024], replicated, may hold values from -0.75 to 0.75
- image_gains: float32 [3, 1024], replicated, may hold values from 0.5 to 1.5
- text_cotangent: bfloat16 [8192, 768], P(('stream', 'dp')), may hold values from -6 to 6
- image_cotangent: bfloat16 [2304, 1024], P(('stream', 'dp')), may hold values from -6 to 6
Outputs:
- text_result: bfloat16 [8192, 768], P(('stream', 'dp'))
- image_result: bfloat16 [2304, 1024], P(('stream', 'dp'))
- text_grad: bfloat16 [8192, 768], P(('stream', 'dp'))
- image_grad: bfloat16 [2304, 1024], P(('stream', 'dp'))
- text_weight_grads: float32 [10223616], P(('stream', 'dp'))
- image_weight_grads: float32 [10485760], P(('stream', 'dp'))
- text_gain_grads: float32 [3, 768], replicated
- image_gain_grads: float32 [3, 1024], replicated
Inputs may be any that keep to these rules, and one draw needn't show every extreme that they name: `caption_lengths`: on every device the first of its pairs has a caption of 128 tokens.
All inputs are finite; a program needn't handle non-finite values.
Results may differ from a plain program's by a relative error of at most 0.02.
Values may be sent and summed in bfloat16 or wider, within the bound.
No kernel may reach another device: no remote copies, remote signals or barrier semaphores. Data moves between devices by JAX's collectives and lax.ppermute only.
A program may use at most 448 MiB of HBM per device.

v0:
```python
import jax
import jax.numpy as jnp
from jax import lax
from jax.sharding import PartitionSpec as P

D_T = 768
H_T = 12
D_I = 1024
H_I = 8
D_C = 1024
H_C = 8


masked_score = -1e30


def swapped(block, axis, apart):
    count = lax.axis_size(axis)
    route = []
    for low in range(count):
        high = low | 1 << apart
        if high != low and high < count:
            route += [(low, high), (high, low)]
    return lax.ppermute(block, axis, route)


def matmul(left_side, right_side):
    return jnp.dot(left_side, right_side, preferred_element_type=jnp.float32)


def matmul_tn(left_side, right_side):
    return lax.dot_general(
        left_side, right_side, (((0,), (0,)), ((), ())), preferred_element_type=jnp.float32
    )


def matmul_nt(left_side, right_side):
    return lax.dot_general(
        left_side, right_side, (((1,), (1,)), ((), ())), preferred_element_type=jnp.float32
    )


def layer_norm(tensor, gain_row):
    centred = tensor - jnp.mean(tensor, axis=-1, keepdims=True)
    inverse = lax.rsqrt(jnp.mean(centred * centred, axis=-1, keepdims=True) + 1e-05)
    return centred * inverse * gain_row


def gelu_exact(tensor):
    return jax.nn.gelu(tensor, approximate=False)


def masked_scores(queries, key_rows, keymask, scaling):
    scores = (
        jnp.einsum("bqhd,bkhd->bhqk", queries, key_rows, preferred_element_type=jnp.float32)
        * scaling
    )
    if keymask is None:
        return scores
    return jnp.where(keymask[:, None, None, :], scores, masked_score)


def attend_forward(queries, key_rows, value_rows, keymask, scaling):
    scores = masked_scores(queries, key_rows, keymask, scaling)
    highest = jnp.max(scores, axis=-1, keepdims=True)
    logsum = highest + jnp.log(jnp.sum(jnp.exp(scores - highest), axis=-1, keepdims=True))
    weights_low = jnp.exp(scores - logsum).astype(jnp.bfloat16)
    context = jnp.einsum(
        "bhqk,bkhd->bqhd", weights_low, value_rows, preferred_element_type=jnp.float32
    )
    return (context, logsum)


def attend_backward(queries, key_rows, value_rows, keymask, scaling, logsum, grad_context):
    weights = jnp.exp(masked_scores(queries, key_rows, keymask, scaling) - logsum)
    grad_values = jnp.einsum(
        "bhqk,bqhd->bkhd",
        weights.astype(jnp.bfloat16),
        grad_context,
        preferred_element_type=jnp.float32,
    )
    grad_weights = jnp.einsum(
        "bqhd,bkhd->bhqk", grad_context, value_rows, preferred_element_type=jnp.float32
    )
    inner_sum = jnp.sum(weights * grad_weights, axis=-1, keepdims=True)
    grad_scores = (weights * (grad_weights - inner_sum)).astype(jnp.bfloat16)
    grad_queries = (
        jnp.einsum("bhqk,bkhd->bqhd", grad_scores, key_rows, preferred_element_type=jnp.float32)
        * scaling
    )
    grad_keys = (
        jnp.einsum("bhqk,bqhd->bkhd", grad_scores, queries, preferred_element_type=jnp.float32)
        * scaling
    )
    return (grad_queries, grad_keys, grad_values)


def rest_forward(states, context_low, weights, gain_rows, head_count, seq_len, keymask):
    attend_proj, up_proj, down_proj, qkv_proj, output_proj = weights
    num_rows, model_width = states.shape
    head_size = model_width // head_count
    before = states.astype(jnp.float32) + matmul(context_low, attend_proj)
    first_norm = layer_norm(before, gain_rows[0])
    first_low = first_norm.astype(jnp.bfloat16)
    hidden_pre = matmul(first_low, up_proj)
    hidden_low = gelu_exact(hidden_pre).astype(jnp.bfloat16)
    middle = first_norm + matmul(hidden_low, down_proj)
    second_norm = layer_norm(middle, gain_rows[1])
    second_low = second_norm.astype(jnp.bfloat16)
    packed = (
        matmul(second_low, qkv_proj)
        .astype(jnp.bfloat16)
        .reshape(num_rows // seq_len, seq_len, 3, head_count, head_size)
    )
    attended, logsum = attend_forward(
        packed[:, :, 0], packed[:, :, 1], packed[:, :, 2], keymask, head_size ** (-0.5)
    )
    attended_low = attended.reshape(num_rows, model_width).astype(jnp.bfloat16)
    closing = second_norm + matmul(attended_low, output_proj)
    kept_values = (
        context_low,
        before,
        first_low,
        hidden_pre,
        hidden_low,
        middle,
        second_low,
        packed,
        logsum,
        attended_low,
        closing,
    )
    return (layer_norm(closing, gain_rows[2]), kept_values)


def rest_backward(weights, gain_rows, head_count, keymask, kept_values, grad_result):
    attend_proj, up_proj, down_proj, qkv_proj, output_proj = weights
    (
        context_low,
        before,
        first_low,
        hidden_pre,
        hidden_low,
        middle,
        second_low,
        packed,
        logsum,
        attended_low,
        closing,
    ) = kept_values
    num_rows, model_width = closing.shape
    head_size = model_width // head_count
    _, pull_back = jax.vjp(layer_norm, closing, gain_rows[2])
    grad_closing, grad_gain_last = pull_back(grad_result)
    grad_closing_low = grad_closing.astype(jnp.bfloat16)
    grad_output = matmul_tn(attended_low, grad_closing_low)
    grad_attended = matmul_nt(grad_closing_low, output_proj).astype(jnp.bfloat16)
    grad_attended = grad_attended.reshape(packed.shape[0], packed.shape[1], head_count, head_size)
    grad_queries, grad_keys, grad_values = attend_backward(
        packed[:, :, 0],
        packed[:, :, 1],
        packed[:, :, 2],
        keymask,
        head_size ** (-0.5),
        logsum,
        grad_attended,
    )
    grad_packed = (
        jnp.stack((grad_queries, grad_keys, grad_values), axis=2)
        .reshape(num_rows, 3 * model_width)
        .astype(jnp.bfloat16)
    )
    grad_qkv = matmul_tn(second_low, grad_packed)
    grad_second = grad_closing + matmul_nt(grad_packed, qkv_proj)
    _, pull_back = jax.vjp(layer_norm, middle, gain_rows[1])
    grad_middle, grad_gain_mid = pull_back(grad_second)
    grad_middle_low = grad_middle.astype(jnp.bfloat16)
    grad_down = matmul_tn(hidden_low, grad_middle_low)
    _, pull_back = jax.vjp(gelu_exact, hidden_pre)
    (grad_hidden,) = pull_back(matmul_nt(grad_middle_low, down_proj))
    grad_hidden_low = grad_hidden.astype(jnp.bfloat16)
    grad_up = matmul_tn(first_low, grad_hidden_low)
    grad_first = grad_middle + matmul_nt(grad_hidden_low, up_proj)
    _, pull_back = jax.vjp(layer_norm, before, gain_rows[0])
    grad_before, grad_gain_first = pull_back(grad_first)
    grad_before_low = grad_before.astype(jnp.bfloat16)
    grad_attend = matmul_tn(context_low, grad_before_low)
    grad_context = matmul_nt(grad_before_low, attend_proj).astype(jnp.bfloat16)
    gain_grads = jnp.stack((grad_gain_first, grad_gain_mid, grad_gain_last))
    return (
        grad_before,
        grad_context,
        (grad_attend, grad_up, grad_down, grad_qkv, grad_output),
        gain_grads,
    )


def stream_work(
    rows,
    cotangent,
    query_proj,
    weights,
    gains,
    head_count,
    seq_len,
    self_mask,
    far_kv,
    far_len,
    far_mask,
    pair_total,
):
    co_size = D_C // H_C
    scaling = co_size ** (-0.5)
    row_total = rows.shape[0]
    queries = (
        matmul(rows, query_proj).astype(jnp.bfloat16).reshape(pair_total, seq_len, H_C, co_size)
    )
    kv_heads = far_kv.reshape(pair_total, far_len, 2, H_C, co_size)
    context, logsum = attend_forward(
        queries, kv_heads[:, :, 0], kv_heads[:, :, 1], far_mask, scaling
    )
    context_low = context.reshape(row_total, D_C).astype(jnp.bfloat16)
    normed, kept = rest_forward(rows, context_low, weights, gains, head_count, seq_len, self_mask)
    back, grad_context, grads, gain_part = rest_backward(
        weights, gains, head_count, self_mask, kept, cotangent
    )
    grad_queries, grad_keys, grad_values = attend_backward(
        queries,
        kv_heads[:, :, 0],
        kv_heads[:, :, 1],
        far_mask,
        scaling,
        logsum,
        grad_context.reshape(pair_total, seq_len, H_C, co_size),
    )
    grad_query_low = grad_queries.reshape(row_total, D_C).astype(jnp.bfloat16)
    grad_in = back + matmul_nt(grad_query_low, query_proj)
    grad_qproj = matmul_tn(rows, grad_query_low)
    far_grads = (
        jnp.stack((grad_keys, grad_values), axis=2)
        .reshape(pair_total * far_len, 2 * D_C)
        .astype(jnp.bfloat16)
    )
    flat = jnp.concatenate([grad_qproj.reshape(-1)] + [member.reshape(-1) for member in grads])
    return (normed, grad_in, far_grads, flat, gain_part)


def local(
    text_states,
    image_states,
    caption_lengths,
    text_query,
    text_keyval,
    text_attend,
    text_up,
    text_down,
    text_qkv,
    text_output,
    text_gains,
    image_query,
    image_keyval,
    image_attend,
    image_up,
    image_down,
    image_qkv,
    image_output,
    image_gains,
    text_cotangent,
    image_cotangent,
):
    pair_count = caption_lengths.shape[0]
    text_count = text_states.shape[0]
    text_len = text_count // pair_count
    region_count = image_states.shape[0] // pair_count
    positions = lax.broadcasted_iota(jnp.int32, (pair_count, text_len), 1)
    text_valid = positions < caption_lengths[:, None]
    valid_low = text_valid.astype(jnp.bfloat16)
    text_weights = (text_attend, text_up, text_down, text_qkv, text_output)
    image_weights = (image_attend, image_up, image_down, image_qkv, image_output)
    text_kv = matmul(text_states, text_keyval).astype(jnp.bfloat16)
    image_kv = matmul(image_states, image_keyval).astype(jnp.bfloat16)
    far_text_kv, far_image_kv, far_valid = swapped((text_kv, image_kv, valid_low), "stream", 0)
    far_mask = far_valid > 0.5
    row_mask = text_valid.reshape(text_count, 1).astype(jnp.float32)
    text_normed, text_in, grad_far_image_kv, text_part, text_gain_part = stream_work(
        text_states,
        text_cotangent.astype(jnp.float32) * row_mask,
        text_query,
        text_weights,
        text_gains,
        H_T,
        text_len,
        text_valid,
        far_image_kv,
        region_count,
        None,
        pair_count,
    )
    image_normed, image_in, grad_far_text_kv, image_part, image_gain_part = stream_work(
        image_states,
        image_cotangent.astype(jnp.float32),
        image_query,
        image_weights,
        image_gains,
        H_I,
        region_count,
        None,
        far_text_kv,
        text_len,
        far_mask,
        pair_count,
    )
    grad_text_kv, grad_image_kv = swapped((grad_far_text_kv, grad_far_image_kv), "stream", 0)
    text_result = (text_normed * row_mask).astype(jnp.bfloat16)
    image_result = image_normed.astype(jnp.bfloat16)
    text_grad = (text_in + matmul_nt(grad_text_kv, text_keyval)).astype(jnp.bfloat16)
    image_grad = (image_in + matmul_nt(grad_image_kv, image_keyval)).astype(jnp.bfloat16)
    text_flat = jnp.concatenate(
        (
            text_part[: D_T * D_C],
            matmul_tn(text_states, grad_text_kv).reshape(-1),
            text_part[D_T * D_C :],
        )
    )
    image_flat = jnp.concatenate(
        (
            image_part[: D_I * D_C],
            matmul_tn(image_states, grad_image_kv).reshape(-1),
            image_part[D_I * D_C :],
        )
    )
    dp_count = lax.axis_size("dp")
    is_first = lax.axis_index("stream") == 0
    text_blocks = text_flat.reshape(2, dp_count, -1)
    image_blocks = image_flat.reshape(2, dp_count, -1)
    text_gathered, image_gathered = (
        lax.all_to_all(
            text_blocks.astype(jnp.bfloat16), "dp", split_axis=1, concat_axis=1, tiled=True
        ).astype(text_blocks.dtype),
        lax.all_to_all(
            image_blocks.astype(jnp.bfloat16), "dp", split_axis=1, concat_axis=1, tiled=True
        ).astype(image_blocks.dtype),
    )
    text_summed = jnp.sum(text_gathered, axis=1)
    image_summed = jnp.sum(image_gathered, axis=1)
    text_other = jnp.where(is_first, text_summed[1], text_summed[0])
    image_other = jnp.where(is_first, image_summed[1], image_summed[0])
    text_far, image_far = (
        swapped(text_other.astype(jnp.bfloat16), "stream", 0).astype(text_other.dtype),
        swapped(image_other.astype(jnp.bfloat16), "stream", 0).astype(image_other.dtype),
    )
    text_share = jnp.where(is_first, text_summed[0], text_summed[1]) + text_far
    image_share = jnp.where(is_first, image_summed[0], image_summed[1]) + image_far
    text_gain_sum, image_gain_sum = lax.psum((text_gain_part, image_gain_part), ("stream", "dp"))
    return (
        text_result,
        image_result,
        text_grad,
        image_grad,
        text_share,
        image_share,
        text_gain_sum,
        image_gain_sum,
    )


def solution(mesh):
    placed = (
        P(("stream", "dp"), None),
        P(("stream", "dp"), None),
        P(("stream", "dp")),
        P(),
        P(),
        P(),
        P(),
        P(),
        P(),
        P(),
        P(),
        P(),
        P(),
        P(),
        P(),
        P(),
        P(),
        P(),
        P(),
        P(("stream", "dp"), None),
        P(("stream", "dp"), None),
    )
    return jax.shard_map(
        local,
        mesh=mesh,
        in_specs=placed,
        out_specs=(
            P(("stream", "dp"), None),
            P(("stream", "dp"), None),
            P(("stream", "dp"), None),
            P(("stream", "dp"), None),
            P(("stream", "dp")),
            P(("stream", "dp")),
            P(),
            P(),
        ),
        check_vma=False,
    )
```

profile of v0, /device:TPU:14, one launch (start us, length us, event | category | flops | bytes accessed | tf_op | source)
XLA Modules:
  0.0 1397.8 jit_solution(7177210072608672650)
XLA Ops:
  0.7 4.0 convolution_convert_fusion.7
  13.9 22.4 %collective-permute-done.2 = bf16[2,128]{1,0:T(2,128)(2,1)} collective-permute-done((bf16[2,128]{1,0:T(2,128)(2,1)S(1)}, bf16[2,128]{1,0:T(2,128)(2,1)}, u32[]{:S(2)}, u32[]{:S(2)}) %collective-permute-start.2) | collective-permute-done | bytes 544 | tf_op jit(solution)/shard_map/ppermute | solution.py:24
  44.7 2.4 fusion.139
  48.0 11.3 multiply_convert_fusion
  64.5 2.4 copy.149
  66.9 3.7 reshape.386
  84.2 2.3 fusion.28
  96.4 2.7 multiply_reduce_fusion.3
  105.9 3.8 fusion.7
  109.7 3.7 convolution_convert_fusion.1
  120.9 3.0 fusion.8
  123.9 2.6 copy.185
  129.6 4.0 reshape.396
  133.6 5.8 copy.224
  139.4 9.4 reshape.398
  148.8 5.8 reshape.399
  159.4 2.6 convolution_add_fusion
  161.9 4.2 convert_bitcast_fusion.1
  166.1 6.7 copy.189
  172.8 5.6 copy.226
  193.2 5.2 multiply_reduce_fusion.13
  210.3 4.6 convert_bitcast_fusion
  218.1 2.7 copy.180
  220.7 2.3 convert_element_type.298
  226.6 3.9 copy.188
  250.7 2.9 constant_dynamic-update-slice_fusion.10
  255.1 28.2 %convert_element_type.310 = bf16[2,16,327680]{2,1,0:T(8,128)(2,1)} reshape(bf16[10485760]{0:T(1024)(128)(2,1)} %constant_dynamic-update-slice_fusion.9) | data formatting | bytes 41943040 | tf_op jit(solution)/shard_map/convert_element_type | solution.py:341
  283.4 38.2 %copy.190 = bf16[2,16,327680]{2,0,1:T(2,128)(2,1)} copy(bf16[2,16,327680]{2,1,0:T(8,128)(2,1)} %convert_element_type.310) | data formatting | bytes 41943040 | tf_op jit(solution)/shard_map/convert_element_type | solution.py:341
  321.5 6.4 all-to-all-start.1
  328.0 472.4 %all-reduce = (f32[3,768]{1,0:T(4,128)}, f32[3,1024]{1,0:T(4,128)}) all-reduce(f32[3,768]{1,0:T(4,128)S(1)} %pad_maximum_fusion.5, f32[3,1024]{1,0:T(4,128)S(1)} %pad_maximum_fusion.4), channel_id=1, replica_groups=mesh['stream'=2,'dp'=16] {'stream','dp'}, use_global_device_ids=true, to_apply=%region_41.42 | all-reduce | flops 5376 | bytes 43008 | tf_op jit(solution)/shard_map/psum | solution.py:354
  801.1 4.4 fusion.36
  805.5 2.3 fusion.6
  807.8 3.0 copy.186
  810.8 2.9 copy.223
  818.2 2.5 constant_dynamic-update-slice_fusion
  821.8 2.6 constant_dynamic-update-slice_fusion.6
  828.5 27.6 %convert_element_type.305 = bf16[2,16,319488]{2,1,0:T(8,128)(2,1)} reshape(bf16[10223616]{0:T(1024)(128)(2,1)} %constant_dynamic-update-slice_fusion.4) | data formatting | bytes 40894464 | tf_op jit(solution)/shard_map/convert_element_type | solution.py:338
  856.1 37.2 %copy.187 = bf16[2,16,319488]{2,0,1:T(2,128)(2,1)} copy(bf16[2,16,319488]{2,1,0:T(8,128)(2,1)} %convert_element_type.305) | data formatting | bytes 40894464 | tf_op jit(solution)/shard_map/convert_element_type | solution.py:338
  893.3 3.0 fusion.15
  896.3 8.2 all-to-all-start
  904.5 20.1 %convert_reduce_fusion = f32[2,327680]{1,0:T(2,128)S(1)} fusion(bf16[2,16,327680]{2,0,1:T(2,128)(2,1)} %all-to-all-done.1), kind=kLoop, calls=%fused_computation | loop fusion | flops 20316160 | bytes 23592960 | tf_op jit(solution)/shard_map/reduce_sum | solution.py:345
  924.6 13.6 fusion.10
  938.5 2.4 broadcast_select_fusion.1
  940.9 404.1 %all-to-all-done = bf16[2,16,319488]{2,0,1:T(2,128)(2,1)} async-done(((bf16[2,16,319488]{2,0,1:T(2,128)(2,1)}), bf16[2,16,319488]{2,0,1:T(2,128)(2,1)}, u32[]{:S(2)}, u32[]{:S(2)}) %all-to-all-start) | async-done | bytes 20447264 | tf_op jit(solution)/shard_map/all_to_all | solution.py:337
  1345.0 19.6 %convert_reduce_fusion.1 = f32[2,319488]{1,0:T(2,128)S(1)} fusion(bf16[2,16,319488]{2,0,1:T(2,128)(2,1)} %all-to-all-done), kind=kLoop, calls=%fused_computation.1 | loop fusion | flops 19808256 | bytes 23003136 | tf_op jit(solution)/shard_map/reduce_sum | solution.py:344
  1366.0 13.5 fusion.14
  1379.8 2.4 convert_add_fusion
  1382.2 14.0 %collective-permute-done.5 = bf16[319488]{0:T(1024)(128)(2,1)S(1)} collective-permute-done((bf16[319488]{0:T(1024)(128)(2,1)S(1)}, bf16[319488]{0:T(1024)(128)(2,1)S(1)}, u32[]{:S(2)}, u32[]{:S(2)}) %collective-permute-start.5) | collective-permute-done | bytes 639008 | tf_op jit(solution)/shard_map/ppermute | solution.py:24
  (462 shorter events, 136.0 us)
Async XLA Ops:
  0.6 61.7 %copy-start = (bf16[768,2304]{1,0:T(8,128)(2,1)S(1)}, bf16[768,2304]{1,0:T(8,128)(2,1)}, u32[]{:S(2)}) copy-start(bf16[768,2304]{1,0:T(8,128)(2,1)} %param.29) | copy-start | bytes 10616836
  0.6 4.6 copy-start.29
  0.7 4.6 copy-start.123
  4.7 4.2 copy-start.122
  4.7 5.3 copy-start.31
  4.7 5.9 copy-start.18
  4.7 5.9 copy-start.44
  4.7 32.8 %collective-permute-start = (bf16[72,2048]{1,0:T(8,128)(2,1)}, bf16[72,2048]{1,0:T(8,128)(2,1)}, u32[]{:S(2)}, u32[]{:S(2)}) collective-permute-start(bf16[72,2048]{1,0:T(8,128)(2,1)} %convolution_convert_fusion.7), channel_id=1, source_target_pairs={{0,16},{16,0},{1,17},{17,1},{2,18},{18,2},{3,19},{19,3},{4,20},{20... | collective-permute-start | bytes 884744 | tf_op jit(solution)/shard_map/ppermute | solution.py:24
  7.3 4.4 copy-start.113
  7.3 171.1 %collective-permute-start.1 = (bf16[256,2048]{1,0:T(8,128)(2,1)}, bf16[256,2048]{1,0:T(8,128)(2,1)}, u32[]{:S(2)}, u32[]{:S(2)}) collective-permute-start(bf16[256,2048]{1,0:T(8,128)(2,1)} %convolution_convert_fusion.6), channel_id=1, source_target_pairs={{0,16},{16,0},{1,17},{17,1},{2,18},{18,2},{3,19},{19,3},{4,20},{20... | collective-permute-start | bytes 3145736 | tf_op jit(solution)/shard_map/ppermute | solution.py:24
  9.5 26.9 %collective-permute-start.2 = (bf16[2,128]{1,0:T(2,128)(2,1)S(1)}, bf16[2,128]{1,0:T(2,128)(2,1)}, u32[]{:S(2)}, u32[]{:S(2)}) collective-permute-start(bf16[2,128]{1,0:T(2,128)(2,1)S(1)} %get-tuple-element.56), channel_id=1, source_target_pairs={{0,16},{16,0},{1,17},{17,1},{2,18},{18,2},{3,19},{19,3},{4,20},{20... | collective-permute-start | bytes 1544 | tf_op jit(solution)/shard_map/ppermute | solution.py:24
  12.3 47.0 %copy-start.82 = (f32[768]{0:T(1024)}, f32[768]{0:T(1024)S(1)}, u32[]{:S(2)}) copy-start(f32[768]{0:T(1024)S(1)} %get-tuple-element.21) | copy-start | bytes 9220
  12.3 49.5 %copy-start.85 = (f32[768]{0:T(1024)}, f32[768]{0:T(1024)S(1)}, u32[]{:S(2)}) copy-start(f32[768]{0:T(1024)S(1)} %get-tuple-element.22) | copy-start | bytes 9220
  44.7 14.6 %slice-start.8 = ((s8[4718592]{0:T(1024)(128)(4,1)}), s8[4194304]{0:T(1024)(128)(4,1)S(1)}, s32[]{:S(2)}) async-start(s8[4718592]{0:T(1024)(128)(4,1)} %bitcast.383), calls=%async_computation.10 | async-start | bytes 8388608
  47.2 12.2 copy-start.5
  47.2 12.1 copy-start.93
  48.0 11.3 copy-start.98
  48.0 11.3 slice-start.9
  99.6 4.4 copy-start.11
  120.3 41.6 %collective-permute-start.4 = (bf16[72,2048]{1,0:T(8,128)(2,1)}, bf16[72,2048]{1,0:T(8,128)(2,1)}, u32[]{:S(2)}, u32[]{:S(2)}) collective-permute-start(bf16[72,2048]{1,0:T(8,128)(2,1)} %convert_element_type.303), channel_id=1, source_target_pairs={{0,16},{16,0},{1,17},{17,1},{2,18},{18,2},{3,19},{19,3},{4,20},{20... | collective-permute-start | bytes 884744 | tf_op jit(solution)/shard_map/ppermute | solution.py:24
  154.6 4.7 copy-start.12
  154.6 4.8 copy-start.32
  180.2 4.0 copy-start.52
  180.2 4.0 copy-start.74
  193.2 5.3 copy-start.121
  193.2 5.5 copy-start.15
  193.2 5.6 copy-start.77
  193.2 5.6 copy-start.78
  206.0 4.3 copy-start.43
  210.3 4.6 copy-start.39
  210.3 4.6 copy-start.64
  210.3 4.6 copy-start.117
  217.0 7.5 copy-start.81
  223.0 582.5 %collective-permute-start.3 = (bf16[256,2048]{1,0:T(8,128)(2,1)}, bf16[256,2048]{1,0:T(8,128)(2,1)}, u32[]{:S(2)}, u32[]{:S(2)}) collective-permute-start(bf16[256,2048]{1,0:T(8,128)(2,1)} %convert_element_type.298), channel_id=1, source_target_pairs={{0,16},{16,0},{1,17},{17,1},{2,18},{18,2},{3,19},{19,3},{4,20},{20... | collective-permute-start | bytes 3145736 | tf_op jit(solution)/shard_map/ppermute | solution.py:24
  234.2 4.5 slice-start.2
  321.5 478.8 %copy-start.19 = (bf16[1024,1024]{1,0:T(8,128)(2,1)S(1)}, bf16[1024,1024]{1,0:T(8,128)(2,1)}, u32[]{:S(2)}) copy-start(bf16[1024,1024]{1,0:T(8,128)(2,1)} %param.32) | copy-start | bytes 6291460
  321.5 478.8 %copy-start.37 = (f32[72,1024]{1,0:T(8,128)S(1)}, f32[72,1024]{1,0:T(8,128)}, u32[]{:S(2)}) copy-start(f32[72,1024]{1,0:T(8,128)} %copy-done.36) | copy-start | bytes 884740
  321.5 478.8 %copy-start.115 = (f32[72]{0:T(128)S(1)}, f32[72]{0:T(128)}, u32[]{:S(2)}) copy-start(f32[72]{0:T(128)} %copy-done.114) | copy-start | bytes 868
  321.5 574.8 %all-to-all-start.1 = ((bf16[2,16,327680]{2,0,1:T(2,128)(2,1)}), bf16[2,16,327680]{2,0,1:T(2,128)(2,1)}, u32[]{:S(2)}, u32[]{:S(2)}) async-start(bf16[2,16,327680]{2,0,1:T(2,128)(2,1)} %copy.190), calls=%async_computation.1 | async-start | bytes 41943040 | tf_op jit(solution)/shard_map/all_to_all | solution.py:340
  801.1 4.4 copy-start.30
  813.7 4.4 slice-start.7
  856.0 37.2 %copy-start.65 = (f32[256,768]{1,0:T(8,128)S(1)}, f32[256,768]{1,0:T(8,128)}, u32[]{:S(2)}) copy-start(f32[256,768]{1,0:T(8,128)} %convolution_add_fusion) | copy-start | bytes 2359300
  856.1 37.2 %copy-start.124 = (bf16[768,2048]{1,0:T(8,128)(2,1)S(1)}, bf16[768,2048]{1,0:T(8,128)(2,1)}, u32[]{:S(2)}) copy-start(bf16[768,2048]{1,0:T(8,128)(2,1)} %param.25) | copy-start | bytes 9437188
  896.3 448.7 %all-to-all-start = ((bf16[2,16,319488]{2,0,1:T(2,128)(2,1)}), bf16[2,16,319488]{2,0,1:T(2,128)(2,1)}, u32[]{:S(2)}, u32[]{:S(2)}) async-start(bf16[2,16,319488]{2,0,1:T(2,128)(2,1)} %copy.187), calls=%async_computation | async-start | bytes 40894464 | tf_op jit(solution)/shard_map/all_to_all | solution.py:337
  938.2 441.5 %collective-permute-start.6 = (bf16[327680]{0:T(1024)(128)(2,1)S(1)}, bf16[327680]{0:T(1024)(128)(2,1)}, u32[]{:S(2)}, u32[]{:S(2)}) collective-permute-start(bf16[327680]{0:T(1024)(128)(2,1)S(1)} %fusion.10), channel_id=1, source_target_pairs={{0,16},{16,0},{1,17},{17,1},{2,18},{18,2},{3,19},{19,3},{4,20},{20... | collective-permute-start | bytes 1966088 | tf_op jit(solution)/shard_map/ppermute | solution.py:24
  1364.6 15.2 %copy-start.35 = (f32[1,327680]{1,0:T(1,128)S(1)}, f32[1,327680]{1,0:T(1,128)}, u32[]{:S(2)}) copy-start(f32[1,327680]{1,0:T(1,128)} %broadcast_select_fusion.1) | copy-start | bytes 3932164
  1379.5 16.6 %collective-permute-start.5 = (bf16[319488]{0:T(1024)(128)(2,1)S(1)}, bf16[319488]{0:T(1024)(128)(2,1)S(1)}, u32[]{:S(2)}, u32[]{:S(2)}) collective-permute-start(bf16[319488]{0:T(1024)(128)(2,1)S(1)} %fusion.14), channel_id=1, source_target_pairs={{0,16},{16,0},{1,17},{17,1},{2,18},{18,2},{3,19},{19,3},{4,20},{20... | collective-permute-start | bytes 1916936 | tf_op jit(solution)/shard_map/ppermute | solution.py:24
  1379.7 17.6 %copy-start.1 = (bf16[768,2304]{1,0:T(8,128)(2,1)S(1)}, bf16[768,2304]{1,0:T(8,128)(2,1)}, u32[]{:S(2)}) copy-start(bf16[768,2304]{1,0:T(8,128)(2,1)} %param.29) | copy-start | bytes 10616836
  (102 other events, 227.0 us)
where the time goes:
time: 1410 us; the launch traced here: 1400 us
  blocking collectives  472 us (33%)
  waiting for transfers between devices  441 us (31%)
  local copies, waits for them, and re-layouts  266 us (19%)
  matrix products  110 us (8%)
  other arithmetic  85.7 us (6%)
  starting transfers between devices  19.7 us (1%)
    psum x1, blocking collectives, local(): lax.psum((text_gain_part, image_gain_part), ('stream', 'dp'))  472 us
    all_to_all x1, waiting for transfers between devices, local(): lax.all_to_all(text_blocks.astype(jnp.bfloat16), 'dp', split_axis=1, conc...  404 us
    convert_element_type x2, local copies, waits for them, and re-layouts, local(): image_blocks.astype(jnp.bfloat16)  66.4 us
    unnamed x312, local copies, waits for them, and re-layouts  66 us
    convert_element_type x2, local copies, waits for them, and re-layouts, local(): text_blocks.astype(jnp.bfloat16)  64.8 us
    ppermute x7, waiting for transfers between devices, swapped(): return lax.ppermute(block, axis, route)  36.4 us
    dot_general x14, matrix products, matmul_tn(): lax.dot_general(left_side, right_side, (((0,), (0,)), ((), ())), preferre...  35.8 us
    dot_general x14, matrix products, matmul(): return jnp.dot(left_side, right_side, preferred_element_type=jnp.float32)  30.1 us
  transfers between devices with their start and end apart: 9, of which 3 were waited for; matrix products, arithmetic and copies ran while one was open for 29% of the time, Pallas kernels for 0%

commit v1 on v0

v1 whole, which is shorter than its diff:
```python
import functools

import jax
import jax.numpy as jnp
from jax import lax
from jax.experimental import pallas as pl
from jax.experimental.pallas import tpu as pltpu
from jax.sharding import PartitionSpec as P

H_T = 12
H_I = 8
H_C = 8
D_C = 1024
LANES = 128
UNIT = 256
masked_score = -1e30
F32 = jnp.float32
BF16 = jnp.bfloat16


def mm(a, b):
    return jnp.dot(a, b, preferred_element_type=F32)


def mm_nt(a, b):
    return lax.dot_general(a, b, (((1,), (1,)), ((), ())), preferred_element_type=F32)


def mm_tn(a, b):
    return lax.dot_general(a, b, (((0,), (0,)), ((), ())), preferred_element_type=F32)


def cost(flops, nbytes, trans=0):
    return pl.CostEstimate(
        flops=int(flops), bytes_accessed=int(nbytes), transcendentals=int(trans)
    )


def key_masks(lens_ref, pairs, rows, keys, fixed):
    columns = lax.broadcasted_iota(jnp.int32, (rows, keys), 1)
    if fixed is not None:
        same = columns < fixed
        return [same] * pairs
    return [columns < lens_ref[p] for p in range(pairs)]


def lane_masks(rows, heads_in):
    if heads_in == 1:
        return [None]
    lanes = lax.broadcasted_iota(jnp.int32, (rows, LANES), 1)
    return [lanes < LANES // 2, lanes >= LANES // 2]


def only(block, mask):
    if mask is None:
        return block
    return jnp.where(mask, block, jnp.zeros_like(block))


def joined(blocks, masks):
    if len(blocks) == 1:
        return blocks[0]
    return jnp.where(masks[0], blocks[0], blocks[1])


def softmax_rows(scores):
    highest = jnp.max(scores, axis=-1, keepdims=True)
    raised = jnp.exp(scores - highest)
    return raised * (1.0 / jnp.sum(raised, axis=-1, keepdims=True))


def attend_kernel(lens_ref, q_ref, k_ref, v_ref, o_ref, *, pairs, heads_in, fixed, scaling):
    ql = q_ref.shape[0] // pairs
    kl = k_ref.shape[0] // pairs
    masks = key_masks(lens_ref, pairs, ql, kl, fixed)
    lanes = lane_masks(ql, heads_in)
    for p in range(pairs):
        q = q_ref[p * ql : (p + 1) * ql, :]
        k = k_ref[p * kl : (p + 1) * kl, :]
        v = v_ref[p * kl : (p + 1) * kl, :]
        parts = []
        for lane in lanes:
            s = jnp.where(masks[p], mm_nt(only(q, lane), k) * scaling, masked_score)
            parts.append(mm(softmax_rows(s).astype(BF16), v))
        o_ref[p * ql : (p + 1) * ql, :] = joined(parts, lanes).astype(BF16)


def attend(lens, q, k, v, cols, pairs, blocks, heads_in, fixed, scaling):
    rows = q.shape[0]
    krows = k.shape[0]

    def spec(count, start):
        return pl.BlockSpec((count, LANES), lambda j, start=start: (0, start + j))

    return pl.pallas_call(
        functools.partial(
            attend_kernel, pairs=pairs, heads_in=heads_in, fixed=fixed, scaling=scaling
        ),
        grid=(blocks,),
        in_specs=[
            pl.BlockSpec(memory_space=pltpu.SMEM),
            spec(rows, cols[0]),
            spec(krows, cols[1]),
            spec(krows, cols[2]),
        ],
        out_specs=spec(rows, 0),
        out_shape=jax.ShapeDtypeStruct((rows, blocks * LANES), BF16),
        cost_estimate=cost(
            4 * blocks * heads_in * rows * krows // pairs * LANES,
            4 * blocks * LANES * (rows + krows),
            blocks * heads_in * rows * krows // pairs,
        ),
        name="attend",
    )(lens, q, k, v)


def attend_back_kernel(
    lens_ref, q_ref, k_ref, v_ref, g_ref, *rest, pairs, heads_in, fixed, scaling, packed
):
    if packed:
        out_ref, dk_ref, dv_ref = rest
        dq_ref, dk_out = out_ref, dk_ref
    else:
        dq_ref, out_ref, dv_ref = rest
        dk_out = out_ref
    step = pl.program_id(1)
    ql = q_ref.shape[0] // pairs
    kl = k_ref.shape[0] // pairs

    @pl.when(step == 0)
    def _():
        masks = key_masks(lens_ref, pairs, ql, kl, fixed)
        qlanes = lane_masks(ql, heads_in)
        klanes = lane_masks(kl, heads_in)
        for p in range(pairs):
            qs = slice(p * ql, (p + 1) * ql)
            ks = slice(p * kl, (p + 1) * kl)
            q, g = q_ref[qs, :], g_ref[qs, :]
            k, v = k_ref[ks, :], v_ref[ks, :]
            dq, dk, dv = [], [], []
            for lane in qlanes:
                s = jnp.where(masks[p], mm_nt(only(q, lane), k) * scaling, masked_score)
                w = softmax_rows(s)
                dv.append(mm_tn(w.astype(BF16), g))
                dp = mm_nt(only(g, lane), v)
                inner = jnp.sum(w * dp, axis=-1, keepdims=True)
                ds = (w * (dp - inner)).astype(BF16)
                dq.append(mm(ds, k))
                dk.append(mm_tn(ds, q))
            dq_ref[qs, :] = (joined(dq, qlanes) * scaling).astype(BF16)
            dk_out[ks, :] = (joined(dk, klanes) * scaling).astype(BF16)
            dv_ref[ks, :] = joined(dv, klanes).astype(BF16)

    if packed:

        @pl.when(step == 1)
        def _():
            out_ref[...] = dk_ref[...]

        @pl.when(step == 2)
        def _():
            out_ref[...] = dv_ref[...]
    else:

        @pl.when(step == 1)
        def _():
            out_ref[...] = dv_ref[...]


def attend_back(lens, q, k, v, g, cols, pairs, blocks, heads_in, fixed, scaling, packed):
    rows = q.shape[0]
    krows = k.shape[0]

    def spec(count, start):
        return pl.BlockSpec((count, LANES), lambda j, t, start=start: (0, start + j))

    if packed:
        steps = 3
        out_specs = pl.BlockSpec((rows, LANES), lambda j, t: (0, t * blocks + j))
        out_shape = jax.ShapeDtypeStruct((rows, 3 * blocks * LANES), BF16)
        scratch = [pltpu.VMEM((krows, LANES), BF16)] * 2
    else:
        steps = 2
        out_specs = [
            spec(rows, 0),
            pl.BlockSpec((krows, LANES), lambda j, t: (0, t * blocks + j)),
        ]
        out_shape = [
            jax.ShapeDtypeStruct((rows, blocks * LANES), BF16),
            jax.ShapeDtypeStruct((krows, 2 * blocks * LANES), BF16),
        ]
        scratch = [pltpu.VMEM((krows, LANES), BF16)]
    return pl.pallas_call(
        functools.partial(
            attend_back_kernel,
            pairs=pairs,
            heads_in=heads_in,
            fixed=fixed,
            scaling=scaling,
            packed=packed,
        ),
        grid=(blocks, steps),
        in_specs=[
            pl.BlockSpec(memory_space=pltpu.SMEM),
            spec(rows, cols[0]),
            spec(krows, cols[1]),
            spec(krows, cols[2]),
            spec(rows, 0),
        ],
        out_specs=out_specs,
        out_shape=out_shape,
        scratch_shapes=scratch,
        cost_estimate=cost(
            10 * blocks * heads_in * rows * krows // pairs * LANES,
            8 * blocks * LANES * (rows + krows),
            blocks * heads_in * rows * krows // pairs,
        ),
        name="attend_back",
    )(lens, q, k, v, g)


def flat_kernel(core_ref, a0_ref, a1_ref, b0_ref, b1_ref, *rest, columns):
    out_ref, stage_ref = rest[-2:]
    core = core_ref[0]
    count = columns // UNIT
    bm = a0_ref.shape[1]
    a0 = a0_ref[...].T
    a1 = a1_ref[...].T
    u = 0
    while u < count:
        width = 2 if u + 1 < count else 1
        picks = [
            pl.ds(pl.multiple_of((2 * (u + i) + core) * LANES, LANES), LANES)
            for i in range(width)
        ]
        b0 = [b0_ref[:, pick] for pick in picks]
        b1 = [b1_ref[:, pick] for pick in picks]
        if width == 2:
            b0, b1 = jnp.concatenate(b0, axis=1), jnp.concatenate(b1, axis=1)
        else:
            b0, b1 = b0[0], b1[0]
        total = mm(a0, b0) + mm(a1, b1)
        for i in range(width):
            stage_ref[pl.ds(u + i, bm, stride=count), :] = total[
                :, i * LANES : (i + 1) * LANES
            ]
        u += width
    out_ref[...] = stage_ref[...].astype(BF16)


def flat_grad(flat, total_rows, core, a, b, rows_from, rows_to, place, bm=128):
    a0, a1 = a
    b0, b1 = b
    depth = a0.shape[0]
    columns = b0.shape[1]
    count = columns // UNIT
    out_rows = bm * count
    first = rows_from // bm
    steps = (rows_to - rows_from) // bm

    in_specs = [
        pl.BlockSpec(memory_space=pltpu.SMEM),
        pl.BlockSpec((depth, bm), lambda i: (0, first + i)),
        pl.BlockSpec((depth, bm), lambda i: (0, first + i)),
        pl.BlockSpec((depth, columns), lambda i: (0, 0)),
        pl.BlockSpec((depth, columns), lambda i: (0, 0)),
    ]
    operands = [core, a0, a1, b0, b1]
    aliases = {}
    if flat is not None:
        in_specs.append(pl.BlockSpec(memory_space=pl.ANY))
        operands.append(flat)
        aliases = {5: 0}
    return pl.pallas_call(
        functools.partial(flat_kernel, columns=columns),
        grid=(steps,),
        in_specs=in_specs,
        out_specs=pl.BlockSpec(
            (pl.Element(out_rows), pl.Element(LANES)),
            lambda i: (pl.multiple_of(place + i * out_rows, LANES), 0),
        ),
        out_shape=jax.ShapeDtypeStruct((total_rows, LANES), BF16),
        scratch_shapes=[pltpu.VMEM((out_rows, LANES), F32)],
        input_output_aliases=aliases,
        compiler_params=pltpu.CompilerParams(vmem_limit_bytes=40 * 1024 * 1024),
        cost_estimate=cost(
            2 * 2 * depth * (rows_to - rows_from) * columns // 2,
            4 * depth * (rows_to - rows_from + columns) + 2 * steps * out_rows * LANES,
        ),
        name="flat_grad",
    )(*operands)


def flat_half(core, total_rows, work):
    flat = None
    place = 0
    for a, b, low, high in work:
        flat = flat_grad(flat, total_rows, core, a, b, low, high, place)
        place += (high - low) * b[0].shape[1] // UNIT
    return flat


def dp_swap(block, bit):
    count = lax.axis_size("dp")
    return lax.ppermute(block, "dp", [(i, i ^ bit) for i in range(count)])


def stream_swap(block):
    return lax.ppermute(block, "stream", [(0, 1), (1, 0)])


def pick(block, index, axis=0):
    return lax.dynamic_index_in_dim(block, index, axis, keepdims=False)


def plus(a, b):
    return (a.astype(F32) + b.astype(F32)).astype(BF16)


def line_step(block, step, span, toward):
    count = lax.axis_size("dp")
    route = []
    for i in range(count):
        at = (i >> 2) % span
        if toward > 0 and at <= step and at + 1 < span:
            route.append((i, i + 4))
        if toward < 0 and span - 1 - at <= step and at > 0:
            route.append((i, i - 4))
    return lax.ppermute(block, "dp", route)


def reduce_scatter(flat):
    count = lax.axis_size("dp")
    me = lax.axis_index("dp")
    span = count // 4
    rows = flat.shape[0] // (2 * span)
    y = (me >> 1) & 1
    blocks = flat.reshape(span, 2, rows, LANES)
    total = plus(pick(blocks, y, 1), dp_swap(pick(blocks, 1 - y, 1), 2))
    while span > 4:
        half = span // 2
        upper = (me >> 2) // half % 2
        halves = total.reshape(2, half, rows, LANES)
        total = plus(pick(halves, upper), dp_swap(pick(halves, 1 - upper), 4 * half))
        span = half
    at = (me >> 2) % span
    up = down = None
    for step in range(span - 1):
        to_up = pick(total, jnp.clip(span - 1 - step + at, 0, span - 1))
        to_down = pick(total, jnp.clip(step - (span - 1) + at, 0, span - 1))
        up = line_step(to_up if up is None else plus(to_up, up), step, span, 1)
        down = line_step(to_down if down is None else plus(to_down, down), step, span, -1)
    result = pick(total, at).astype(F32)
    if up is not None:
        result = result + up.astype(F32) + down.astype(F32)
    return result


def share_of(result):
    core = lax.axis_index("dp") & 1
    halves = result.reshape(2, result.shape[0] // 2, LANES)
    mine = pick(halves, core)
    far = dp_swap(pick(halves, 1 - core), 1)
    first = jnp.where(core == 0, mine, far)
    second = jnp.where(core == 0, far, mine)
    return jnp.stack([first, second], axis=1).reshape(-1)


def normed(tensor):
    centred = tensor - jnp.mean(tensor, axis=-1, keepdims=True)
    inverse = lax.rsqrt(jnp.mean(centred * centred, axis=-1, keepdims=True) + 1e-05)
    return centred * inverse, inverse


def normed_back(grad, n, inverse, gain_row):
    scaled = grad * gain_row
    low = jnp.mean(scaled, axis=-1, keepdims=True)
    tilt = jnp.mean(scaled * n, axis=-1, keepdims=True)
    return (scaled - low - n * tilt) * inverse, jnp.sum(grad * n, axis=0)


def gelu_and_slope(u):
    share = 0.5 * (1.0 + lax.erf(u * 0.7071067811865476))
    slope = share + u * (0.3989422804014327 * jnp.exp(-0.5 * u * u))
    return (u * share).astype(BF16), slope


def stream_layer(states, context, cot, lens, weights, gains, heads, fixed, pairs):
    attend_w, up_w, down_w, qkv_w, output_w = weights
    width = states.shape[1]
    size = width // heads
    heads_in = LANES // size
    blocks = width // LANES
    scaling = size ** (-0.5)
    n1, inv1 = normed(states.astype(F32) + mm(context, attend_w))
    h1 = n1 * gains[0]
    h1_low = h1.astype(BF16)
    hidden_low, slope = gelu_and_slope(mm(h1_low, up_w))
    n2, inv2 = normed(h1 + mm(hidden_low, down_w))
    h2 = n2 * gains[1]
    h2_low = h2.astype(BF16)
    packed = mm(h2_low, qkv_w).astype(BF16)
    cols = (0, blocks, 2 * blocks)
    z = attend(lens, packed, packed, packed, cols, pairs, blocks, heads_in, fixed, scaling)
    n3, inv3 = normed(h2 + mm(z, output_w))
    result = n3 * gains[2]
    de, dg2 = normed_back(cot, n3, inv3, gains[2])
    de_low = de.astype(BF16)
    dz = mm_nt(de_low, output_w).astype(BF16)
    dr = attend_back(
        lens, packed, packed, packed, dz, cols, pairs, blocks, heads_in, fixed, scaling, True
    )
    dh2 = de + mm_nt(dr, qkv_w)
    db, dg1 = normed_back(dh2, n2, inv2, gains[1])
    db_low = db.astype(BF16)
    du = (mm_nt(db_low, down_w) * slope).astype(BF16)
    dh1 = db + mm_nt(du, up_w)
    da, dg0 = normed_back(dh1, n1, inv1, gains[0])
    da_low = da.astype(BF16)
    dc = mm_nt(da_low, attend_w).astype(BF16)
    sides = {
        "attend": (context, da_low),
        "up": (h1_low, du),
        "down": (hidden_low, db_low),
        "qkv": (h2_low, dr),
        "output": (z, de_low),
    }
    return result, da, dc, sides, jnp.stack((dg0, dg1, dg2))


def with_far(sides):
    near, far = {}, {}
    for name, (a, b) in sides.items():
        near[name] = (a, b)
        far[name] = (dp_swap(a, 1), dp_swap(b, 1))
    return {
        name: ((near[name][0], far[name][0]), (near[name][1], far[name][1])) for name in sides
    }


def local(
    text_states,
    image_states,
    caption_lengths,
    text_query,
    text_keyval,
    text_attend,
    text_up,
    text_down,
    text_qkv,
    text_output,
    text_gains,
    image_query,
    image_keyval,
    image_attend,
    image_up,
    image_down,
    image_qkv,
    image_output,
    image_gains,
    text_cotangent,
    image_cotangent,
):
    own_pairs = caption_lengths.shape[0]
    own_text = text_states.shape[0]
    text_len = own_text // own_pairs
    regions = image_states.shape[0] // own_pairs
    padded = -(-regions // 16) * 16
    own_image = own_pairs * padded
    pairs = 2 * own_pairs
    d_i = image_states.shape[1]
    stream = lax.axis_index("stream")
    core = (lax.axis_index("dp") & 1).astype(jnp.int32).reshape(1)

    def padded_rows(block):
        block = block.reshape(own_pairs, regions, d_i)
        return jnp.pad(block, ((0, 0), (0, padded - regions), (0, 0))).reshape(own_image, d_i)

    def trimmed(block):
        return block.reshape(own_pairs, padded, d_i)[:, :regions].reshape(-1, d_i)

    image_near = padded_rows(image_states)
    image_cot_near = padded_rows(image_cotangent)
    image_all = jnp.concatenate([stream_swap(image_near), image_near])
    text_all = jnp.concatenate([text_states, stream_swap(text_states)])
    lens = jnp.concatenate([caption_lengths, stream_swap(caption_lengths)])
    image_cot = jnp.concatenate([stream_swap(image_cot_near), image_cot_near])
    text_cot = jnp.concatenate([text_cotangent, stream_swap(text_cotangent)])

    positions = lax.broadcasted_iota(jnp.int32, (pairs, text_len), 1)
    valid = (positions < lens[:, None]).reshape(pairs * text_len, 1).astype(F32)

    co_blocks = D_C // LANES
    co_scale = (D_C // H_C) ** (-0.5)

    text_kv = mm(text_all, text_keyval).astype(BF16)
    image_q = mm(image_all, image_query).astype(BF16)
    ci = attend(lens, image_q, text_kv, text_kv, (0, 0, co_blocks), pairs, co_blocks, 1, None, co_scale)
    image_out, image_da, image_dc, image_sides, image_dg = stream_layer(
        image_all,
        ci,
        image_cot.astype(F32),
        lens,
        (image_attend, image_up, image_down, image_qkv, image_output),
        image_gains,
        H_I,
        regions,
        pairs,
    )
    image_dq, text_dkv = attend_back(
        lens, image_q, text_kv, text_kv, image_dc, (0, 0, co_blocks), pairs, co_blocks, 1, None, co_scale, False
    )

    image_kv = mm(image_all, image_keyval).astype(BF16)
    text_q = mm(text_all, text_query).astype(BF16)
    ct = attend(lens, text_q, image_kv, image_kv, (0, 0, co_blocks), pairs, co_blocks, 1, regions, co_scale)
    text_out, text_da, text_dc, text_sides, text_dg = stream_layer(
        text_all,
        ct,
        text_cot.astype(F32) * valid,
        lens,
        (text_attend, text_up, text_down, text_qkv, text_output),
        text_gains,
        H_T,
        None,
        pairs,
    )
    text_dq, image_dkv = attend_back(
        lens, text_q, image_kv, image_kv, text_dc, (0, 0, co_blocks), pairs, co_blocks, 1, regions, co_scale, False
    )

    text_result = (text_out[:own_text] * valid[:own_text]).astype(BF16)
    image_result = trimmed(image_out[own_image:].astype(BF16))
    text_grad = (
        text_da[:own_text]
        + mm_nt(text_dq[:own_text], text_query)
        + mm_nt(text_dkv[:own_text], text_keyval)
    ).astype(BF16)
    image_grad = trimmed(
        (
            image_da[own_image:]
            + mm_nt(image_dq[own_image:], image_query)
            + mm_nt(image_dkv[own_image:], image_keyval)
        ).astype(BF16)
    )

    image_sides["query"] = (image_all, image_dq)
    image_sides["keyval"] = (image_all, image_dkv)
    text_sides["query"] = (text_all, text_dq)
    text_sides["keyval"] = (text_all, text_dkv)

    def halves(sides, width):
        both = with_far(sides)
        total = sum(a[0].shape[1] * b[0].shape[1] for a, b in both.values())
        total_rows = total // (2 * UNIT)
        names = ("query", "keyval", "attend", "up", "down", "qkv", "output")
        first, second, filled = [], [], 0
        for name in names:
            a, b = both[name]
            m, n = a[0].shape[1], b[0].shape[1]
            room = min(max((total // 2 - filled) // n, 0), m)
            if room:
                first.append((a, b, 0, room))
            if room < m:
                second.append((a, b, room, m))
            filled += m * n
        return lax.cond(
            stream == 0,
            lambda: flat_half(core, total_rows, first),
            lambda: flat_half(core, total_rows, second),
        )

    image_share = share_of(reduce_scatter(halves(image_sides, d_i)))
    text_share = share_of(reduce_scatter(halves(text_sides, text_states.shape[1])))
    text_gain_sum, image_gain_sum = lax.psum((text_dg, image_dg), "dp")
    return (
        text_result,
        image_result,
        text_grad,
        image_grad,
        text_share,
        image_share,
        text_gain_sum,
        image_gain_sum,
    )


def solution(mesh):
    split = P(("stream", "dp"), None)
    flat = P(("stream", "dp"))
    whole = P()
    return jax.shard_map(
        local,
        mesh=mesh,
        in_specs=(split, split, flat) + (whole,) * 16 + (split, split),
        out_specs=(split, split, split, split, flat, flat, whole, whole),
        check_vma=False,
    )
```

time: 1410 us -> 640 us (0.45)
  the two profiles are of different devices: /device:TPU:14 before, /device:TPU:9 now
where the time goes in v1:
time: 640 us; the launch traced here: 633 us
  Pallas kernels  218 us (34%)
  blocking collectives  109 us (17%)
  matrix products  98.9 us (15%)
  waiting for transfers between devices  79 us (12%)
  starting transfers between devices  58.5 us (9%)
  other arithmetic  36.1 us (6%)
  local copies, waits for them, and re-layouts  31.4 us (5%)
    pallas_call x4, Pallas kernels, attend_back(): pl.pallas_call(functools.partial(attend_back_kernel, pairs=pairs, heads_i...  114 us
    psum x1, blocking collectives, local(): text_gain_sum, image_gain_sum = lax.psum((text_dg, image_dg), 'dp')  109 us
    ppermute x12, waiting for transfers between devices, line_step(): return lax.ppermute(block, 'dp', route)  68.5 us
    pallas_call x8, Pallas kernels, flat_grad(): pl.pallas_call(functools.partial(flat_kernel, columns=columns), grid=(ste...  55.6 us
    dot_general x14, matrix products, mm_nt(): lax.dot_general(a, b, (((1,), (1,)), ((), ())), preferred_element_type=F32)  53.7 us
    pallas_call x4, Pallas kernels, attend(): pl.pallas_call(functools.partial(attend_kernel, pairs=pairs, heads_in=hea...  48.1 us
    dot_general x14, matrix products, mm(): return jnp.dot(a, b, preferred_element_type=F32)  45.3 us
    ppermute x30, starting transfers between devices, dp_swap(): return lax.ppermute(block, 'dp', [(i, i ^ bit) for i in range(count)])  34.1 us
  transfers between devices with their start and end apart: 47, of which 10 were waited for; matrix products, arithmetic and copies ran while one was open for 24% of the time, Pallas kernels for 34%

profile of v1, /device:TPU:9, one launch (start us, length us, event | category | flops | bytes accessed | tf_op | source)
XLA Modules:
  0.0 633.0 jit_solution(6531982317780680510)
XLA Ops:
  19.1 2.9 convolution_convert_fusion.9.q_ref
  26.8 8.8 %attend.4 = bf16[512,1024]{1,0:T(8,128)(2,1)} custom-call(s32[4]{0:T(128)} %copy-done.71, bf16[512,1024]{1,0:T(8,128)(2,1)} %convolution_convert_fusion.5.q_ref, bf16[192,2048]{1,0:T(8,128)(2,1)} %convolution_convert_fusion.3.k_ref.v_ref, bf16[192,2048]{1,0:T(8,128)(2,1)} %convolution_convert_fusion.3.k_ref.v_ref), custom_call_target="tpu_custom_call" | custom-call | flops 100663296 | bytes 2883584 | tf_op jit(solution)/shard_map/attend/pallas_call | solution.py:95
  35.7 3.1 fusion.52
  40.9 3.1 convolution_convert_fusion.2.k_ref.v_ref
  44.0 12.8 %attend.6 = bf16[192,1024]{1,0:T(8,128)(2,1)} custom-call(s32[4]{0:T(128)} %copy-done.71, bf16[192,1024]{1,0:T(8,128)(2,1)} %convolution_convert_fusion.9.q_ref, bf16[512,2048]{1,0:T(8,128)(2,1)} %convolution_convert_fusion.2.k_ref.v_ref, bf16[512,2048]{1,0:T(8,128)(2,1)} %convolution_convert_fusion.2.k_ref.v_ref), custom_call_target="tpu_custom_call" | custom-call | flops 100663296 | bytes 2883584 | tf_op jit(solution)/shard_map/attend/pallas_call | solution.py:95
  63.3 2.8 multiply_convert_fusion.3
  69.8 5.3 convolution_convert_fusion.1.q_ref.k_ref.v_ref
  75.1 7.9 %attend.7 = bf16[192,1024]{1,0:T(8,128)(2,1)} custom-call(s32[4]{0:T(128)} %copy-done.71, bf16[192,3072]{1,0:T(8,128)(2,1)} %convolution_convert_fusion.1.q_ref.k_ref.v_ref, bf16[192,3072]{1,0:T(8,128)(2,1)} %convolution_convert_fusion.1.q_ref.k_ref.v_ref, bf16[192,3072]{1,0:T(8,128)(2,1)} %convolution_convert_fusion.1.q_ref.k_ref.v_ref), custom_call_target="tpu_custom_call" | custom-call | flops 37748736 | bytes 1572864 | tf_op jit(solution)/shard_map/attend/pallas_call | solution.py:95
  93.1 28.3 %attend_back.6 = bf16[192,3072]{1,0:T(8,128)(2,1)} custom-call(s32[4]{0:T(128)} %copy-done.71, bf16[192,3072]{1,0:T(8,128)(2,1)} %convolution_convert_fusion.1.q_ref.k_ref.v_ref, bf16[192,3072]{1,0:T(8,128)(2,1)} %convolution_convert_fusion.1.q_ref.k_ref.v_ref, bf16[192,3072]{1,0:T(8,128)(2,1)} %convolution_convert_fusion.1.q_ref.k_ref.v_ref, ...), custom_call_target="tpu_custom_call" | custom-call | flops 94371840 | bytes 3145728 | tf_op jit(solution)/shard_map/attend_back/pallas_call | solution.py:193
  121.4 6.8 %multiply_reduce_fusion.11 = (f32[1024]{0:T(1024)}, f32[192]{0:T(256)S(1)}, f32[192]{0:T(256)S(1)}, f32[192,1024]{1,0:T(8,128)S(1)}) fusion(f32[192,1024]{1,0:T(8,128)} %copy-done.5, f32[192]{0:T(256)} %copy-done.94, f32[192]{0:T(256)} %copy-done.83, f32[1024]{0:T(1024)S(1)} %bitcast.166, bf16[192,3072]{1,0:T(8,128)(2,1)} %attend_back.6, ...), kind=kOutput, calls=%fused_computation.105 | convolution fusion | flops 1211496960 | bytes 10241280 | tf_op jit(solution)/shard_map/dot_general | solution.py:26
  136.8 6.9 %multiply_convert_fusion = (bf16[512,3072]{1,0:T(8,128)(2,1)S(1)}, f32[512,3072]{1,0:T(8,128)}) fusion(bf16[512,768]{1,0:T(8,128)(2,1)} %multiply_convert_fusion.2, bf16[768,3072]{1,0:T(8,128)(2,1)} %param.31), kind=kOutput, calls=%fused_computation.7 | convolution fusion | flops 2423783424 | bytes 14942208 | tf_op jit(solution)/shard_map/dot_general | solution.py:22
  143.6 2.8 fusion.54
  148.7 4.6 convolution_convert_fusion.q_ref.k_ref.v_ref
  153.3 18.5 %attend.5 = bf16[512,768]{1,0:T(8,128)(2,1)} custom-call(s32[4]{0:T(128)} %copy-done.71, bf16[512,2304]{1,0:T(8,128)(2,1)} %convolution_convert_fusion.q_ref.k_ref.v_ref, bf16[512,2304]{1,0:T(8,128)(2,1)} %convolution_convert_fusion.q_ref.k_ref.v_ref, bf16[512,2304]{1,0:T(8,128)(2,1)} %convolution_convert_fusion.q_ref.k_ref.v_ref), custom_call_target="tpu_custom_call" | custom-call | flops 402653184 | bytes 3145728 | tf_op jit(solution)/shard_map/attend/pallas_call | solution.py:95
  171.8 2.9 fusion.55
  182.8 34.1 %attend_back.4 = bf16[512,2304]{1,0:T(8,128)(2,1)} custom-call(s32[4]{0:T(128)} %copy-done.71, bf16[512,2304]{1,0:T(8,128)(2,1)} %convolution_convert_fusion.q_ref.k_ref.v_ref, bf16[512,2304]{1,0:T(8,128)(2,1)} %convolution_convert_fusion.q_ref.k_ref.v_ref, bf16[512,2304]{1,0:T(8,128)(2,1)} %convolution_convert_fusion.q_ref.k_ref.v_ref, ...), custom_call_target="tpu_custom_call" | custom-call | flops 1006632960 | bytes 6291456 | tf_op jit(solution)/shard_map/attend_back/pallas_call | solution.py:193
  216.9 6.0 multiply_reduce_fusion.1
  225.5 10.6 %fusion.5 = bf16[512,3072]{1,0:T(8,128)(2,1)} fusion(f32[512,3072]{1,0:T(8,128)} %get-tuple-element.261, bf16[512,768]{1,0:T(8,128)(2,1)S(1)} %get-tuple-element.231, bf16[3072,768]{1,0:T(8,128)(2,1)} %param.32), kind=kOutput, calls=%fused_computation.6 | convolution fusion | flops 2431647744 | bytes 14942208 | tf_op jit(solution)/shard_map/dot_general | solution.py:26
  239.7 27.9 %attend_back.7 = (bf16[192,1024]{1,0:T(8,128)(2,1)}, bf16[512,2048]{1,0:T(8,128)(2,1)}) custom-call(s32[4]{0:T(128)} %copy-done.71, bf16[192,1024]{1,0:T(8,128)(2,1)} %convolution_convert_fusion.9.q_ref, bf16[512,2048]{1,0:T(8,128)(2,1)} %convolution_convert_fusion.2.k_ref.v_ref, bf16[512,2048]{1,0:T(8,128)(2,1)} %convolution_convert_fusion.2.k_ref.v_ref, ...), custom_call_target="tpu_custom_call" | custom-call | flops 251658240 | bytes 5767168 | tf_op jit(solution)/shard_map/attend_back/pallas_call | solution.py:193
  268.4 7.4 %multiply_reduce_fusion.2 = (f32[768]{0:T(1024)}, f32[512]{0:T(512)S(1)}, f32[512]{0:T(512)S(1)}, f32[512,768]{1,0:T(8,128)S(1)}) fusion(f32[512,768]{1,0:T(8,128)S(1)} %copy-done.9, f32[512]{0:T(512)} %add_rsqrt_fusion.2, f32[512]{0:T(512)S(1)} %copy-done.80, f32[768]{0:T(1024)S(1)} %copy-done.72, f32[512,768]{1,0:T(8,128)} %get-tuple-element.232, ...), kind=kOutput, calls=%fused_computation.21 | convolution fusion | flops 2419456256 | bytes 12597248 | tf_op jit(solution)/shard_map/dot_general | solution.py:26
  284.0 3.1 convolution_convert_fusion.4.g_ref
  287.1 24.2 %attend_back.5 = (bf16[512,1024]{1,0:T(8,128)(2,1)}, bf16[192,2048]{1,0:T(8,128)(2,1)}) custom-call(s32[4]{0:T(128)} %copy-done.71, bf16[512,1024]{1,0:T(8,128)(2,1)} %convolution_convert_fusion.5.q_ref, bf16[192,2048]{1,0:T(8,128)(2,1)} %convolution_convert_fusion.3.k_ref.v_ref, bf16[192,2048]{1,0:T(8,128)(2,1)} %convolution_convert_fusion.3.k_ref.v_ref, ...), custom_call_target="tpu_custom_call" | custom-call | flops 251658240 | bytes 5767168 | tf_op jit(solution)/shard_map/attend_back/pallas_call | solution.py:193
  315.8 5.8 collective-permute-done.29
  322.0 25.6 %conditional.3 = (bf16[4,2,2560,128]{3,2,1,0:T(8,128)(2,1)}) conditional(s32[]{:T(128)} %convert_element_type.294, (s32[1]{0:T(128)}, bf16[192,1024]{1,0:T(8,128)(2,1)}, bf16[192,1024]{1,0:T(8,128)(2,1)}, bf16[192,1024]{1,0:T(8,128)(2,1)}, bf16[192,1024]{1,0:T(8,128)(2,1)}, /*index=5*/bf16[192,1024]{1,0:T(8,128)(2,1)}, ...), branch_computations={%region_26.27_spmd, %region_27.28_spmd} | conditional | flops 2013265920 | bytes 23330992 | solution.py:567
  322.0 6.4 %flat_grad.26.rest_0_ = bf16[20480,128]{1,0:T(8,128)(2,1)} custom-call(s32[1]{0:T(128)} %get-tuple-element.175.core_ref, bf16[192,1024]{1,0:T(8,128)(2,1)} %get-tuple-element.184.a0_ref, bf16[192,1024]{1,0:T(8,128)(2,1)} %get-tuple-element.185.a1_ref, bf16[192,1024]{1,0:T(8,128)(2,1)} %get-tuple-element.188.b0_ref, bf16[192,1024]{1,0:T(8,128)(2,1)} %get-tuple-element.189.b1_ref), custom_call_target="tpu_custom_call" | custom-call | flops 402653184 | bytes 2621440 | tf_op jit(solution)/shard_map/cond/branch_1_fun/flat_grad/pallas_call | solution.py:274
  328.4 7.2 %flat_grad.27.rest_0_ = bf16[20480,128]{1,0:T(8,128)(2,1)} custom-call(s32[1]{0:T(128)} %get-tuple-element.175.core_ref, bf16[192,1024]{1,0:T(8,128)(2,1)} %get-tuple-element.184.a0_ref, bf16[192,1024]{1,0:T(8,128)(2,1)} %get-tuple-element.185.a1_ref, bf16[192,2048]{1,0:T(8,128)(2,1)S(1)} %copy-done.52, ...), custom_call_target="tpu_custom_call", output_to_operand_aliasing={{}: (5, {})} | custom-call | flops 805306368 | bytes 4456448 | tf_op jit(solution)/shard_map/cond/branch_1_fun/flat_grad/pallas_call | solution.py:274
  335.6 6.0 flat_grad.28.rest_0_
  341.6 6.0 flat_grad.29
  347.6 3.5 dynamic-slice_bitcast_fusion
  358.3 30.4 %conditional.2 = (bf16[4,2,2496,128]{3,2,1,0:T(8,128)(2,1)}) conditional(s32[]{:T(128)} %convert_element_type.294, (s32[1]{0:T(128)}, bf16[512,768]{1,0:T(8,128)(2,1)}, bf16[512,768]{1,0:T(8,128)(2,1)}, bf16[512,3072]{1,0:T(8,128)(2,1)}, bf16[512,3072]{1,0:T(8,128)(2,1)S(1)}, /*index=5*/bf16[512,3072]{1,0:T(8,128)(2,1)S(1)}, ...), branch_computations={%region_24.25_spmd, %region_25.26_spmd} | conditional | flops 5234491392 | bytes 44695672 | solution.py:567
  358.5 6.7 %flat_grad.19.rest_0_ = bf16[19968,128]{1,0:T(8,128)(2,1)} custom-call(s32[1]{0:T(128)} %get-tuple-element.147.core_ref, bf16[512,768]{1,0:T(8,128)(2,1)} %get-tuple-element.156.a0_ref, bf16[512,768]{1,0:T(8,128)(2,1)} %get-tuple-element.157.a1_ref, bf16[512,1024]{1,0:T(8,128)(2,1)} %get-tuple-element.160.b0_ref, bf16[512,1024]{1,0:T(8,128)(2,1)} %get-tuple-element.161.b1_ref), custom_call_target="tpu_custom_call" | custom-call | flops 805306368 | bytes 4456448 | tf_op jit(solution)/shard_map/cond/branch_1_fun/flat_grad/pallas_call | solution.py:274
  365.3 7.8 %flat_grad.20.rest_0_ = bf16[19968,128]{1,0:T(8,128)(2,1)} custom-call(s32[1]{0:T(128)} %get-tuple-element.147.core_ref, bf16[512,768]{1,0:T(8,128)(2,1)S(1)} %copy-done.22, bf16[512,768]{1,0:T(8,128)(2,1)S(1)} %copy-done.38, bf16[512,2048]{1,0:T(8,128)(2,1)S(1)} %copy-done.48, ...), custom_call_target="tpu_custom_call", output_to_operand_aliasing={{}: (5, {})} | custom-call | flops 1610612736 | bytes 7340032 | tf_op jit(solution)/shard_map/cond/branch_1_fun/flat_grad/pallas_call | solution.py:274
  373.0 7.1 %flat_grad.21.rest_0_ = bf16[19968,128]{1,0:T(8,128)(2,1)} custom-call(s32[1]{0:T(128)} %get-tuple-element.147.core_ref, bf16[512,1024]{1,0:T(8,128)(2,1)S(1)} %copy-done.28, bf16[512,1024]{1,0:T(8,128)(2,1)} %get-tuple-element.153.a1_ref, bf16[512,768]{1,0:T(8,128)(2,1)} %get-tuple-element.154.b0_ref, ...), custom_call_target="tpu_custom_call", output_to_operand_aliasing={{}: (5, {})} | custom-call | flops 805306368 | bytes 4456448 | tf_op jit(solution)/shard_map/cond/branch_1_fun/flat_grad/pallas_call | solution.py:274
  380.1 8.5 %flat_grad.22 = bf16[19968,128]{1,0:T(8,128)(2,1)} custom-call(s32[1]{0:T(128)} %get-tuple-element.147.core_ref, bf16[512,768]{1,0:T(8,128)(2,1)} %get-tuple-element.148.a0_ref, bf16[512,768]{1,0:T(8,128)(2,1)} %get-tuple-element.149.a1_ref, bf16[512,3072]{1,0:T(8,128)(2,1)} %get-tuple-element.150.b0_ref, ...), custom_call_target="tpu_custom_call", output_to_operand_aliasing={{}: (5, {})} | custom-call | flops 2013265920 | bytes 9568256 | tf_op jit(solution)/shard_map/cond/branch_1_fun/flat_grad/pallas_call | solution.py:274
  388.7 3.4 dynamic-slice_bitcast_fusion.1
  394.8 108.5 %all-reduce.2 = (f32[3,768]{1,0:T(4,128)}, f32[3,1024]{1,0:T(4,128)}) all-reduce(f32[3,768]{1,0:T(4,128)S(1)} %pad_maximum_fusion.6, f32[3,1024]{1,0:T(4,128)S(1)} %pad_maximum_fusion.5), channel_id=1, replica_groups=mesh['stream'=2,'dp'=16] {'dp'}, use_global_device_ids=true, to_apply=%region_31.32 | all-reduce | flops 5376 | bytes 43008 | tf_op jit(solution)/shard_map/psum | solution.py:575
  506.4 3.9 fusion.20
  510.3 3.2 fusion.6
  515.6 3.2 fusion.7
  520.2 12.9 %collective-permute-done.40 = bf16[2560,128]{1,0:T(8,128)(2,1)S(1)} collective-permute-done((bf16[2560,128]{1,0:T(8,128)(2,1)S(1)}, bf16[2560,128]{1,0:T(8,128)(2,1)S(1)}, u32[]{:S(2)}, u32[]{:S(2)}) %collective-permute-start.40) | collective-permute-done | bytes 655392 | tf_op jit(solution)/shard_map/ppermute | solution.py:329
  535.9 10.9 %collective-permute-done.19 = bf16[2496,128]{1,0:T(8,128)(2,1)S(1)} collective-permute-done((bf16[2496,128]{1,0:T(8,128)(2,1)S(1)}, bf16[2496,128]{1,0:T(8,128)(2,1)S(1)}, u32[]{:S(2)}, u32[]{:S(2)}) %collective-permute-start.19) | collective-permute-done | bytes 639008 | tf_op jit(solution)/shard_map/ppermute | solution.py:329
  548.9 11.9 %collective-permute-done.41 = bf16[2560,128]{1,0:T(8,128)(2,1)S(1)} collective-permute-done((bf16[2560,128]{1,0:T(8,128)(2,1)S(1)}, bf16[2560,128]{1,0:T(8,128)(2,1)S(1)}, u32[]{:S(2)}, u32[]{:S(2)}) %collective-permute-start.41) | collective-permute-done | bytes 655392 | tf_op jit(solution)/shard_map/ppermute | solution.py:329
  564.4 10.1 %collective-permute-done.20 = bf16[2496,128]{1,0:T(8,128)(2,1)S(1)} collective-permute-done((bf16[2496,128]{1,0:T(8,128)(2,1)S(1)}, bf16[2496,128]{1,0:T(8,128)(2,1)S(1)}, u32[]{:S(2)}, u32[]{:S(2)}) %collective-permute-start.20) | collective-permute-done | bytes 639008 | tf_op jit(solution)/shard_map/ppermute | solution.py:329
  578.3 4.0 collective-permute-start.21
  582.3 10.8 %collective-permute-done.23 = bf16[2496,128]{1,0:T(8,128)(2,1)S(1)} collective-permute-done((bf16[2496,128]{1,0:T(8,128)(2,1)S(1)}, bf16[2496,128]{1,0:T(8,128)(2,1)S(1)}, u32[]{:S(2)}, u32[]{:S(2)}) %collective-permute-start.23) | collective-permute-done | bytes 639008 | tf_op jit(solution)/shard_map/ppermute | solution.py:329
  595.1 11.9 %collective-permute-done.45 = bf16[2560,128]{1,0:T(8,128)(2,1)S(1)} collective-permute-done((bf16[2560,128]{1,0:T(8,128)(2,1)S(1)}, bf16[2560,128]{1,0:T(8,128)(2,1)S(1)}, u32[]{:S(2)}, u32[]{:S(2)}) %collective-permute-start.45) | collective-permute-done | bytes 655392 | tf_op jit(solution)/shard_map/ppermute | solution.py:329
  607.4 14.0 %collective-permute-start.46 = (f32[1280,128]{1,0:T(8,128)S(1)}, f32[1280,128]{1,0:T(8,128)S(1)}, u32[]{:S(2)}, u32[]{:S(2)}) collective-permute-start(f32[1280,128]{1,0:T(8,128)S(1)} %dynamic-slice_bitcast_fusion.2), channel_id=1, source_target_pairs={{0,1},{1,0},{2,3},{3,2},{4,5},{5,4},{6,7},{7,6},{8,9},{9,8},{10,11... | collective-permute-start | bytes 1966088 | tf_op jit(solution)/shard_map/ppermute | solution.py:305
  621.6 6.6 %collective-permute-start.25 = (f32[1248,128]{1,0:T(8,128)S(1)}, f32[1248,128]{1,0:T(8,128)S(1)}, u32[]{:S(2)}, u32[]{:S(2)}) collective-permute-start(f32[1248,128]{1,0:T(8,128)S(1)} %dynamic-slice_bitcast_fusion.5), channel_id=1, source_target_pairs={{0,1},{1,0},{2,3},{3,2},{4,5},{5,4},{6,7},{7,6},{8,9},{9,8},{10,11... | collective-permute-start | bytes 1916936 | tf_op jit(solution)/shard_map/ppermute | solution.py:305
  (401 shorter events, 119.2 us)
Async XLA Ops:
  0.6 148.1 %copy-start = (bf16[768,2304]{1,0:T(8,128)(2,1)S(1)}, bf16[768,2304]{1,0:T(8,128)(2,1)}, u32[]{:S(2)}) copy-start(bf16[768,2304]{1,0:T(8,128)(2,1)} %param.33) | copy-start | bytes 10616836
  0.6 13.6 %collective-permute-start.1 = (s32[2]{0:T(128)}, s32[2]{0:T(128)}, u32[]{:S(2)}, u32[]{:S(2)}) collective-permute-start(s32[2]{0:T(128)} %param.27), channel_id=1, source_target_pairs={{0,16},{16,0},{1,17},{17,1},{2,18},{18,2},{3,19},{19,3},{4,20},{20... | collective-permute-start | bytes 32 | tf_op jit(solution)/shard_map/ppermute | solution.py:309
  5.2 80.7 %collective-permute-start.4 = (bf16[96,1024]{1,0:T(8,128)(2,1)}, bf16[96,1024]{1,0:T(8,128)(2,1)}, u32[]{:S(2)}, u32[]{:S(2)}) collective-permute-start(bf16[96,1024]{1,0:T(8,128)(2,1)} %bitcast.11), channel_id=1, source_target_pairs={{0,16},{16,0},{1,17},{17,1},{2,18},{18,2},{3,19},{19,3},{4,20},{20... | collective-permute-start | bytes 589832 | tf_op jit(solution)/shard_map/ppermute | solution.py:309
  8.1 7.6 %collective-permute-start.2 = (bf16[96,1024]{1,0:T(8,128)(2,1)S(1)}, bf16[96,1024]{1,0:T(8,128)(2,1)S(1)}, u32[]{:S(2)}, u32[]{:S(2)}) collective-permute-start(bf16[96,1024]{1,0:T(8,128)(2,1)S(1)} %bitcast.147), channel_id=1, source_target_pairs={{0,16},{16,0},{1,17},{17,1},{2,18},{18,2},{3,19},{19,3},{4,20},{20... | collective-permute-start | bytes 589832 | tf_op jit(solution)/shard_map/ppermute | solution.py:309
  9.2 14.7 %collective-permute-start = (bf16[256,768]{1,0:T(8,128)(2,1)}, bf16[256,768]{1,0:T(8,128)(2,1)S(1)}, u32[]{:S(2)}, u32[]{:S(2)}) collective-permute-start(bf16[256,768]{1,0:T(8,128)(2,1)} %param.25), channel_id=1, source_target_pairs={{0,16},{16,0},{1,17},{17,1},{2,18},{18,2},{3,19},{19,3},{4,20},{20... | collective-permute-start | bytes 1179656 | tf_op jit(solution)/shard_map/ppermute | solution.py:309
  9.7 165.5 %collective-permute-start.3 = (bf16[256,768]{1,0:T(8,128)(2,1)}, bf16[256,768]{1,0:T(8,128)(2,1)}, u32[]{:S(2)}, u32[]{:S(2)}) collective-permute-start(bf16[256,768]{1,0:T(8,128)(2,1)} %param.44), channel_id=1, source_target_pairs={{0,16},{16,0},{1,17},{17,1},{2,18},{18,2},{3,19},{19,3},{4,20},{20... | collective-permute-start | bytes 1179656 | tf_op jit(solution)/shard_map/ppermute | solution.py:309
  16.6 251.1 %collective-permute-start.32 = (bf16[192,1024]{1,0:T(8,128)(2,1)}, bf16[192,1024]{1,0:T(8,128)(2,1)}, u32[]{:S(2)}, u32[]{:S(2)}) collective-permute-start(bf16[192,1024]{1,0:T(8,128)(2,1)} %pad_maximum_fusion.3), channel_id=1, source_target_pairs={{0,1},{1,0},{2,3},{3,2},{4,5},{5,4},{6,7},{7,6},{8,9},{9,8},{10,11... | collective-permute-start | bytes 1179656 | tf_op jit(solution)/shard_map/ppermute | solution.py:305
  56.8 211.4 %collective-permute-start.35 = (bf16[192,1024]{1,0:T(8,128)(2,1)}, bf16[192,1024]{1,0:T(8,128)(2,1)}, u32[]{:S(2)}, u32[]{:S(2)}) collective-permute-start(bf16[192,1024]{1,0:T(8,128)(2,1)} %attend.6), channel_id=1, source_target_pairs={{0,1},{1,0},{2,3},{3,2},{4,5},{5,4},{6,7},{7,6},{8,9},{9,8},{10,11... | collective-permute-start | bytes 1179656 | tf_op jit(solution)/shard_map/ppermute | solution.py:305
  63.3 204.4 %collective-permute-start.37 = (bf16[192,1024]{1,0:T(8,128)(2,1)}, bf16[192,1024]{1,0:T(8,128)(2,1)}, u32[]{:S(2)}, u32[]{:S(2)}) collective-permute-start(bf16[192,1024]{1,0:T(8,128)(2,1)} %multiply_convert_fusion.5), channel_id=1, source_target_pairs={{0,1},{1,0},{2,3},{3,2},{4,5},{5,4},{6,7},{7,6},{8,9},{9,8},{10,11... | collective-permute-start | bytes 1179656 | tf_op jit(solution)/shard_map/ppermute | solution.py:305
  85.9 189.9 %collective-permute-start.26 = (bf16[192,1024]{1,0:T(8,128)(2,1)}, bf16[192,1024]{1,0:T(8,128)(2,1)}, u32[]{:S(2)}, u32[]{:S(2)}) collective-permute-start(bf16[192,1024]{1,0:T(8,128)(2,1)} %get-tuple-element.266), channel_id=1, source_target_pairs={{0,1},{1,0},{2,3},{3,2},{4,5},{5,4},{6,7},{7,6},{8,9},{9,8},{10,11... | collective-permute-start | bytes 1179656 | tf_op jit(solution)/shard_map/ppermute | solution.py:305
  175.1 101.1 %collective-permute-start.28 = (bf16[192,1024]{1,0:T(8,128)(2,1)}, bf16[192,1024]{1,0:T(8,128)(2,1)}, u32[]{:S(2)}, u32[]{:S(2)}) collective-permute-start(bf16[192,1024]{1,0:T(8,128)(2,1)} %multiply_convert_fusion.4), channel_id=1, source_target_pairs={{0,1},{1,0},{2,3},{3,2},{4,5},{5,4},{6,7},{7,6},{8,9},{9,8},{10,11... | collective-permute-start | bytes 1179656 | tf_op jit(solution)/shard_map/ppermute | solution.py:305
  267.7 8.7 %collective-permute-start.30 = (bf16[192,1024]{1,0:T(8,128)(2,1)S(1)}, bf16[192,1024]{1,0:T(8,128)(2,1)S(1)}, u32[]{:S(2)}, u32[]{:S(2)}) collective-permute-start(bf16[192,1024]{1,0:T(8,128)(2,1)S(1)} %copy-done.29), channel_id=1, source_target_pairs={{0,1},{1,0},{2,3},{3,2},{4,5},{5,4},{6,7},{7,6},{8,9},{9,8},{10,11... | collective-permute-start | bytes 1179656 | tf_op jit(solution)/shard_map/ppermute | solution.py:305
  267.8 9.2 %collective-permute-start.36 = (bf16[192,1024]{1,0:T(8,128)(2,1)S(1)}, bf16[192,1024]{1,0:T(8,128)(2,1)S(1)}, u32[]{:S(2)}, u32[]{:S(2)}) collective-permute-start(bf16[192,1024]{1,0:T(8,128)(2,1)S(1)} %copy-done.35), channel_id=1, source_target_pairs={{0,1},{1,0},{2,3},{3,2},{4,5},{5,4},{6,7},{7,6},{8,9},{9,8},{10,11... | collective-permute-start | bytes 1179656 | tf_op jit(solution)/shard_map/ppermute | solution.py:305
  268.2 8.6 %collective-permute-start.33 = (bf16[192,1024]{1,0:T(8,128)(2,1)}, bf16[192,1024]{1,0:T(8,128)(2,1)S(1)}, u32[]{:S(2)}, u32[]{:S(2)}) collective-permute-start(bf16[192,1024]{1,0:T(8,128)(2,1)} %get-tuple-element.204), channel_id=1, source_target_pairs={{0,1},{1,0},{2,3},{3,2},{4,5},{5,4},{6,7},{7,6},{8,9},{9,8},{10,11... | collective-permute-start | bytes 1179656 | tf_op jit(solution)/shard_map/ppermute | solution.py:305
  275.8 7.1 %collective-permute-start.13 = (bf16[512,768]{1,0:T(8,128)(2,1)S(1)}, bf16[512,768]{1,0:T(8,128)(2,1)S(1)}, u32[]{:S(2)}, u32[]{:S(2)}) collective-permute-start(bf16[512,768]{1,0:T(8,128)(2,1)S(1)} %copy-done.21), channel_id=1, source_target_pairs={{0,1},{1,0},{2,3},{3,2},{4,5},{5,4},{6,7},{7,6},{8,9},{9,8},{10,11... | collective-permute-start | bytes 2359304 | tf_op jit(solution)/shard_map/ppermute | solution.py:305
  276.2 3.0 collective-permute-start.38
  276.3 34.9 %collective-permute-start.5 = (bf16[512,768]{1,0:T(8,128)(2,1)}, bf16[512,768]{1,0:T(8,128)(2,1)}, u32[]{:S(2)}, u32[]{:S(2)}) collective-permute-start(bf16[512,768]{1,0:T(8,128)(2,1)} %multiply_convert_fusion.2), channel_id=1, source_target_pairs={{0,1},{1,0},{2,3},{3,2},{4,5},{5,4},{6,7},{7,6},{8,9},{9,8},{10,11... | collective-permute-start | bytes 2359304 | tf_op jit(solution)/shard_map/ppermute | solution.py:305
  276.8 5.5 collective-permute-start.27
  277.0 5.6 collective-permute-start.31
  280.1 31.6 %collective-permute-start.9 = (bf16[512,768]{1,0:T(8,128)(2,1)}, bf16[512,768]{1,0:T(8,128)(2,1)}, u32[]{:S(2)}, u32[]{:S(2)}) collective-permute-start(bf16[512,768]{1,0:T(8,128)(2,1)} %multiply_convert_fusion.1), channel_id=1, source_target_pairs={{0,1},{1,0},{2,3},{3,2},{4,5},{5,4},{6,7},{7,6},{8,9},{9,8},{10,11... | collective-permute-start | bytes 2359304 | tf_op jit(solution)/shard_map/ppermute | solution.py:305
  282.3 29.5 %collective-permute-start.11 = (bf16[512,768]{1,0:T(8,128)(2,1)}, bf16[512,768]{1,0:T(8,128)(2,1)}, u32[]{:S(2)}, u32[]{:S(2)}) collective-permute-start(bf16[512,768]{1,0:T(8,128)(2,1)} %attend.5), channel_id=1, source_target_pairs={{0,1},{1,0},{2,3},{3,2},{4,5},{5,4},{6,7},{7,6},{8,9},{9,8},{10,11... | collective-permute-start | bytes 2359304 | tf_op jit(solution)/shard_map/ppermute | solution.py:305
  282.5 69.1 %collective-permute-start.6 = (bf16[512,3072]{1,0:T(8,128)(2,1)}, bf16[512,3072]{1,0:T(8,128)(2,1)S(1)}, u32[]{:S(2)}, u32[]{:S(2)}) collective-permute-start(bf16[512,3072]{1,0:T(8,128)(2,1)} %fusion.5), channel_id=1, source_target_pairs={{0,1},{1,0},{2,3},{3,2},{4,5},{5,4},{6,7},{7,6},{8,9},{9,8},{10,11... | collective-permute-start | bytes 9437192 | tf_op jit(solution)/shard_map/ppermute | solution.py:305
  283.8 28.4 %collective-permute-start.17 = (bf16[512,768]{1,0:T(8,128)(2,1)}, bf16[512,768]{1,0:T(8,128)(2,1)}, u32[]{:S(2)}, u32[]{:S(2)}) collective-permute-start(bf16[512,768]{1,0:T(8,128)(2,1)} %get-tuple-element.229), channel_id=1, source_target_pairs={{0,1},{1,0},{2,3},{3,2},{4,5},{5,4},{6,7},{7,6},{8,9},{9,8},{10,11... | collective-permute-start | bytes 2359304 | tf_op jit(solution)/shard_map/ppermute | solution.py:305
  311.3 2.7 collective-permute-start.34
  311.7 3.8 collective-permute-start.16
  311.8 46.4 %collective-permute-start.7 = (bf16[512,3072]{1,0:T(8,128)(2,1)}, bf16[512,3072]{1,0:T(8,128)(2,1)}, u32[]{:S(2)}, u32[]{:S(2)}) collective-permute-start(bf16[512,3072]{1,0:T(8,128)(2,1)} %copy-done.40), channel_id=1, source_target_pairs={{0,1},{1,0},{2,3},{3,2},{4,5},{5,4},{6,7},{7,6},{8,9},{9,8},{10,11... | collective-permute-start | bytes 9437192 | tf_op jit(solution)/shard_map/ppermute | solution.py:305
  312.2 9.4 %collective-permute-start.29 = (bf16[192,3072]{1,0:T(8,128)(2,1)}, bf16[192,3072]{1,0:T(8,128)(2,1)}, u32[]{:S(2)}, u32[]{:S(2)}) collective-permute-start(bf16[192,3072]{1,0:T(8,128)(2,1)} %attend_back.6), channel_id=1, source_target_pairs={{0,1},{1,0},{2,3},{3,2},{4,5},{5,4},{6,7},{7,6},{8,9},{9,8},{10,11... | collective-permute-start | bytes 3538952 | tf_op jit(solution)/shard_map/ppermute | solution.py:305
  314.0 37.3 %collective-permute-start.15 = (bf16[512,2048]{1,0:T(8,128)(2,1)}, bf16[512,2048]{1,0:T(8,128)(2,1)}, u32[]{:S(2)}, u32[]{:S(2)}) collective-permute-start(bf16[512,2048]{1,0:T(8,128)(2,1)} %get-tuple-element.203), channel_id=1, source_target_pairs={{0,1},{1,0},{2,3},{3,2},{4,5},{5,4},{6,7},{7,6},{8,9},{9,8},{10,11... | collective-permute-start | bytes 6291464 | tf_op jit(solution)/shard_map/ppermute | solution.py:305
  315.5 42.8 %collective-permute-start.10 = (bf16[512,2304]{1,0:T(8,128)(2,1)}, bf16[512,2304]{1,0:T(8,128)(2,1)}, u32[]{:S(2)}, u32[]{:S(2)}) collective-permute-start(bf16[512,2304]{1,0:T(8,128)(2,1)} %attend_back.4), channel_id=1, source_target_pairs={{0,1},{1,0},{2,3},{3,2},{4,5},{5,4},{6,7},{7,6},{8,9},{9,8},{10,11... | collective-permute-start | bytes 7077896 | tf_op jit(solution)/shard_map/ppermute | solution.py:305
  321.6 29.5 %collective-permute-start.14 = (bf16[512,1024]{1,0:T(8,128)(2,1)}, bf16[512,1024]{1,0:T(8,128)(2,1)}, u32[]{:S(2)}, u32[]{:S(2)}) collective-permute-start(bf16[512,1024]{1,0:T(8,128)(2,1)} %get-tuple-element.202), channel_id=1, source_target_pairs={{0,1},{1,0},{2,3},{3,2},{4,5},{5,4},{6,7},{7,6},{8,9},{9,8},{10,11... | collective-permute-start | bytes 3145736 | tf_op jit(solution)/shard_map/ppermute | solution.py:305
  351.1 7.1 %collective-permute-start.8 = (bf16[512,768]{1,0:T(8,128)(2,1)S(1)}, bf16[512,768]{1,0:T(8,128)(2,1)S(1)}, u32[]{:S(2)}, u32[]{:S(2)}) collective-permute-start(bf16[512,768]{1,0:T(8,128)(2,1)S(1)} %copy-done.43), channel_id=1, source_target_pairs={{0,1},{1,0},{2,3},{3,2},{4,5},{5,4},{6,7},{7,6},{8,9},{9,8},{10,11... | collective-permute-start | bytes 2359304 | tf_op jit(solution)/shard_map/ppermute | solution.py:305
  351.3 7.0 %collective-permute-start.12 = (bf16[512,768]{1,0:T(8,128)(2,1)}, bf16[512,768]{1,0:T(8,128)(2,1)S(1)}, u32[]{:S(2)}, u32[]{:S(2)}) collective-permute-start(bf16[512,768]{1,0:T(8,128)(2,1)} %copy-done.44), channel_id=1, source_target_pairs={{0,1},{1,0},{2,3},{3,2},{4,5},{5,4},{6,7},{7,6},{8,9},{9,8},{10,11... | collective-permute-start | bytes 2359304 | tf_op jit(solution)/shard_map/ppermute | solution.py:305
  351.6 158.6 %collective-permute-start.39 = (bf16[4,2560,128]{2,1,0:T(8,128)(2,1)}, bf16[4,2560,128]{2,1,0:T(8,128)(2,1)}, u32[]{:S(2)}, u32[]{:S(2)}) collective-permute-start(bf16[4,2560,128]{2,1,0:T(8,128)(2,1)} %dynamic-slice_bitcast_fusion), channel_id=1, source_target_pairs={{0,2},{1,3},{2,0},{3,1},{4,6},{5,7},{6,4},{7,5},{8,10},{9,11},{10,... | collective-permute-start | bytes 7864328 | tf_op jit(solution)/shard_map/ppermute | solution.py:305
  392.1 123.5 %collective-permute-start.18 = (bf16[4,2496,128]{2,1,0:T(8,128)(2,1)}, bf16[4,2496,128]{2,1,0:T(8,128)(2,1)}, u32[]{:S(2)}, u32[]{:S(2)}) collective-permute-start(bf16[4,2496,128]{2,1,0:T(8,128)(2,1)} %dynamic-slice_bitcast_fusion.1), channel_id=1, source_target_pairs={{0,2},{1,3},{2,0},{3,1},{4,6},{5,7},{6,4},{7,5},{8,10},{9,11},{10,... | collective-permute-start | bytes 7667720 | tf_op jit(solution)/shard_map/ppermute | solution.py:305
  513.6 19.5 %collective-permute-start.40 = (bf16[2560,128]{1,0:T(8,128)(2,1)S(1)}, bf16[2560,128]{1,0:T(8,128)(2,1)S(1)}, u32[]{:S(2)}, u32[]{:S(2)}) collective-permute-start(bf16[2560,128]{1,0:T(8,128)(2,1)S(1)} %get-tuple-element.245), channel_id=1, source_target_pairs={{0,4},{1,5},{2,6},{3,7},{16,20},{17,21},{18,22},{19,23}} | collective-permute-start | bytes 1966088 | tf_op jit(solution)/shard_map/ppermute | solution.py:329
  514.9 34.0 %collective-permute-start.43 = (bf16[2560,128]{1,0:T(8,128)(2,1)S(1)}, bf16[2560,128]{1,0:T(8,128)(2,1)S(1)}, u32[]{:S(2)}, u32[]{:S(2)}) collective-permute-start(bf16[2560,128]{1,0:T(8,128)(2,1)S(1)} %get-tuple-element.246), channel_id=1, source_target_pairs={{12,8},{13,9},{14,10},{15,11},{28,24},{29,25},{30,26},{31,27}} | collective-permute-start | bytes 1966088 | tf_op jit(solution)/shard_map/ppermute | solution.py:329
  518.9 27.9 %collective-permute-start.19 = (bf16[2496,128]{1,0:T(8,128)(2,1)S(1)}, bf16[2496,128]{1,0:T(8,128)(2,1)S(1)}, u32[]{:S(2)}, u32[]{:S(2)}) collective-permute-start(bf16[2496,128]{1,0:T(8,128)(2,1)S(1)} %get-tuple-element.249), channel_id=1, source_target_pairs={{0,4},{1,5},{2,6},{3,7},{16,20},{17,21},{18,22},{19,23}} | collective-permute-start | bytes 1916936 | tf_op jit(solution)/shard_map/ppermute | solution.py:329
  533.2 27.6 %collective-permute-start.41 = (bf16[2560,128]{1,0:T(8,128)(2,1)S(1)}, bf16[2560,128]{1,0:T(8,128)(2,1)S(1)}, u32[]{:S(2)}, u32[]{:S(2)}) collective-permute-start(bf16[2560,128]{1,0:T(8,128)(2,1)S(1)} %fusion.12), channel_id=1, source_target_pairs={{0,4},{1,5},{2,6},{3,7},{4,8},{5,9},{6,10},{7,11},{16,20},{17,21},... | collective-permute-start | bytes 1966088 | tf_op jit(solution)/shard_map/ppermute | solution.py:329
  535.2 29.2 %collective-permute-start.22 = (bf16[2496,128]{1,0:T(8,128)(2,1)S(1)}, bf16[2496,128]{1,0:T(8,128)(2,1)S(1)}, u32[]{:S(2)}, u32[]{:S(2)}) collective-permute-start(bf16[2496,128]{1,0:T(8,128)(2,1)S(1)} %get-tuple-element.250), channel_id=1, source_target_pairs={{12,8},{13,9},{14,10},{15,11},{28,24},{29,25},{30,26},{31,27}} | collective-permute-start | bytes 1916936 | tf_op jit(solution)/shard_map/ppermute | solution.py:329
  546.9 27.6 %collective-permute-start.20 = (bf16[2496,128]{1,0:T(8,128)(2,1)S(1)}, bf16[2496,128]{1,0:T(8,128)(2,1)S(1)}, u32[]{:S(2)}, u32[]{:S(2)}) collective-permute-start(bf16[2496,128]{1,0:T(8,128)(2,1)S(1)} %fusion.17), channel_id=1, source_target_pairs={{0,4},{1,5},{2,6},{3,7},{4,8},{5,9},{6,10},{7,11},{16,20},{17,21},... | collective-permute-start | bytes 1916936 | tf_op jit(solution)/shard_map/ppermute | solution.py:329
  561.1 34.0 %collective-permute-start.42 = (bf16[2560,128]{1,0:T(8,128)(2,1)S(1)}, bf16[2560,128]{1,0:T(8,128)(2,1)S(1)}, u32[]{:S(2)}, u32[]{:S(2)}) collective-permute-start(bf16[2560,128]{1,0:T(8,128)(2,1)S(1)} %get-tuple-element.243), channel_id=1, source_target_pairs={{0,4},{1,5},{2,6},{3,7},{4,8},{5,9},{6,10},{7,11},{8,12},{9,13},{1... | collective-permute-start | bytes 1966088 | tf_op jit(solution)/shard_map/ppermute | solution.py:329
  563.1 13.1 %collective-permute-start.44 = (bf16[2560,128]{1,0:T(8,128)(2,1)S(1)}, bf16[2560,128]{1,0:T(8,128)(2,1)S(1)}, u32[]{:S(2)}, u32[]{:S(2)}) collective-permute-start(bf16[2560,128]{1,0:T(8,128)(2,1)S(1)} %get-tuple-element.244), channel_id=1, source_target_pairs={{8,4},{9,5},{10,6},{11,7},{12,8},{13,9},{14,10},{15,11},{24,20},{2... | collective-permute-start | bytes 1966088 | tf_op jit(solution)/shard_map/ppermute | solution.py:329
  574.8 18.2 %collective-permute-start.23 = (bf16[2496,128]{1,0:T(8,128)(2,1)S(1)}, bf16[2496,128]{1,0:T(8,128)(2,1)S(1)}, u32[]{:S(2)}, u32[]{:S(2)}) collective-permute-start(bf16[2496,128]{1,0:T(8,128)(2,1)S(1)} %get-tuple-element.248), channel_id=1, source_target_pairs={{8,4},{9,5},{10,6},{11,7},{12,8},{13,9},{14,10},{15,11},{24,20},{2... | collective-permute-start | bytes 1916936 | tf_op jit(solution)/shard_map/ppermute | solution.py:329
  576.3 30.7 %collective-permute-start.45 = (bf16[2560,128]{1,0:T(8,128)(2,1)S(1)}, bf16[2560,128]{1,0:T(8,128)(2,1)S(1)}, u32[]{:S(2)}, u32[]{:S(2)}) collective-permute-start(bf16[2560,128]{1,0:T(8,128)(2,1)S(1)} %fusion.11), channel_id=1, source_target_pairs={{4,0},{5,1},{6,2},{7,3},{8,4},{9,5},{10,6},{11,7},{12,8},{13,9},{1... | collective-permute-start | bytes 1966088 | tf_op jit(solution)/shard_map/ppermute | solution.py:329
  578.3 43.1 %collective-permute-start.21 = (bf16[2496,128]{1,0:T(8,128)(2,1)S(1)}, bf16[2496,128]{1,0:T(8,128)(2,1)S(1)}, u32[]{:S(2)}, u32[]{:S(2)}) collective-permute-start(bf16[2496,128]{1,0:T(8,128)(2,1)S(1)} %get-tuple-element.247), channel_id=1, source_target_pairs={{0,4},{1,5},{2,6},{3,7},{4,8},{5,9},{6,10},{7,11},{8,12},{9,13},{1... | collective-permute-start | bytes 1916936 | tf_op jit(solution)/shard_map/ppermute | solution.py:329
  593.2 28.2 %collective-permute-start.24 = (bf16[2496,128]{1,0:T(8,128)(2,1)S(1)}, bf16[2496,128]{1,0:T(8,128)(2,1)S(1)}, u32[]{:S(2)}, u32[]{:S(2)}) collective-permute-start(bf16[2496,128]{1,0:T(8,128)(2,1)S(1)} %fusion.16), channel_id=1, source_target_pairs={{4,0},{5,1},{6,2},{7,3},{8,4},{9,5},{10,6},{11,7},{12,8},{13,9},{1... | collective-permute-start | bytes 1916936 | tf_op jit(solution)/shard_map/ppermute | solution.py:329
  607.4 20.9 %collective-permute-start.46 = (f32[1280,128]{1,0:T(8,128)S(1)}, f32[1280,128]{1,0:T(8,128)S(1)}, u32[]{:S(2)}, u32[]{:S(2)}) collective-permute-start(f32[1280,128]{1,0:T(8,128)S(1)} %dynamic-slice_bitcast_fusion.2), channel_id=1, source_target_pairs={{0,1},{1,0},{2,3},{3,2},{4,5},{5,4},{6,7},{7,6},{8,9},{9,8},{10,11... | collective-permute-start | bytes 1966088 | tf_op jit(solution)/shard_map/ppermute | solution.py:305
  621.6 8.9 %collective-permute-start.25 = (f32[1248,128]{1,0:T(8,128)S(1)}, f32[1248,128]{1,0:T(8,128)S(1)}, u32[]{:S(2)}, u32[]{:S(2)}) collective-permute-start(f32[1248,128]{1,0:T(8,128)S(1)} %dynamic-slice_bitcast_fusion.5), channel_id=1, source_target_pairs={{0,1},{1,0},{2,3},{3,2},{4,5},{5,4},{6,7},{7,6},{8,9},{9,8},{10,11... | collective-permute-start | bytes 1916936 | tf_op jit(solution)/shard_map/ppermute | solution.py:305
  (111 other events, 839.2 us)

commit v2 on v1

v2 whole, which is shorter than its diff:
```python
import functools

import jax
import jax.numpy as jnp
from jax import lax
from jax.experimental import pallas as pl
from jax.experimental.pallas import tpu as pltpu
from jax.sharding import PartitionSpec as P

H_T = 12
H_I = 8
H_C = 8
D_C = 1024
LANES = 128
UNIT = 256
masked_score = -1e30
F32 = jnp.float32
BF16 = jnp.bfloat16


def mm(a, b):
    return jnp.dot(a, b, preferred_element_type=F32)


def mm_nt(a, b):
    return lax.dot_general(a, b, (((1,), (1,)), ((), ())), preferred_element_type=F32)


def mm_tn(a, b):
    return lax.dot_general(a, b, (((0,), (0,)), ((), ())), preferred_element_type=F32)


def cost(flops, nbytes, trans=0):
    return pl.CostEstimate(
        flops=int(flops), bytes_accessed=int(nbytes), transcendentals=int(trans)
    )


def lane_block(ref, rows, block):
    return ref[rows, pl.ds(pl.multiple_of(block * LANES, LANES), LANES)]


def put_block(ref, rows, block, value):
    ref[rows, pl.ds(pl.multiple_of(block * LANES, LANES), LANES)] = value


def split_heads(block, heads_in):
    if heads_in == 1:
        return block
    lanes = lax.broadcasted_iota(jnp.int32, block.shape, 1)
    zero = jnp.zeros_like(block)
    low = lanes < LANES // 2
    return jnp.concatenate([jnp.where(low, block, zero), jnp.where(low, zero, block)], axis=0)


def side_by_side(block, heads_in):
    if heads_in == 1:
        return block
    rows = block.shape[0] // 2
    return jnp.concatenate([block[:rows], block[rows:]], axis=1)


def attend_kernel(
    lens_ref, q_ref, k_ref, v_ref, o_ref, *, pairs, blocks, cols, heads_in, fixed, scaling
):
    ql = q_ref.shape[0] // pairs
    kl = k_ref.shape[0] // pairs
    chain = heads_in * ql
    keys = lax.broadcasted_iota(jnp.int32, (chain, kl), 1)
    if fixed is None:
        masks = [keys < lens_ref[p] for p in range(pairs)]
    else:
        masks = [keys < fixed] * pairs

    @pl.loop(0, blocks)
    def _(j):
        scores = []
        for p in range(pairs):
            q = split_heads(lane_block(q_ref, slice(p * ql, (p + 1) * ql), cols[0] + j), heads_in)
            k = lane_block(k_ref, slice(p * kl, (p + 1) * kl), cols[1] + j)
            scores.append(jnp.where(masks[p], mm_nt(q, k) * scaling, masked_score))
        s = jnp.concatenate(scores, axis=0)
        raised = jnp.exp(s - jnp.max(s, axis=-1, keepdims=True))
        w = (raised * (1.0 / jnp.sum(raised, axis=-1, keepdims=True))).astype(BF16)
        for p in range(pairs):
            v = split_heads(lane_block(v_ref, slice(p * kl, (p + 1) * kl), cols[2] + j), heads_in)
            o = mm(side_by_side(w[p * chain : (p + 1) * chain], heads_in), v)
            put_block(o_ref, slice(p * ql, (p + 1) * ql), j, o.astype(BF16))


def attend(lens, q, k, v, cols, pairs, blocks, heads_in, fixed, scaling):
    rows = q.shape[0]
    krows = k.shape[0]
    same = k is v
    vmem = pl.BlockSpec(memory_space=pltpu.VMEM)
    operands = [lens, q, k] if same else [lens, q, k, v]
    if q is k:
        operands = [lens, q]

    def body(lens_ref, *refs, **kw):
        refs = list(refs)
        o_ref = refs.pop()
        while len(refs) < 3:
            refs.append(refs[-1])
        attend_kernel(lens_ref, *refs, o_ref, **kw)

    return pl.pallas_call(
        functools.partial(
            body,
            pairs=pairs,
            blocks=blocks,
            cols=cols,
            heads_in=heads_in,
            fixed=fixed,
            scaling=scaling,
        ),
        in_specs=[pl.BlockSpec(memory_space=pltpu.SMEM)] + [vmem] * (len(operands) - 1),
        out_specs=vmem,
        out_shape=jax.ShapeDtypeStruct((rows, blocks * LANES), BF16),
        compiler_params=pltpu.CompilerParams(vmem_limit_bytes=24 * 1024 * 1024),
        cost_estimate=cost(
            16 * blocks * heads_in * rows * krows // pairs * LANES,
            4 * blocks * LANES * (rows + krows),
            blocks * heads_in * rows * krows // pairs,
        ),
        name="attend",
    )(*operands)


def attend_back_kernel(
    lens_ref,
    q_ref,
    k_ref,
    v_ref,
    g_ref,
    dq_ref,
    dk_ref,
    dv_ref,
    *,
    pairs,
    blocks,
    cols,
    out_cols,
    heads_in,
    fixed,
    scaling,
):
    ql = q_ref.shape[0] // pairs
    kl = k_ref.shape[0] // pairs
    keys = lax.broadcasted_iota(jnp.int32, (heads_in * kl, ql), 0)
    if heads_in == 2:
        keys = jnp.where(keys >= kl, keys - kl, keys)
    if fixed is None:
        masks = [keys < lens_ref[p] for p in range(pairs)]
    else:
        masks = [keys < fixed] * pairs

    @pl.loop(0, blocks)
    def _(j):
        scores, slopes = [], []
        for p in range(pairs):
            qs, ks = slice(p * ql, (p + 1) * ql), slice(p * kl, (p + 1) * kl)
            q, g = lane_block(q_ref, qs, cols[0] + j), lane_block(g_ref, qs, j)
            k = split_heads(lane_block(k_ref, ks, cols[1] + j), heads_in)
            v = split_heads(lane_block(v_ref, ks, cols[2] + j), heads_in)
            scores.append(jnp.where(masks[p], mm_nt(k, q) * scaling, masked_score))
            slopes.append(mm_nt(v, g))
        stacked = (pairs * heads_in, kl, ql)
        s = jnp.concatenate(scores, axis=0).reshape(stacked)
        dp = jnp.concatenate(slopes, axis=0).reshape(stacked)
        raised = jnp.exp(s - jnp.max(s, axis=1, keepdims=True))
        w = raised * (1.0 / jnp.sum(raised, axis=1, keepdims=True))
        inner = jnp.sum(w * dp, axis=1, keepdims=True)
        ds = (w * (dp - inner)).astype(BF16).reshape(-1, ql)
        w = w.astype(BF16).reshape(-1, ql)
        chain = heads_in * kl
        for p in range(pairs):
            qs, ks = slice(p * ql, (p + 1) * ql), slice(p * kl, (p + 1) * kl)
            own = slice(p * chain, (p + 1) * chain)
            q = split_heads(lane_block(q_ref, qs, cols[0] + j), heads_in)
            g = split_heads(lane_block(g_ref, qs, j), heads_in)
            k = split_heads(lane_block(k_ref, ks, cols[1] + j), heads_in)
            dq = mm_tn(ds[own], k) * scaling
            dk = mm(side_by_side(ds[own], heads_in), q) * scaling
            dv = mm(side_by_side(w[own], heads_in), g)
            put_block(dq_ref, qs, out_cols[0] + j, dq.astype(BF16))
            put_block(dk_ref, ks, out_cols[1] + j, dk.astype(BF16))
            put_block(dv_ref, ks, out_cols[2] + j, dv.astype(BF16))


def attend_back(lens, q, k, v, g, cols, pairs, blocks, heads_in, fixed, scaling, packed):
    rows = q.shape[0]
    krows = k.shape[0]
    vmem = pl.BlockSpec(memory_space=pltpu.VMEM)
    width = blocks * LANES
    if packed:
        operands = [lens, q, g]
        out_cols = (0, blocks, 2 * blocks)
        out_shape = jax.ShapeDtypeStruct((rows, 3 * width), BF16)
        out_specs = vmem
    else:
        operands = [lens, q, k, g]
        out_cols = (0, 0, blocks)
        out_shape = [
            jax.ShapeDtypeStruct((rows, width), BF16),
            jax.ShapeDtypeStruct((krows, 2 * width), BF16),
        ]
        out_specs = [vmem, vmem]

    def body(lens_ref, *refs, **kw):
        if packed:
            q_ref, g_ref, out_ref = refs
            ins, outs = (q_ref, q_ref, q_ref, g_ref), (out_ref,) * 3
        else:
            q_ref, k_ref, g_ref, dq_ref, dkv_ref = refs
            ins, outs = (q_ref, k_ref, k_ref, g_ref), (dq_ref, dkv_ref, dkv_ref)
        attend_back_kernel(lens_ref, *ins, *outs, **kw)

    return pl.pallas_call(
        functools.partial(
            body,
            pairs=pairs,
            blocks=blocks,
            cols=cols,
            out_cols=out_cols,
            heads_in=heads_in,
            fixed=fixed,
            scaling=scaling,
        ),
        in_specs=[pl.BlockSpec(memory_space=pltpu.SMEM)] + [vmem] * (len(operands) - 1),
        out_specs=out_specs,
        out_shape=out_shape,
        compiler_params=pltpu.CompilerParams(vmem_limit_bytes=24 * 1024 * 1024),
        cost_estimate=cost(
            40 * blocks * heads_in * rows * krows // pairs * LANES,
            8 * blocks * LANES * (rows + krows),
            blocks * heads_in * rows * krows // pairs,
        ),
        name="attend_back",
    )(*operands)


def flat_kernel(
    side_ref, a0_ref, a1_ref, b0_ref, b1_ref, *rest, place, bm, low, units, quarter
):
    out_ref, stage_ref, low_ref, b_ref, sem = rest[-5:]
    core = side_ref[0]
    depth = a0_ref.shape[0]
    for u in range(units):
        at = 2 * u + core
        if quarter:
            at = 4 * u + 2 * side_ref[1] + core
        chosen = pl.ds(pl.multiple_of(at * LANES, LANES), LANES)
        b_ref[:depth, u * LANES : (u + 1) * LANES] = b0_ref[:, chosen]
        b_ref[depth:, u * LANES : (u + 1) * LANES] = b1_ref[:, chosen]
    rows = bm * units
    steps = (low[1] - low[0]) // bm

    def copy(i):
        return pltpu.make_async_copy(
            low_ref.at[i % 2], out_ref.at[pl.ds(place + i * rows, rows)], sem.at[i % 2]
        )

    for i in range(steps):
        columns = slice(low[0] + i * bm, low[0] + (i + 1) * bm)
        a = jnp.concatenate([a0_ref[:, columns], a1_ref[:, columns]], axis=0).T
        for u0 in range(0, units, 4):
            u1 = min(u0 + 4, units)
            total = mm(a, b_ref[:, u0 * LANES : u1 * LANES])
            for u in range(u0, u1):
                stage_ref[pl.ds(u, bm, stride=units), :] = total[
                    :, (u - u0) * LANES : (u - u0 + 1) * LANES
                ]
        if i >= 2:
            copy(i - 2).wait()
        low_ref[i % 2] = stage_ref[...].astype(BF16)
        copy(i).start()
    for i in range(max(steps - 2, 0), steps):
        copy(i).wait()


def flat_grad(flat, total_rows, side, a, b, low, high, place, quarter=False):
    a0, a1 = a
    b0, b1 = b
    depth = a0.shape[0]
    columns = b0.shape[1]
    units = columns // (2 * UNIT if quarter else UNIT)
    most = 512 if units <= 8 else 384
    bm = LANES
    for size in range(LANES, most + 1, LANES):
        if (high - low) % size == 0:
            bm = size
    out_rows = bm * units
    vmem = pl.BlockSpec(memory_space=pltpu.VMEM)
    in_specs = [pl.BlockSpec(memory_space=pltpu.SMEM)] + [vmem] * 4
    operands = [side, a0, a1, b0, b1]
    aliases = {}
    if flat is not None:
        in_specs.append(pl.BlockSpec(memory_space=pl.ANY))
        operands.append(flat)
        aliases = {5: 0}
    return pl.pallas_call(
        functools.partial(
            flat_kernel, place=place, bm=bm, low=(low, high), units=units, quarter=quarter
        ),
        in_specs=in_specs,
        out_specs=pl.BlockSpec(memory_space=pl.ANY),
        out_shape=jax.ShapeDtypeStruct((total_rows, LANES), BF16),
        scratch_shapes=[
            pltpu.VMEM((out_rows, LANES), F32),
            pltpu.VMEM((2, out_rows, LANES), BF16),
            pltpu.VMEM((2 * depth, units * LANES), BF16),
            pltpu.SemaphoreType.DMA((2,)),
        ],
        input_output_aliases=aliases,
        compiler_params=pltpu.CompilerParams(vmem_limit_bytes=24 * 1024 * 1024),
        cost_estimate=cost(
            4 * depth * (high - low) * units * LANES,
            4 * depth * (high - low + columns) + 2 * (high - low) * units * LANES,
        ),
        name="flat_grad",
    )(*operands)


def flat_half(side, total_rows, work):
    flat = None
    place = 0
    for a, b, low, high in work:
        if a is None:
            place += b
            continue
        flat = flat_grad(flat, total_rows, side, a, b, low, high, place)
        place += (high - low) * b[0].shape[1] // UNIT
    return flat


def dp_swap(block, bit):
    count = lax.axis_size("dp")
    return lax.ppermute(block, "dp", [(i, i ^ bit) for i in range(count)])


def stream_swap(block):
    return lax.ppermute(block, "stream", [(0, 1), (1, 0)])


def pick(block, index, axis=0):
    return lax.dynamic_index_in_dim(block, index, axis, keepdims=False)


def plus(a, b):
    return (a.astype(F32) + b.astype(F32)).astype(BF16)


def halved(block, bits, order):
    me = lax.axis_index("dp")
    left = list(bits)
    for step, bit in enumerate(order):
        axis = left.index(bit)
        left.remove(bit)
        mine = (me >> bit) & 1
        keep = pick(block, mine, axis)
        far = dp_swap(pick(block, 1 - mine, axis), 1 << bit)
        if step + 1 < len(order):
            block = plus(keep, far)
        else:
            block = keep.astype(F32) + far.astype(F32)
    return block


def reduce_scatter(flat, cuts):
    count = lax.axis_size("dp")
    top = count.bit_length() - 2
    bits = tuple(range(top, 0, -1))
    chips = count // 2
    rows = flat.shape[0] // chips
    blocks = flat.reshape((2,) * len(bits) + (rows, LANES))
    natural = tuple(range(1, top + 1))
    turned = natural[1:2] + natural[:1] + natural[2:]
    done, start = [], 0
    for share, turn in cuts:
        part = lax.slice_in_dim(blocks, start, start + rows * share // 8, axis=len(bits))
        start += rows * share // 8
        done.append(halved(part, bits, turned if turn else natural))
    return jnp.concatenate(done) if len(done) > 1 else done[0]


def share_of(result):
    core = lax.axis_index("dp") & 1
    halves = result.reshape(2, result.shape[0] // 2, LANES)
    mine = pick(halves, core)
    far = dp_swap(pick(halves, 1 - core), 1)
    return interleaved(mine, far, core).reshape(-1)


def interleaved(mine, far, odd):
    first = jnp.where(odd == 0, mine, far)
    second = jnp.where(odd == 0, far, mine)
    return jnp.stack([first, second], axis=1).reshape(-1, LANES)


def normed(tensor):
    centred = tensor - jnp.mean(tensor, axis=-1, keepdims=True)
    inverse = lax.rsqrt(jnp.mean(centred * centred, axis=-1, keepdims=True) + 1e-05)
    return centred * inverse, inverse


def normed_back(grad, n, inverse, gain_row):
    scaled = grad * gain_row
    low = jnp.mean(scaled, axis=-1, keepdims=True)
    tilt = jnp.mean(scaled * n, axis=-1, keepdims=True)
    return (scaled - low - n * tilt) * inverse, jnp.sum(grad * n, axis=0)


def gelu_and_slope(u):
    share = 0.5 * (1.0 + lax.erf(u * 0.7071067811865476))
    slope = share + u * (0.3989422804014327 * jnp.exp(-0.5 * u * u))
    return (u * share).astype(BF16), slope


def stream_layer(states, context, cot, lens, weights, gains, heads, fixed, pairs):
    attend_w, up_w, down_w, qkv_w, output_w = weights
    width = states.shape[1]
    size = width // heads
    heads_in = LANES // size
    blocks = width // LANES
    scaling = size ** (-0.5)
    n1, inv1 = normed(states.astype(F32) + mm(context, attend_w))
    h1 = n1 * gains[0]
    h1_low = h1.astype(BF16)
    hidden_low, slope = gelu_and_slope(mm(h1_low, up_w))
    n2, inv2 = normed(h1 + mm(hidden_low, down_w))
    h2 = n2 * gains[1]
    h2_low = h2.astype(BF16)
    packed = mm(h2_low, qkv_w).astype(BF16)
    cols = (0, blocks, 2 * blocks)
    z = attend(lens, packed, packed, packed, cols, pairs, blocks, heads_in, fixed, scaling)
    n3, inv3 = normed(h2 + mm(z, output_w))
    result = n3 * gains[2]
    de, dg2 = normed_back(cot, n3, inv3, gains[2])
    de_low = de.astype(BF16)
    dz = mm_nt(de_low, output_w).astype(BF16)
    dr = attend_back(
        lens, packed, packed, packed, dz, cols, pairs, blocks, heads_in, fixed, scaling, True
    )
    dh2 = de + mm_nt(dr, qkv_w)
    db, dg1 = normed_back(dh2, n2, inv2, gains[1])
    db_low = db.astype(BF16)
    du = (mm_nt(db_low, down_w) * slope).astype(BF16)
    dh1 = db + mm_nt(du, up_w)
    da, dg0 = normed_back(dh1, n1, inv1, gains[0])
    da_low = da.astype(BF16)
    dc = mm_nt(da_low, attend_w).astype(BF16)
    sides = {
        "attend": (context, da_low),
        "up": (h1_low, du),
        "down": (hidden_low, db_low),
        "qkv": (h2_low, dr),
        "output": (z, de_low),
    }
    return result, da, dc, sides, jnp.stack((dg0, dg1, dg2))


def with_far(sides):
    return {name: ((a, dp_swap(a, 1)), (b, dp_swap(b, 1))) for name, (a, b) in sides.items()}


NAMES = ("query", "keyval", "attend", "up", "down", "qkv", "output")


def half_work(both, sizes, total):
    first, second, filled = [], [], 0
    for name in NAMES:
        m, n = sizes[name]
        a, b = both.get(name, (None, m * n // UNIT))
        room = min(max((total // 2 - filled) // n, 0), m)
        if room:
            first.append((a, b, 0, room))
        if room < m:
            second.append((a, b, room, m))
        filled += m * n
    return first, second


def spread(count, regions, padded, offset, rows):
    target = lax.broadcasted_iota(jnp.int32, (rows, count * regions), 0) - offset
    source = lax.broadcasted_iota(jnp.int32, (rows, count * regions), 1)
    return (target == source // regions * padded + source % regions).astype(BF16)


def local(
    text_states,
    image_states,
    caption_lengths,
    text_query,
    text_keyval,
    text_attend,
    text_up,
    text_down,
    text_qkv,
    text_output,
    text_gains,
    image_query,
    image_keyval,
    image_attend,
    image_up,
    image_down,
    image_qkv,
    image_output,
    image_gains,
    text_cotangent,
    image_cotangent,
):
    own_pairs = caption_lengths.shape[0]
    own_text = text_states.shape[0]
    text_len = own_text // own_pairs
    regions = image_states.shape[0] // own_pairs
    padded = -(-regions // 16) * 16
    own_image = own_pairs * padded
    pairs = 2 * own_pairs
    d_t, d_i = text_states.shape[1], image_states.shape[1]
    stream = lax.axis_index("stream")
    core = lax.axis_index("dp") & 1
    side = jnp.stack([core, stream]).astype(jnp.int32)

    far_put = spread(own_pairs, regions, padded, 0, 2 * own_image)
    near_put = spread(own_pairs, regions, padded, own_image, 2 * own_image)
    trim = near_put[own_image:].T

    def both_images(near):
        return (mm(far_put, stream_swap(near)) + mm(near_put, near)).astype(BF16)

    image_all = both_images(image_states)
    text_all = jnp.concatenate([text_states, stream_swap(text_states)])
    lens = jnp.concatenate([caption_lengths, stream_swap(caption_lengths)])
    image_cot = both_images(image_cotangent)
    text_cot = jnp.concatenate([text_cotangent, stream_swap(text_cotangent)])

    positions = lax.broadcasted_iota(jnp.int32, (pairs, text_len), 1)
    valid = (positions < lens[:, None]).reshape(pairs * text_len, 1).astype(F32)

    co_blocks = D_C // LANES
    co_cols = (0, 0, co_blocks)
    co_scale = (D_C // H_C) ** (-0.5)

    text_kv = mm(text_all, text_keyval).astype(BF16)
    image_q = mm(image_all, image_query).astype(BF16)
    ci = attend(lens, image_q, text_kv, text_kv, co_cols, pairs, co_blocks, 1, None, co_scale)
    image_out, image_da, image_dc, image_sides, image_dg = stream_layer(
        image_all,
        ci,
        image_cot.astype(F32),
        lens,
        (image_attend, image_up, image_down, image_qkv, image_output),
        image_gains,
        H_I,
        regions,
        pairs,
    )
    image_dq, text_dkv = attend_back(
        lens, image_q, text_kv, text_kv, image_dc, co_cols, pairs, co_blocks, 1, None, co_scale, False
    )
    image_sides["query"] = (image_all, image_dq)

    def sizes_of(*weights):
        return {name: weight.shape for name, weight in zip(NAMES, weights)}

    def gather_half(sides, sizes):
        both = with_far(sides)
        total = sum(m * n for m, n in sizes.values())
        total_rows = total // (2 * UNIT)
        first, second = half_work(both, sizes, total)
        return lax.cond(
            stream == 0,
            lambda: flat_half(side, total_rows, first),
            lambda: flat_half(side, total_rows, second),
        )

    image_sizes = sizes_of(
        image_query, image_keyval, image_attend, image_up, image_down, image_qkv, image_output
    )
    text_sizes = sizes_of(
        text_query, text_keyval, text_attend, text_up, text_down, text_qkv, text_output
    )
    early = lax.axis_size("dp") == 16
    if early:
        image_flat = gather_half(image_sides, image_sizes)

    image_kv = mm(image_all, image_keyval).astype(BF16)
    text_q = mm(text_all, text_query).astype(BF16)
    ct = attend(lens, text_q, image_kv, image_kv, co_cols, pairs, co_blocks, 1, regions, co_scale)
    if early:
        ct, image_flat = lax.optimization_barrier((ct, image_flat))
        image_part = reduce_scatter(image_flat, ((4, False), (4, True)))
    text_out, text_da, text_dc, text_sides, text_dg = stream_layer(
        text_all,
        ct,
        text_cot.astype(F32) * valid,
        lens,
        (text_attend, text_up, text_down, text_qkv, text_output),
        text_gains,
        H_T,
        None,
        pairs,
    )
    text_dq, image_dkv = attend_back(
        lens, text_q, image_kv, image_kv, text_dc, co_cols, pairs, co_blocks, 1, regions, co_scale, False
    )

    text_result = (text_out[:own_text] * valid[:own_text]).astype(BF16)
    image_result = mm(trim, image_out[own_image:].astype(BF16)).astype(BF16)
    text_grad = (
        text_da[:own_text]
        + mm_nt(text_dq[:own_text], text_query)
        + mm_nt(text_dkv[:own_text], text_keyval)
    ).astype(BF16)
    image_grad = (
        image_da[own_image:]
        + mm_nt(image_dq[own_image:], image_query)
        + mm_nt(image_dkv[own_image:], image_keyval)
    ).astype(BF16)
    image_grad = mm(trim, image_grad).astype(BF16)

    text_sides["query"] = (text_all, text_dq)
    text_sides["keyval"] = (text_all, text_dkv)
    if early:
        late = late_keyval(side, image_all, image_dkv)
        image_part = merged_keyval(image_part, late)
        cuts = ((2, False), (2, True), (2, False), (2, False))
    else:
        image_sides["keyval"] = (image_all, image_dkv)
        image_part = reduce_scatter(gather_half(image_sides, image_sizes), ((8, False),))
        cuts = ((8, False),)
    text_part = reduce_scatter(gather_half(text_sides, text_sizes), cuts)
    image_share = share_of(image_part)
    text_share = share_of(text_part)
    text_gain_sum, image_gain_sum = lax.psum((text_dg, image_dg), "dp")
    return (
        text_result,
        image_result,
        text_grad,
        image_grad,
        text_share,
        image_share,
        text_gain_sum,
        image_gain_sum,
    )


def late_keyval(side, states, grads):
    me = lax.axis_index("dp")
    far = (dp_swap(states, 1), dp_swap(grads, 1))
    flat = flat_grad(
        None, 4 * 1280, side, (states, far[0]), (grads, far[1]), 0, states.shape[1], 768, True
    )
    blocks = flat.reshape(2, 2, 1280, LANES)
    y = (me >> 1) & 1
    odd = (me >> 2) & 1
    total = plus(pick(blocks, 1 - y, 1), dp_swap(pick(blocks, y, 1), 2))
    own = jnp.where(y == 1, odd, 1 - odd)
    total = plus(pick(total, own), dp_swap(pick(total, 1 - own), 4))
    route = []
    for i in range(16):
        z, y_of = i >> 2, (i >> 1) & 1
        goal = 1 if z & 1 else (0 if y_of else 2)
        if z != goal:
            route.append((i, goal * 4 + (i & 3)))
    total = plus(total, lax.ppermute(total, "dp", route))
    far = lax.ppermute(total, "stream", [(1, 0)])
    return jnp.stack([total, far], axis=1).reshape(2 * 1280, LANES)


def merged_keyval(part, late):
    chip = lax.axis_index("dp") >> 1
    low = jnp.where(chip == 1, 1536, 0)
    high = jnp.where((chip >= 1) & (chip <= 4), jnp.where(chip == 4, 2048, 2560), 0)
    high = jnp.where(lax.axis_index("stream") == 0, high, 0)
    rows = lax.broadcasted_iota(jnp.int32, (part.shape[0], 1), 0)
    return jnp.where((rows >= low) & (rows < high), late.astype(F32), part)


def solution(mesh):
    split = P(("stream", "dp"), None)
    flat = P(("stream", "dp"))
    whole = P()
    return jax.shard_map(
        local,
        mesh=mesh,
        in_specs=(split, split, flat) + (whole,) * 16 + (split, split),
        out_specs=(split, split, split, split, flat, flat, whole, whole),
        check_vma=False,
    )
```

time: 640 us -> 464 us (0.72)
  the two profiles are of different devices: /device:TPU:9 before, /device:TPU:1 now
where the time goes in v2:
time: 464 us; the launch traced here: 460 us
  waiting for transfers between devices  147 us (32%)
  Pallas kernels  70 us (15%)
  blocking collectives  68.9 us (15%)
  matrix products  67.2 us (14%)
  starting transfers between devices  50.5 us (11%)
  local copies, waits for them, and re-layouts  28.1 us (6%)
  other arithmetic  25.8 us (6%)
    ppermute x48, waiting for transfers between devices, dp_swap(): return lax.ppermute(block, 'dp', [(i, i ^ bit) for i in range(count)])  138 us
    psum x1, blocking collectives, local(): text_gain_sum, image_gain_sum = lax.psum((text_dg, image_dg), 'dp')  68.9 us
    ppermute x48, starting transfers between devices, dp_swap(): return lax.ppermute(block, 'dp', [(i, i ^ bit) for i in range(count)])  42.4 us
    dot_general x20, matrix products, mm(): return jnp.dot(a, b, preferred_element_type=F32)  38.3 us
    pallas_call x8, Pallas kernels, flat_grad(): pl.pallas_call(functools.partial(flat_kernel, place=place, bm=bm, low=(lo...  29 us
    dot_general x13, matrix products, mm_nt(): lax.dot_general(a, b, (((1,), (1,)), ((), ())), preferred_element_type=F32)  28.9 us
    pallas_call x4, Pallas kernels, attend_back(): pl.pallas_call(functools.partial(body, pairs=pairs, blocks=blocks, cols=c...  22.1 us
    pallas_call x4, Pallas kernels, attend(): pl.pallas_call(functools.partial(body, pairs=pairs, blocks=blocks, cols=c...  19 us
  transfers between devices with their start and end apart: 55, of which 19 were waited for; matrix products, arithmetic and copies ran while one was open for 24% of the time, Pallas kernels for 11%

profile of v2, /device:TPU:1, one launch (start us, length us, event | category | flops | bytes accessed | tf_op | source)
XLA Modules:
  0.0 460.0 jit_solution(10889546423750957299)
XLA Ops:
  21.4 3.0 convolution_convert_fusion.2.refs_1_
  24.3 4.6 %attend.5 = bf16[192,1024]{1,0:T(8,128)(2,1)S(1)} custom-call(s32[4]{0:T(128)S(1)} %pad_add_fusion.lens_ref, bf16[192,1024]{1,0:T(8,128)(2,1)S(1)} %convolution_convert_fusion.9.refs_0_, bf16[512,2048]{1,0:T(8,128)(2,1)S(1)} %convolution_convert_fusion.2.refs_1_), custom_call_target="tpu_custom_call" | custom-call | flops 402653184 | bytes 2883584 | tf_op jit(solution)/shard_map/attend/pallas_call | solution.py:107
  36.5 4.2 attend.6
  44.4 4.3 attend_back.4
  48.8 2.6 multiply_reduce_fusion.12
  55.9 6.7 %attend_back.5 = (bf16[192,1024]{1,0:T(8,128)(2,1)S(1)}, bf16[512,2048]{1,0:T(8,128)(2,1)}) custom-call(s32[4]{0:T(128)S(1)} %pad_add_fusion.lens_ref, bf16[192,1024]{1,0:T(8,128)(2,1)S(1)} %convolution_convert_fusion.9.refs_0_, bf16[512,2048]{1,0:T(8,128)(2,1)S(1)} %convolution_convert_fusion.2.refs_1_, bf16[192,1024]{1,0:T(8,128)(2,1)S(1)} %convolution_convert_fusion.7.refs_2_), custom_call_target="tpu_custom_call" | custom-call | flops 1006632960 | bytes 5767168 | tf_op jit(solution)/shard_map/attend_back/pallas_call | solution.py:219
  70.0 5.5 %attend.4 = bf16[512,1024]{1,0:T(8,128)(2,1)} custom-call(s32[4]{0:T(128)S(1)} %pad_add_fusion.lens_ref, bf16[512,1024]{1,0:T(8,128)(2,1)S(1)} %convolution_convert_fusion.5.refs_0_, bf16[192,2048]{1,0:T(8,128)(2,1)S(1)} %convolution_convert_fusion.3.refs_1_), custom_call_target="tpu_custom_call" | custom-call | flops 402653184 | bytes 2883584 | tf_op jit(solution)/shard_map/attend/pallas_call | solution.py:107
  78.3 7.4 %conditional.2 = (bf16[20480,128]{1,0:T(8,128)(2,1)}) conditional(s32[]{:T(128)} %convert_element_type.370, (s32[2]{0:T(128)S(1)}, bf16[192,1024]{1,0:T(8,128)(2,1)S(1)}, bf16[192,1024]{1,0:T(8,128)(2,1)S(1)}, bf16[192,1024]{1,0:T(8,128)(2,1)S(1)}, bf16[192,1024]{1,0:T(8,128)(2,1)S(1)}, /*index=5*/bf16[192,1024]{1,0:T(8,128)(2,1)S(1)}, ...), branch_computations={%region_12.13_spmd, %region_13.14_spmd} | conditional | flops 2013265920 | bytes 11534344 | solution.py:572
  78.3 2.8 flat_grad.26.rest_0_
  85.7 3.0 fusion.61
  91.0 5.9 %multiply_convert_fusion = (bf16[512,3072]{1,0:T(8,128)(2,1)S(1)}, f32[512,3072]{1,0:T(8,128)S(1)}) fusion(bf16[512,768]{1,0:T(8,128)(2,1)} %multiply_convert_fusion.2, bf16[768,3072]{1,0:T(8,128)(2,1)} %param.31), kind=kOutput, calls=%fused_computation.7 | convolution fusion | flops 2423783424 | bytes 14942208 | tf_op jit(solution)/shard_map/dot_general | solution.py:22
  96.9 2.8 fusion.70
  102.7 4.6 attend.7
  113.4 5.0 %attend_back.6 = bf16[512,2304]{1,0:T(8,128)(2,1)S(1)} custom-call(s32[4]{0:T(128)S(1)} %pad_add_fusion.lens_ref, bf16[512,2304]{1,0:T(8,128)(2,1)S(1)} %convolution_convert_fusion.refs_0_, bf16[512,768]{1,0:T(8,128)(2,1)S(1)} %convolution_convert_fusion.6.refs_1_), custom_call_target="tpu_custom_call" | custom-call | flops 4026531840 | bytes 6291456 | tf_op jit(solution)/shard_map/attend_back/pallas_call | solution.py:219
  118.4 4.4 multiply_reduce_fusion.1
  123.4 4.5 fusion.5
  128.0 3.1 multiply_reduce_fusion.2
  135.2 6.0 %attend_back.7 = (bf16[512,1024]{1,0:T(8,128)(2,1)}, bf16[192,2048]{1,0:T(8,128)(2,1)S(1)}) custom-call(s32[4]{0:T(128)S(1)} %pad_add_fusion.lens_ref, bf16[512,1024]{1,0:T(8,128)(2,1)S(1)} %copy-done.5, bf16[192,2048]{1,0:T(8,128)(2,1)S(1)} %copy-done.3, bf16[512,1024]{1,0:T(8,128)(2,1)S(1)} %convolution_convert_fusion.4.refs_2_), custom_call_target="tpu_custom_call" | custom-call | flops 1006632960 | bytes 5767168 | tf_op jit(solution)/shard_map/attend_back/pallas_call | solution.py:219
  142.8 3.0 fusion.65
  152.6 2.7 fusion.36
  156.2 68.9 %all-reduce = (f32[3,768]{1,0:T(4,128)}, f32[3,1024]{1,0:T(4,128)}) all-reduce(f32[3,768]{1,0:T(4,128)S(1)} %pad_maximum_fusion.6, f32[3,1024]{1,0:T(4,128)S(1)} %copy-done.51), channel_id=1, replica_groups=mesh['stream'=2,'dp'=16] {'dp'}, use_global_device_ids=true, to_apply=%region_31.32 | all-reduce | flops 5376 | bytes 43008 | tf_op jit(solution)/shard_map/psum | solution.py:636
  225.1 3.2 convolution_convert_fusion.10
  228.3 4.5 fusion.17
  237.7 8.3 %collective-permute-done.44 = bf16[2,1280,128]{2,1,0:T(8,128)(2,1)S(1)} collective-permute-done((bf16[2,1280,128]{2,1,0:T(8,128)(2,1)S(1)}, bf16[2,1280,128]{2,1,0:T(8,128)(2,1)S(1)}, u32[]{:S(2)}, u32[]{:S(2)}) %collective-permute-start.44) | collective-permute-done | bytes 655392 | tf_op jit(solution)/shard_map/ppermute | solution.py:339
  247.4 10.7 %collective-permute-done.51 = bf16[2,2,1280,128]{3,2,0,1:T(8,128)(2,1)S(1)} collective-permute-done((bf16[2,2,1280,128]{3,2,0,1:T(8,128)(2,1)S(1)}, bf16[2,2,1280,128]{3,2,0,1:T(8,128)(2,1)S(1)}, u32[]{:S(2)}, u32[]{:S(2)}) %collective-permute-start.51) | collective-permute-done | bytes 1310752 | tf_op jit(solution)/shard_map/ppermute | solution.py:339
  259.6 11.2 %collective-permute-start.21 = (bf16[512,768]{1,0:T(8,128)(2,1)S(1)}, bf16[512,768]{1,0:T(8,128)(2,1)S(1)}, u32[]{:S(2)}, u32[]{:S(2)}) collective-permute-start(bf16[512,768]{1,0:T(8,128)(2,1)S(1)} %copy-done.19), channel_id=1, source_target_pairs={{0,1},{1,0},{2,3},{3,2},{4,5},{5,4},{6,7},{7,6},{8,9},{9,8},{10,11... | collective-permute-start | bytes 2359304 | tf_op jit(solution)/shard_map/ppermute | solution.py:339
  270.8 8.4 %collective-permute-done.45 = bf16[1280,128]{1,0:T(8,128)(2,1)S(1)} collective-permute-done((bf16[1280,128]{1,0:T(8,128)(2,1)S(1)}, bf16[1280,128]{1,0:T(8,128)(2,1)S(1)}, u32[]{:S(2)}, u32[]{:S(2)}) %collective-permute-start.45) | collective-permute-done | bytes 327712 | tf_op jit(solution)/shard_map/ppermute | solution.py:339
  279.2 5.9 %collective-permute-start.29 = (bf16[512,768]{1,0:T(8,128)(2,1)S(1)}, bf16[512,768]{1,0:T(8,128)(2,1)S(1)}, u32[]{:S(2)}, u32[]{:S(2)}) collective-permute-start(bf16[512,768]{1,0:T(8,128)(2,1)S(1)} %copy-done.26), channel_id=1, source_target_pairs={{0,1},{1,0},{2,3},{3,2},{4,5},{5,4},{6,7},{7,6},{8,9},{9,8},{10,11... | collective-permute-start | bytes 2359304 | tf_op jit(solution)/shard_map/ppermute | solution.py:339
  289.6 11.7 %collective-permute-done.52 = bf16[2,1280,128]{2,1,0:T(8,128)(2,1)S(1)} collective-permute-done((bf16[2,1280,128]{2,1,0:T(8,128)(2,1)S(1)}, bf16[2,1280,128]{2,1,0:T(8,128)(2,1)S(1)}, u32[]{:S(2)}, u32[]{:S(2)}) %collective-permute-start.52) | collective-permute-done | bytes 655392 | tf_op jit(solution)/shard_map/ppermute | solution.py:339
  303.2 15.4 %collective-permute-done.50 = bf16[1280,128]{1,0:T(8,128)(2,1)S(1)} collective-permute-done((bf16[1280,128]{1,0:T(8,128)(2,1)S(1)}, bf16[1280,128]{1,0:T(8,128)(2,1)S(1)}, u32[]{:S(2)}, u32[]{:S(2)}) %collective-permute-start.50) | collective-permute-done | bytes 327712 | tf_op jit(solution)/shard_map/ppermute | solution.py:339
  318.7 16.8 %collective-permute-done.53 = bf16[1280,128]{1,0:T(8,128)(2,1)S(1)} collective-permute-done((bf16[1280,128]{1,0:T(8,128)(2,1)S(1)}, bf16[1280,128]{1,0:T(8,128)(2,1)S(1)}, u32[]{:S(2)}, u32[]{:S(2)}) %collective-permute-start.53) | collective-permute-done | bytes 327712 | tf_op jit(solution)/shard_map/ppermute | solution.py:339
  339.0 8.5 %collective-permute-done.47 = bf16[1280,128]{1,0:T(8,128)(2,1)S(1)} collective-permute-done((bf16[1280,128]{1,0:T(8,128)(2,1)S(1)}, bf16[1280,128]{1,0:T(8,128)(2,1)S(1)}, u32[]{:S(2)}, u32[]{:S(2)}) %collective-permute-start.47) | collective-permute-done | bytes 327712 | tf_op jit(solution)/shard_map/ppermute | solution.py:668
  348.5 4.8 %copy.57 = f32[1280,2,128]{2,1,0:T(2,128)S(1)} copy(f32[1280,2,128]{2,0,1:T(8,128)S(1)} %maximum_convert_fusion) | data formatting | bytes 2621440 | tf_op jit(solution)/shard_map/convert_element_type | solution.py:678
  354.7 20.1 %conditional.3 = (bf16[2,2,2,2496,128]{4,3,2,1,0:T(8,128)(2,1)}) conditional(s32[]{:T(128)} %convert_element_type.370, (s32[2]{0:T(128)S(1)}, bf16[512,768]{1,0:T(8,128)(2,1)}, bf16[512,768]{1,0:T(8,128)(2,1)}, bf16[512,3072]{1,0:T(8,128)(2,1)S(1)}, bf16[512,3072]{1,0:T(8,128)(2,1)S(1)}, /*index=5*/bf16[512,3072]{1,0:T(8,128)(2,1)S(1)}, ...), branch_computations={%region_26.27_spmd, %region_27.28_spmd} | conditional | flops 5234491392 | bytes 32112704 | solution.py:572
  354.9 4.0 flat_grad.33.rest_0_
  359.0 6.1 %flat_grad.34.rest_0_ = bf16[19968,128]{1,0:T(8,128)(2,1)} custom-call(s32[2]{0:T(128)S(1)} %get-tuple-element.199.side_ref, bf16[512,768]{1,0:T(8,128)(2,1)} %get-tuple-element.208.a0_ref, bf16[512,768]{1,0:T(8,128)(2,1)} %get-tuple-element.209.a1_ref, bf16[512,2048]{1,0:T(8,128)(2,1)} %get-tuple-element.210.b0_ref, ...), custom_call_target="tpu_custom_call", output_to_operand_aliasing={{}: (5, {})} | custom-call | flops 1610612736 | bytes 7340032 | tf_op jit(solution)/shard_map/cond/branch_1_fun/flat_grad/pallas_call | solution.py:302
  365.1 3.8 flat_grad.35.rest_0_
  368.9 5.9 %flat_grad.36 = bf16[19968,128]{1,0:T(8,128)(2,1)} custom-call(s32[2]{0:T(128)S(1)} %get-tuple-element.199.side_ref, bf16[512,768]{1,0:T(8,128)(2,1)} %get-tuple-element.200.a0_ref, bf16[512,768]{1,0:T(8,128)(2,1)} %get-tuple-element.201.a1_ref, bf16[512,3072]{1,0:T(8,128)(2,1)S(1)} %get-tuple-element.202.b0_ref, ...), custom_call_target="tpu_custom_call", output_to_operand_aliasing={{}: (5, {})} | custom-call | flops 2013265920 | bytes 9568256 | tf_op jit(solution)/shard_map/cond/branch_1_fun/flat_grad/pallas_call | solution.py:302
  374.8 2.9 fusion.66
  381.9 11.6 %collective-permute-done.36 = bf16[2,2,624,128]{3,2,0,1:T(8,128)(2,1)S(1)} collective-permute-done((bf16[2,2,624,128]{3,2,0,1:T(8,128)(2,1)S(1)}, bf16[2,2,624,128]{3,2,0,1:T(8,128)(2,1)S(1)}, u32[]{:S(2)}, u32[]{:S(2)}) %collective-permute-start.36) | collective-permute-done | bytes 639008 | tf_op jit(solution)/shard_map/ppermute | solution.py:339
  397.1 10.1 %collective-permute-done.39 = bf16[2,2,624,128]{3,2,1,0:T(8,128)(2,1)S(1)} collective-permute-done((bf16[2,2,624,128]{3,2,1,0:T(8,128)(2,1)S(1)}, bf16[2,2,624,128]{3,2,1,0:T(8,128)(2,1)S(1)}, u32[]{:S(2)}, u32[]{:S(2)}) %collective-permute-start.39) | collective-permute-done | bytes 639008 | tf_op jit(solution)/shard_map/ppermute | solution.py:339
  407.5 13.4 %collective-permute-done.30 = bf16[2,2,624,128]{3,2,0,1:T(8,128)(2,1)S(1)} collective-permute-done((bf16[2,2,624,128]{3,2,0,1:T(8,128)(2,1)S(1)}, bf16[2,2,624,128]{3,2,0,1:T(8,128)(2,1)S(1)}, u32[]{:S(2)}, u32[]{:S(2)}) %collective-permute-start.30) | collective-permute-done | bytes 639008 | tf_op jit(solution)/shard_map/ppermute | solution.py:339
  421.3 2.8 collective-permute-start.38
  424.1 3.6 collective-permute-done.34
  430.5 2.9 collective-permute-done.31
  434.1 12.9 %collective-permute-done.35 = bf16[624,128]{1,0:T(8,128)(2,1)S(1)} collective-permute-done((bf16[624,128]{1,0:T(8,128)(2,1)S(1)}, bf16[624,128]{1,0:T(8,128)(2,1)S(1)}, u32[]{:S(2)}, u32[]{:S(2)}) %collective-permute-start.35) | collective-permute-done | bytes 159776 | tf_op jit(solution)/shard_map/ppermute | solution.py:339
  447.1 3.4 collective-permute-done.41
  450.5 3.4 collective-permute-done.32
  (392 shorter events, 113.2 us)
Async XLA Ops:
  0.7 12.2 %collective-permute-start.1 = (s32[2]{0:T(128)}, s32[2]{0:T(128)}, u32[]{:S(2)}, u32[]{:S(2)}) collective-permute-start(s32[2]{0:T(128)} %param.27), channel_id=1, source_target_pairs={{0,16},{16,0},{1,17},{17,1},{2,18},{18,2},{3,19},{19,3},{4,20},{20... | collective-permute-start | bytes 32 | tf_op jit(solution)/shard_map/ppermute | solution.py:343
  2.8 11.5 %collective-permute-start.2 = (bf16[72,1024]{1,0:T(8,128)(2,1)}, bf16[72,1024]{1,0:T(8,128)(2,1)}, u32[]{:S(2)}, u32[]{:S(2)}) collective-permute-start(bf16[72,1024]{1,0:T(8,128)(2,1)} %param.26), channel_id=1, source_target_pairs={{0,16},{16,0},{1,17},{17,1},{2,18},{18,2},{3,19},{19,3},{4,20},{20... | collective-permute-start | bytes 442376 | tf_op jit(solution)/shard_map/ppermute | solution.py:343
  2.8 39.0 %collective-permute-start.4 = (bf16[72,1024]{1,0:T(8,128)(2,1)}, bf16[72,1024]{1,0:T(8,128)(2,1)}, u32[]{:S(2)}, u32[]{:S(2)}) collective-permute-start(bf16[72,1024]{1,0:T(8,128)(2,1)} %param.45), channel_id=1, source_target_pairs={{0,16},{16,0},{1,17},{17,1},{2,18},{18,2},{3,19},{19,3},{4,20},{20... | collective-permute-start | bytes 442376 | tf_op jit(solution)/shard_map/ppermute | solution.py:343
  4.2 15.3 %collective-permute-start = (bf16[256,768]{1,0:T(8,128)(2,1)}, bf16[256,768]{1,0:T(8,128)(2,1)}, u32[]{:S(2)}, u32[]{:S(2)}) collective-permute-start(bf16[256,768]{1,0:T(8,128)(2,1)} %param.25), channel_id=1, source_target_pairs={{0,16},{16,0},{1,17},{17,1},{2,18},{18,2},{3,19},{19,3},{4,20},{20... | collective-permute-start | bytes 1179656 | tf_op jit(solution)/shard_map/ppermute | solution.py:343
  15.8 46.8 %collective-permute-start.10 = (bf16[192,1024]{1,0:T(8,128)(2,1)S(1)}, bf16[192,1024]{1,0:T(8,128)(2,1)S(1)}, u32[]{:S(2)}, u32[]{:S(2)}) collective-permute-start(bf16[192,1024]{1,0:T(8,128)(2,1)S(1)} %fusion.18.a0_ref), channel_id=1, source_target_pairs={{0,1},{1,0},{2,3},{3,2},{4,5},{5,4},{6,7},{7,6},{8,9},{9,8},{10,11... | collective-permute-start | bytes 1179656 | tf_op jit(solution)/shard_map/ppermute | solution.py:339
  29.0 34.2 %collective-permute-start.12 = (bf16[192,1024]{1,0:T(8,128)(2,1)S(1)}, bf16[192,1024]{1,0:T(8,128)(2,1)S(1)}, u32[]{:S(2)}, u32[]{:S(2)}) collective-permute-start(bf16[192,1024]{1,0:T(8,128)(2,1)S(1)} %attend.5), channel_id=1, source_target_pairs={{0,1},{1,0},{2,3},{3,2},{4,5},{5,4},{6,7},{7,6},{8,9},{9,8},{10,11... | collective-permute-start | bytes 1179656 | tf_op jit(solution)/shard_map/ppermute | solution.py:339
  31.5 31.7 %collective-permute-start.14 = (bf16[192,1024]{1,0:T(8,128)(2,1)S(1)}, bf16[192,1024]{1,0:T(8,128)(2,1)S(1)}, u32[]{:S(2)}, u32[]{:S(2)}) collective-permute-start(bf16[192,1024]{1,0:T(8,128)(2,1)S(1)} %multiply_convert_fusion.5), channel_id=1, source_target_pairs={{0,1},{1,0},{2,3},{3,2},{4,5},{5,4},{6,7},{7,6},{8,9},{9,8},{10,11... | collective-permute-start | bytes 1179656 | tf_op jit(solution)/shard_map/ppermute | solution.py:339
  32.6 32.5 %collective-permute-start.3 = (bf16[192,1024]{1,0:T(8,128)(2,1)S(1)}, bf16[192,1024]{1,0:T(8,128)(2,1)S(1)}, u32[]{:S(2)}, u32[]{:S(2)}) collective-permute-start(bf16[192,1024]{1,0:T(8,128)(2,1)S(1)} %get-tuple-element.296), channel_id=1, source_target_pairs={{0,1},{1,0},{2,3},{3,2},{4,5},{5,4},{6,7},{7,6},{8,9},{9,8},{10,11... | collective-permute-start | bytes 1179656 | tf_op jit(solution)/shard_map/ppermute | solution.py:339
  55.0 12.1 %collective-permute-start.13 = (bf16[192,1024]{1,0:T(8,128)(2,1)S(1)}, bf16[192,1024]{1,0:T(8,128)(2,1)S(1)}, u32[]{:S(2)}, u32[]{:S(2)}) collective-permute-start(bf16[192,1024]{1,0:T(8,128)(2,1)S(1)} %get-tuple-element.264), channel_id=1, source_target_pairs={{0,1},{1,0},{2,3},{3,2},{4,5},{5,4},{6,7},{7,6},{8,9},{9,8},{10,11... | collective-permute-start | bytes 1179656 | tf_op jit(solution)/shard_map/ppermute | solution.py:339
  63.1 15.1 %collective-permute-start.7 = (bf16[192,3072]{1,0:T(8,128)(2,1)S(1)}, bf16[192,3072]{1,0:T(8,128)(2,1)S(1)}, u32[]{:S(2)}, u32[]{:S(2)}) collective-permute-start(bf16[192,3072]{1,0:T(8,128)(2,1)S(1)} %attend_back.4), channel_id=1, source_target_pairs={{0,1},{1,0},{2,3},{3,2},{4,5},{5,4},{6,7},{7,6},{8,9},{9,8},{10,11... | collective-permute-start | bytes 3538952 | tf_op jit(solution)/shard_map/ppermute | solution.py:339
  65.2 11.9 %collective-permute-start.6 = (bf16[192,1024]{1,0:T(8,128)(2,1)S(1)}, bf16[192,1024]{1,0:T(8,128)(2,1)S(1)}, u32[]{:S(2)}, u32[]{:S(2)}) collective-permute-start(bf16[192,1024]{1,0:T(8,128)(2,1)S(1)} %multiply_convert_fusion.4), channel_id=1, source_target_pairs={{0,1},{1,0},{2,3},{3,2},{4,5},{5,4},{6,7},{7,6},{8,9},{9,8},{10,11... | collective-permute-start | bytes 1179656 | tf_op jit(solution)/shard_map/ppermute | solution.py:339
  66.7 10.9 %collective-permute-start.8 = (bf16[192,1024]{1,0:T(8,128)(2,1)S(1)}, bf16[192,1024]{1,0:T(8,128)(2,1)S(1)}, u32[]{:S(2)}, u32[]{:S(2)}) collective-permute-start(bf16[192,1024]{1,0:T(8,128)(2,1)S(1)} %attend.6), channel_id=1, source_target_pairs={{0,1},{1,0},{2,3},{3,2},{4,5},{5,4},{6,7},{7,6},{8,9},{9,8},{10,11... | collective-permute-start | bytes 1179656 | tf_op jit(solution)/shard_map/ppermute | solution.py:339
  67.1 11.1 %collective-permute-start.5 = (bf16[192,1024]{1,0:T(8,128)(2,1)S(1)}, bf16[192,1024]{1,0:T(8,128)(2,1)S(1)}, u32[]{:S(2)}, u32[]{:S(2)}) collective-permute-start(bf16[192,1024]{1,0:T(8,128)(2,1)S(1)} %get-tuple-element.266), channel_id=1, source_target_pairs={{0,1},{1,0},{2,3},{3,2},{4,5},{5,4},{6,7},{7,6},{8,9},{9,8},{10,11... | collective-permute-start | bytes 1179656 | tf_op jit(solution)/shard_map/ppermute | solution.py:339
  67.5 10.8 %collective-permute-start.9 = (bf16[192,1024]{1,0:T(8,128)(2,1)S(1)}, bf16[192,1024]{1,0:T(8,128)(2,1)S(1)}, u32[]{:S(2)}, u32[]{:S(2)}) collective-permute-start(bf16[192,1024]{1,0:T(8,128)(2,1)S(1)} %fusion.57), channel_id=1, source_target_pairs={{0,1},{1,0},{2,3},{3,2},{4,5},{5,4},{6,7},{7,6},{8,9},{9,8},{10,11... | collective-permute-start | bytes 1179656 | tf_op jit(solution)/shard_map/ppermute | solution.py:339
  77.1 31.5 %collective-permute-start.16 = (bf16[256,768]{1,0:T(8,128)(2,1)}, bf16[256,768]{1,0:T(8,128)(2,1)}, u32[]{:S(2)}, u32[]{:S(2)}) collective-permute-start(bf16[256,768]{1,0:T(8,128)(2,1)} %param.44), channel_id=1, source_target_pairs={{0,16},{16,0},{1,17},{17,1},{2,18},{18,2},{3,19},{19,3},{4,20},{20... | collective-permute-start | bytes 1179656 | tf_op jit(solution)/shard_map/ppermute | solution.py:343
  77.6 181.2 %collective-permute-start.25 = (bf16[512,768]{1,0:T(8,128)(2,1)}, bf16[512,768]{1,0:T(8,128)(2,1)}, u32[]{:S(2)}, u32[]{:S(2)}) collective-permute-start(bf16[512,768]{1,0:T(8,128)(2,1)} %constant_dynamic-update-slice_fusion), channel_id=1, source_target_pairs={{0,1},{1,0},{2,3},{3,2},{4,5},{5,4},{6,7},{7,6},{8,9},{9,8},{10,11... | collective-permute-start | bytes 2359304 | tf_op jit(solution)/shard_map/ppermute | solution.py:339
  78.2 223.9 %collective-permute-start.27 = (bf16[512,2048]{1,0:T(8,128)(2,1)}, bf16[512,2048]{1,0:T(8,128)(2,1)}, u32[]{:S(2)}, u32[]{:S(2)}) collective-permute-start(bf16[512,2048]{1,0:T(8,128)(2,1)} %get-tuple-element.231), channel_id=1, source_target_pairs={{0,1},{1,0},{2,3},{3,2},{4,5},{5,4},{6,7},{7,6},{8,9},{9,8},{10,11... | collective-permute-start | bytes 6291464 | tf_op jit(solution)/shard_map/ppermute | solution.py:339
  90.6 194.7 %collective-permute-start.17 = (bf16[512,768]{1,0:T(8,128)(2,1)}, bf16[512,768]{1,0:T(8,128)(2,1)}, u32[]{:S(2)}, u32[]{:S(2)}) collective-permute-start(bf16[512,768]{1,0:T(8,128)(2,1)} %multiply_convert_fusion.2), channel_id=1, source_target_pairs={{0,1},{1,0},{2,3},{3,2},{4,5},{5,4},{6,7},{7,6},{8,9},{9,8},{10,11... | collective-permute-start | bytes 2359304 | tf_op jit(solution)/shard_map/ppermute | solution.py:339
  142.6 90.3 %collective-permute-start.43 = (bf16[192,2048]{1,0:T(8,128)(2,1)S(1)}, bf16[192,2048]{1,0:T(8,128)(2,1)S(1)}, u32[]{:S(2)}, u32[]{:S(2)}) collective-permute-start(bf16[192,2048]{1,0:T(8,128)(2,1)S(1)} %get-tuple-element.232.b0_ref), channel_id=1, source_target_pairs={{0,1},{1,0},{2,3},{3,2},{4,5},{5,4},{6,7},{7,6},{8,9},{9,8},{10,11... | collective-permute-start | bytes 2359304 | tf_op jit(solution)/shard_map/ppermute | solution.py:339
  148.3 86.5 %collective-permute-start.48 = (bf16[2,2,1280,128]{3,2,0,1:T(8,128)(2,1)}, bf16[2,2,1280,128]{3,2,0,1:T(8,128)(2,1)}, u32[]{:S(2)}, u32[]{:S(2)}) collective-permute-start(bf16[2,2,1280,128]{3,2,0,1:T(8,128)(2,1)} %bitcast.211), channel_id=1, source_target_pairs={{0,2},{1,3},{2,0},{3,1},{4,6},{5,7},{6,4},{7,5},{8,10},{9,11},{10,... | collective-permute-start | bytes 3932168 | tf_op jit(solution)/shard_map/ppermute | solution.py:339
  232.9 25.2 %collective-permute-start.51 = (bf16[2,2,1280,128]{3,2,0,1:T(8,128)(2,1)S(1)}, bf16[2,2,1280,128]{3,2,0,1:T(8,128)(2,1)S(1)}, u32[]{:S(2)}, u32[]{:S(2)}) collective-permute-start(bf16[2,2,1280,128]{3,2,0,1:T(8,128)(2,1)S(1)} %bitcast.226), channel_id=1, source_target_pairs={{0,4},{1,5},{2,6},{3,7},{4,0},{5,1},{6,2},{7,3},{8,12},{9,13},{10,... | collective-permute-start | bytes 3932168 | tf_op jit(solution)/shard_map/ppermute | solution.py:339
  234.8 11.3 %collective-permute-start.44 = (bf16[2,1280,128]{2,1,0:T(8,128)(2,1)S(1)}, bf16[2,1280,128]{2,1,0:T(8,128)(2,1)S(1)}, u32[]{:S(2)}, u32[]{:S(2)}) collective-permute-start(bf16[2,1280,128]{2,1,0:T(8,128)(2,1)S(1)} %dynamic-slice_bitcast_fusion.3), channel_id=1, source_target_pairs={{0,2},{1,3},{2,0},{3,1},{4,6},{5,7},{6,4},{7,5},{8,10},{9,11},{10,... | collective-permute-start | bytes 1966088 | tf_op jit(solution)/shard_map/ppermute | solution.py:339
  246.0 39.3 %collective-permute-start.49 = (bf16[2,1280,128]{2,1,0:T(8,128)(2,1)S(1)}, bf16[2,1280,128]{2,1,0:T(8,128)(2,1)S(1)}, u32[]{:S(2)}, u32[]{:S(2)}) collective-permute-start(bf16[2,1280,128]{2,1,0:T(8,128)(2,1)S(1)} %dynamic-slice_bitcast_fusion.2), channel_id=1, source_target_pairs={{0,4},{1,5},{2,6},{3,7},{4,0},{5,1},{6,2},{7,3},{8,12},{9,13},{10,... | collective-permute-start | bytes 1966088 | tf_op jit(solution)/shard_map/ppermute | solution.py:339
  258.1 21.1 %collective-permute-start.45 = (bf16[1280,128]{1,0:T(8,128)(2,1)S(1)}, bf16[1280,128]{1,0:T(8,128)(2,1)S(1)}, u32[]{:S(2)}, u32[]{:S(2)}) collective-permute-start(bf16[1280,128]{1,0:T(8,128)(2,1)S(1)} %dynamic-slice_bitcast_fusion.8), channel_id=1, source_target_pairs={{0,4},{1,5},{2,6},{3,7},{4,0},{5,1},{6,2},{7,3},{8,12},{9,13},{10,... | collective-permute-start | bytes 983048 | tf_op jit(solution)/shard_map/ppermute | solution.py:339
  259.6 26.1 %collective-permute-start.21 = (bf16[512,768]{1,0:T(8,128)(2,1)S(1)}, bf16[512,768]{1,0:T(8,128)(2,1)S(1)}, u32[]{:S(2)}, u32[]{:S(2)}) collective-permute-start(bf16[512,768]{1,0:T(8,128)(2,1)S(1)} %copy-done.19), channel_id=1, source_target_pairs={{0,1},{1,0},{2,3},{3,2},{4,5},{5,4},{6,7},{7,6},{8,9},{9,8},{10,11... | collective-permute-start | bytes 2359304 | tf_op jit(solution)/shard_map/ppermute | solution.py:339
  285.3 63.1 %collective-permute-start.18 = (bf16[512,3072]{1,0:T(8,128)(2,1)S(1)}, bf16[512,3072]{1,0:T(8,128)(2,1)S(1)}, u32[]{:S(2)}, u32[]{:S(2)}) collective-permute-start(bf16[512,3072]{1,0:T(8,128)(2,1)S(1)} %copy-done.11), channel_id=1, source_target_pairs={{0,1},{1,0},{2,3},{3,2},{4,5},{5,4},{6,7},{7,6},{8,9},{9,8},{10,11... | collective-permute-start | bytes 9437192 | tf_op jit(solution)/shard_map/ppermute | solution.py:339
  285.4 15.9 %collective-permute-start.52 = (bf16[2,1280,128]{2,1,0:T(8,128)(2,1)S(1)}, bf16[2,1280,128]{2,1,0:T(8,128)(2,1)S(1)}, u32[]{:S(2)}, u32[]{:S(2)}) collective-permute-start(bf16[2,1280,128]{2,1,0:T(8,128)(2,1)S(1)} %dynamic-slice_bitcast_fusion.1), channel_id=1, source_target_pairs={{0,2},{1,3},{2,0},{3,1},{4,6},{5,7},{6,4},{7,5},{8,10},{9,11},{10,... | collective-permute-start | bytes 1966088 | tf_op jit(solution)/shard_map/ppermute | solution.py:339
  285.7 69.0 %collective-permute-start.19 = (bf16[512,3072]{1,0:T(8,128)(2,1)S(1)}, bf16[512,3072]{1,0:T(8,128)(2,1)S(1)}, u32[]{:S(2)}, u32[]{:S(2)}) collective-permute-start(bf16[512,3072]{1,0:T(8,128)(2,1)S(1)} %copy-done.22), channel_id=1, source_target_pairs={{0,1},{1,0},{2,3},{3,2},{4,5},{5,4},{6,7},{7,6},{8,9},{9,8},{10,11... | collective-permute-start | bytes 9437192 | tf_op jit(solution)/shard_map/ppermute | solution.py:339
  287.1 16.0 %collective-permute-start.46 = (bf16[1280,128]{1,0:T(8,128)(2,1)S(1)}, bf16[1280,128]{1,0:T(8,128)(2,1)S(1)}, u32[]{:S(2)}, u32[]{:S(2)}) collective-permute-start(bf16[1280,128]{1,0:T(8,128)(2,1)S(1)} %fusion.31), channel_id=1, source_target_pairs={{0,8},{1,9},{10,2},{11,3},{12,4},{13,5},{14,6},{15,7},{16,24},{17,... | collective-permute-start | bytes 983048 | tf_op jit(solution)/shard_map/ppermute | solution.py:667
  301.3 17.3 %collective-permute-start.50 = (bf16[1280,128]{1,0:T(8,128)(2,1)S(1)}, bf16[1280,128]{1,0:T(8,128)(2,1)S(1)}, u32[]{:S(2)}, u32[]{:S(2)}) collective-permute-start(bf16[1280,128]{1,0:T(8,128)(2,1)S(1)} %dynamic-slice_bitcast_fusion.7), channel_id=1, source_target_pairs={{0,8},{1,9},{2,10},{3,11},{4,12},{5,13},{6,14},{7,15},{8,0},{9,1},... | collective-permute-start | bytes 983048 | tf_op jit(solution)/shard_map/ppermute | solution.py:339
  302.1 34.1 %collective-permute-start.28 = (bf16[512,1024]{1,0:T(8,128)(2,1)}, bf16[512,1024]{1,0:T(8,128)(2,1)}, u32[]{:S(2)}, u32[]{:S(2)}) collective-permute-start(bf16[512,1024]{1,0:T(8,128)(2,1)} %attend.4), channel_id=1, source_target_pairs={{0,1},{1,0},{2,3},{3,2},{4,5},{5,4},{6,7},{7,6},{8,9},{9,8},{10,11... | collective-permute-start | bytes 3145736 | tf_op jit(solution)/shard_map/ppermute | solution.py:339
  303.1 51.6 %collective-permute-start.22 = (bf16[512,2304]{1,0:T(8,128)(2,1)S(1)}, bf16[512,2304]{1,0:T(8,128)(2,1)S(1)}, u32[]{:S(2)}, u32[]{:S(2)}) collective-permute-start(bf16[512,2304]{1,0:T(8,128)(2,1)S(1)} %copy-done.31), channel_id=1, source_target_pairs={{0,1},{1,0},{2,3},{3,2},{4,5},{5,4},{6,7},{7,6},{8,9},{9,8},{10,11... | collective-permute-start | bytes 7077896 | tf_op jit(solution)/shard_map/ppermute | solution.py:339
  318.6 16.9 %collective-permute-start.53 = (bf16[1280,128]{1,0:T(8,128)(2,1)S(1)}, bf16[1280,128]{1,0:T(8,128)(2,1)S(1)}, u32[]{:S(2)}, u32[]{:S(2)}) collective-permute-start(bf16[1280,128]{1,0:T(8,128)(2,1)S(1)} %dynamic-slice_bitcast_fusion.6), channel_id=1, source_target_pairs={{0,8},{1,9},{2,10},{3,11},{4,12},{5,13},{6,14},{7,15},{8,0},{9,1},... | collective-permute-start | bytes 983048 | tf_op jit(solution)/shard_map/ppermute | solution.py:339
  336.2 11.3 %collective-permute-start.47 = (bf16[1280,128]{1,0:T(8,128)(2,1)S(1)}, bf16[1280,128]{1,0:T(8,128)(2,1)S(1)}, u32[]{:S(2)}, u32[]{:S(2)}) collective-permute-start(bf16[1280,128]{1,0:T(8,128)(2,1)S(1)} %add_convert_fusion), channel_id=1, source_target_pairs={{16,0},{17,1},{18,2},{19,3},{20,4},{21,5},{22,6},{23,7},{24,8},{25... | collective-permute-start | bytes 983048 | tf_op jit(solution)/shard_map/ppermute | solution.py:668
  338.6 16.0 %collective-permute-start.23 = (bf16[512,768]{1,0:T(8,128)(2,1)S(1)}, bf16[512,768]{1,0:T(8,128)(2,1)S(1)}, u32[]{:S(2)}, u32[]{:S(2)}) collective-permute-start(bf16[512,768]{1,0:T(8,128)(2,1)S(1)} %copy-done.42), channel_id=1, source_target_pairs={{0,1},{1,0},{2,3},{3,2},{4,5},{5,4},{6,7},{7,6},{8,9},{9,8},{10,11... | collective-permute-start | bytes 2359304 | tf_op jit(solution)/shard_map/ppermute | solution.py:339
  377.8 15.7 %collective-permute-start.36 = (bf16[2,2,624,128]{3,2,0,1:T(8,128)(2,1)S(1)}, bf16[2,2,624,128]{3,2,0,1:T(8,128)(2,1)S(1)}, u32[]{:S(2)}, u32[]{:S(2)}) collective-permute-start(bf16[2,2,624,128]{3,2,0,1:T(8,128)(2,1)S(1)} %bitcast.231), channel_id=1, source_target_pairs={{0,2},{1,3},{2,0},{3,1},{4,6},{5,7},{6,4},{7,5},{8,10},{9,11},{10,... | collective-permute-start | bytes 1916936 | tf_op jit(solution)/shard_map/ppermute | solution.py:339
  379.2 76.2 %collective-permute-start.54 = (f32[1280,128]{1,0:T(8,128)S(1)}, f32[1280,128]{1,0:T(8,128)S(1)}, u32[]{:S(2)}, u32[]{:S(2)}) collective-permute-start(f32[1280,128]{1,0:T(8,128)S(1)} %dynamic-slice_bitcast_fusion), channel_id=1, source_target_pairs={{0,1},{1,0},{2,3},{3,2},{4,5},{5,4},{6,7},{7,6},{8,9},{9,8},{10,11... | collective-permute-start | bytes 1966088 | tf_op jit(solution)/shard_map/ppermute | solution.py:339
  380.1 16.1 %collective-permute-start.33 = (bf16[2,2,624,128]{3,2,0,1:T(8,128)(2,1)S(1)}, bf16[2,2,624,128]{3,2,0,1:T(8,128)(2,1)S(1)}, u32[]{:S(2)}, u32[]{:S(2)}) collective-permute-start(bf16[2,2,624,128]{3,2,0,1:T(8,128)(2,1)S(1)} %bitcast.232), channel_id=1, source_target_pairs={{0,4},{1,5},{2,6},{3,7},{4,0},{5,1},{6,2},{7,3},{8,12},{9,13},{10,... | collective-permute-start | bytes 1916936 | tf_op jit(solution)/shard_map/ppermute | solution.py:339
  380.4 26.8 %collective-permute-start.39 = (bf16[2,2,624,128]{3,2,1,0:T(8,128)(2,1)S(1)}, bf16[2,2,624,128]{3,2,1,0:T(8,128)(2,1)S(1)}, u32[]{:S(2)}, u32[]{:S(2)}) collective-permute-start(bf16[2,2,624,128]{3,2,1,0:T(8,128)(2,1)S(1)} %dynamic-slice_bitcast_fusion.5), channel_id=1, source_target_pairs={{0,2},{1,3},{2,0},{3,1},{4,6},{5,7},{6,4},{7,5},{8,10},{9,11},{10,... | collective-permute-start | bytes 1916936 | tf_op jit(solution)/shard_map/ppermute | solution.py:339
  381.2 39.6 %collective-permute-start.30 = (bf16[2,2,624,128]{3,2,0,1:T(8,128)(2,1)S(1)}, bf16[2,2,624,128]{3,2,0,1:T(8,128)(2,1)S(1)}, u32[]{:S(2)}, u32[]{:S(2)}) collective-permute-start(bf16[2,2,624,128]{3,2,0,1:T(8,128)(2,1)S(1)} %bitcast.230), channel_id=1, source_target_pairs={{0,2},{1,3},{2,0},{3,1},{4,6},{5,7},{6,4},{7,5},{8,10},{9,11},{10,... | collective-permute-start | bytes 1916936 | tf_op jit(solution)/shard_map/ppermute | solution.py:339
  393.7 27.5 %collective-permute-start.37 = (bf16[2,624,128]{2,1,0:T(8,128)(2,1)S(1)}, bf16[2,624,128]{2,1,0:T(8,128)(2,1)S(1)}, u32[]{:S(2)}, u32[]{:S(2)}) collective-permute-start(bf16[2,624,128]{2,1,0:T(8,128)(2,1)S(1)} %dynamic-slice_bitcast_fusion.10), channel_id=1, source_target_pairs={{0,4},{1,5},{2,6},{3,7},{4,0},{5,1},{6,2},{7,3},{8,12},{9,13},{10,... | collective-permute-start | bytes 958472 | tf_op jit(solution)/shard_map/ppermute | solution.py:339
  396.4 31.4 %collective-permute-start.34 = (bf16[2,624,128]{2,1,0:T(8,128)(2,1)S(1)}, bf16[2,624,128]{2,1,0:T(8,128)(2,1)S(1)}, u32[]{:S(2)}, u32[]{:S(2)}) collective-permute-start(bf16[2,624,128]{2,1,0:T(8,128)(2,1)S(1)} %dynamic-slice_bitcast_fusion.11), channel_id=1, source_target_pairs={{0,2},{1,3},{2,0},{3,1},{4,6},{5,7},{6,4},{7,5},{8,10},{9,11},{10,... | collective-permute-start | bytes 958472 | tf_op jit(solution)/shard_map/ppermute | solution.py:339
  407.4 20.5 %collective-permute-start.40 = (bf16[2,624,128]{2,1,0:T(8,128)(2,1)S(1)}, bf16[2,624,128]{2,1,0:T(8,128)(2,1)S(1)}, u32[]{:S(2)}, u32[]{:S(2)}) collective-permute-start(bf16[2,624,128]{2,1,0:T(8,128)(2,1)S(1)} %dynamic-slice_bitcast_fusion.9), channel_id=1, source_target_pairs={{0,4},{1,5},{2,6},{3,7},{4,0},{5,1},{6,2},{7,3},{8,12},{9,13},{10,... | collective-permute-start | bytes 958472 | tf_op jit(solution)/shard_map/ppermute | solution.py:339
  421.1 12.3 %collective-permute-start.31 = (bf16[2,624,128]{2,1,0:T(8,128)(2,1)S(1)}, bf16[2,624,128]{2,1,0:T(8,128)(2,1)S(1)}, u32[]{:S(2)}, u32[]{:S(2)}) collective-permute-start(bf16[2,624,128]{2,1,0:T(8,128)(2,1)S(1)} %dynamic-slice_bitcast_fusion.12), channel_id=1, source_target_pairs={{0,4},{1,5},{2,6},{3,7},{4,0},{5,1},{6,2},{7,3},{8,12},{9,13},{10,... | collective-permute-start | bytes 958472 | tf_op jit(solution)/shard_map/ppermute | solution.py:339
  421.3 12.7 %collective-permute-start.38 = (bf16[624,128]{1,0:T(8,128)(2,1)S(1)}, bf16[624,128]{1,0:T(8,128)(2,1)S(1)}, u32[]{:S(2)}, u32[]{:S(2)}) collective-permute-start(bf16[624,128]{1,0:T(8,128)(2,1)S(1)} %dynamic-slice_bitcast_fusion.14), channel_id=1, source_target_pairs={{0,8},{1,9},{2,10},{3,11},{4,12},{5,13},{6,14},{7,15},{8,0},{9,1},... | collective-permute-start | bytes 479240 | tf_op jit(solution)/shard_map/ppermute | solution.py:339
  427.9 19.2 %collective-permute-start.35 = (bf16[624,128]{1,0:T(8,128)(2,1)S(1)}, bf16[624,128]{1,0:T(8,128)(2,1)S(1)}, u32[]{:S(2)}, u32[]{:S(2)}) collective-permute-start(bf16[624,128]{1,0:T(8,128)(2,1)S(1)} %dynamic-slice_bitcast_fusion.15), channel_id=1, source_target_pairs={{0,8},{1,9},{2,10},{3,11},{4,12},{5,13},{6,14},{7,15},{8,0},{9,1},... | collective-permute-start | bytes 479240 | tf_op jit(solution)/shard_map/ppermute | solution.py:339
  428.1 22.4 %collective-permute-start.41 = (bf16[624,128]{1,0:T(8,128)(2,1)S(1)}, bf16[624,128]{1,0:T(8,128)(2,1)S(1)}, u32[]{:S(2)}, u32[]{:S(2)}) collective-permute-start(bf16[624,128]{1,0:T(8,128)(2,1)S(1)} %dynamic-slice_bitcast_fusion.13), channel_id=1, source_target_pairs={{0,8},{1,9},{2,10},{3,11},{4,12},{5,13},{6,14},{7,15},{8,0},{9,1},... | collective-permute-start | bytes 479240 | tf_op jit(solution)/shard_map/ppermute | solution.py:339
  433.5 20.4 %collective-permute-start.32 = (bf16[624,128]{1,0:T(8,128)(2,1)S(1)}, bf16[624,128]{1,0:T(8,128)(2,1)S(1)}, u32[]{:S(2)}, u32[]{:S(2)}) collective-permute-start(bf16[624,128]{1,0:T(8,128)(2,1)S(1)} %dynamic-slice_bitcast_fusion.16), channel_id=1, source_target_pairs={{0,8},{1,9},{2,10},{3,11},{4,12},{5,13},{6,14},{7,15},{8,0},{9,1},... | collective-permute-start | bytes 479240 | tf_op jit(solution)/shard_map/ppermute | solution.py:339
  (85 other events, 823.5 us)

commit v3 on v2

--- a/solution.py
+++ b/solution.py
@@ -351,37 +351,54 @@
     return (a.astype(F32) + b.astype(F32)).astype(BF16)
 
 
-def halved(block, bits, order):
+def tied(*values):
+    return lax.optimization_barrier(values)
+
+
+def scatter_parts(flat, cuts):
+    count = lax.axis_size("dp")
+    top = count.bit_length() - 2
+    bits = tuple(range(top, 0, -1))
+    rows = flat.shape[0] // (count // 2)
+    blocks = flat.reshape((2,) * len(bits) + (rows, LANES))
+    natural = tuple(range(1, top + 1))
+    turned = natural[1:2] + natural[:1] + natural[2:]
+    parts, start = [], 0
+    for share, turn in cuts:
+        part = lax.slice_in_dim(blocks, start, start + rows * share // 8, axis=len(bits))
+        start += rows * share // 8
+        parts.append((part, bits, turned if turn else natural))
+    return parts
+
+
+def scatter_step(parts):
     me = lax.axis_index("dp")
-    left = list(bits)
-    for step, bit in enumerate(order):
+    done = []
+    for block, left, order in parts:
+        bit = order[0]
         axis = left.index(bit)
-        left.remove(bit)
         mine = (me >> bit) & 1
         keep = pick(block, mine, axis)
         far = dp_swap(pick(block, 1 - mine, axis), 1 << bit)
-        if step + 1 < len(order):
-            block = plus(keep, far)
-        else:
-            block = keep.astype(F32) + far.astype(F32)
-    return block
+        block = plus(keep, far) if len(order) > 1 else keep.astype(F32) + far.astype(F32)
+        done.append((block, left[:axis] + left[axis + 1 :], order[1:]))
+    return done
+
+
+def tied_parts(value, parts):
+    value, *blocks = tied(value, *(block for block, _, _ in parts))
+    return value, [(block, *part[1:]) for block, part in zip(blocks, parts)]
+
+
+def scatter_end(parts):
+    while parts[0][2]:
+        parts = scatter_step(parts)
+    blocks = [block for block, _, _ in parts]
+    return jnp.concatenate(blocks) if len(blocks) > 1 else blocks[0]
 
 
 def reduce_scatter(flat, cuts):
-    count = lax.axis_size("dp")
-    top = count.bit_length() - 2
-    bits = tuple(range(top, 0, -1))
-    chips = count // 2
-    rows = flat.shape[0] // chips
-    blocks = flat.reshape((2,) * len(bits) + (rows, LANES))
-    natural = tuple(range(1, top + 1))
-    turned = natural[1:2] + natural[:1] + natural[2:]
-    done, start = [], 0
-    for share, turn in cuts:
-        part = lax.slice_in_dim(blocks, start, start + rows * share // 8, axis=len(bits))
-        start += rows * share // 8
-        done.append(halved(part, bits, turned if turn else natural))
-    return jnp.concatenate(done) if len(done) > 1 else done[0]
+    return scatter_end(scatter_parts(flat, cuts))
 
 
 def share_of(result):
@@ -417,7 +434,9 @@
     return (u * share).astype(BF16), slope
 
 
-def stream_layer(states, context, cot, lens, weights, gains, heads, fixed, pairs):
+def stream_layer(
+    states, context, cot, lens, weights, gains, heads, fixed, pairs, hook=lambda name, value: value
+):
     attend_w, up_w, down_w, qkv_w, output_w = weights
     width = states.shape[1]
     size = width // heads
@@ -442,13 +461,14 @@
     dr = attend_back(
         lens, packed, packed, packed, dz, cols, pairs, blocks, heads_in, fixed, scaling, True
     )
+    dr = hook("dr", dr)
     dh2 = de + mm_nt(dr, qkv_w)
     db, dg1 = normed_back(dh2, n2, inv2, gains[1])
     db_low = db.astype(BF16)
     du = (mm_nt(db_low, down_w) * slope).astype(BF16)
     dh1 = db + mm_nt(du, up_w)
     da, dg0 = normed_back(dh1, n1, inv1, gains[0])
-    da_low = da.astype(BF16)
+    da_low = hook("da", da.astype(BF16))
     dc = mm_nt(da_low, attend_w).astype(BF16)
     sides = {
         "attend": (context, da_low),
@@ -590,7 +610,15 @@
     ct = attend(lens, text_q, image_kv, image_kv, co_cols, pairs, co_blocks, 1, regions, co_scale)
     if early:
         ct, image_flat = lax.optimization_barrier((ct, image_flat))
-        image_part = reduce_scatter(image_flat, ((4, False), (4, True)))
+        running = {"parts": scatter_step(scatter_parts(image_flat, ((4, False), (4, True))))}
+
+    def hook(name, value):
+        if not early:
+            return value
+        value, parts = tied_parts(value, running["parts"])
+        running["parts"] = scatter_step(parts)
+        return value
+
     text_out, text_da, text_dc, text_sides, text_dg = stream_layer(
         text_all,
         ct,
@@ -601,11 +629,40 @@
         H_T,
         None,
         pairs,
-    )
+        hook,
+    )
+    gains = gain_step(pack_gains(text_dg, image_dg), 1)
+    text_dc, gains = tied(text_dc, gains)
+    gains = gain_step(gains, 2)
     text_dq, image_dkv = attend_back(
         lens, text_q, image_kv, image_kv, text_dc, co_cols, pairs, co_blocks, 1, regions, co_scale, False
     )
 
+    text_dq, image_dkv, gains = tied(text_dq, image_dkv, gains)
+    bit = 4
+    while bit < lax.axis_size("dp"):
+        gains = gain_step(gains, bit)
+        bit *= 2
+
+    text_sides["query"] = (text_all, text_dq)
+    text_sides["keyval"] = (text_all, text_dkv)
+    if early:
+        late = late_start(side, image_all, image_dkv)
+        text_flat, late = tied(gather_half(text_sides, text_sizes), late)
+        late = late_end(late)
+        text_parts = scatter_step(
+            scatter_parts(text_flat, ((2, False), (2, True), (2, False), (2, False)))
+        )
+        image_part = merged_keyval(scatter_end(running["parts"]), late)
+    else:
+        image_sides["keyval"] = (image_all, image_dkv)
+        image_part = reduce_scatter(gather_half(image_sides, image_sizes), ((8, False),))
+        text_flat = gather_half(text_sides, text_sizes)
+        text_parts = scatter_parts(text_flat, ((8, False),))
+
+    text_da, image_da, text_out, image_out, text_flat = tied(
+        text_da, image_da, text_out, image_out, text_flat
+    )
     text_result = (text_out[:own_text] * valid[:own_text]).astype(BF16)
     image_result = mm(trim, image_out[own_image:].astype(BF16)).astype(BF16)
     text_grad = (
@@ -620,20 +677,9 @@
     ).astype(BF16)
     image_grad = mm(trim, image_grad).astype(BF16)
 
-    text_sides["query"] = (text_all, text_dq)
-    text_sides["keyval"] = (text_all, text_dkv)
-    if early:
-        late = late_keyval(side, image_all, image_dkv)
-        image_part = merged_keyval(image_part, late)
-        cuts = ((2, False), (2, True), (2, False), (2, False))
-    else:
-        image_sides["keyval"] = (image_all, image_dkv)
-        image_part = reduce_scatter(gather_half(image_sides, image_sizes), ((8, False),))
-        cuts = ((8, False),)
-    text_part = reduce_scatter(gather_half(text_sides, text_sizes), cuts)
     image_share = share_of(image_part)
-    text_share = share_of(text_part)
-    text_gain_sum, image_gain_sum = lax.psum((text_dg, image_dg), "dp")
+    text_share = share_of(scatter_end(text_parts))
+    text_gain_sum, image_gain_sum = unpack_gains(gains, text_dg.shape[1])
     return (
         text_result,
         image_result,
@@ -646,7 +692,19 @@
     )
 
 
-def late_keyval(side, states, grads):
+def pack_gains(text_dg, image_dg):
+    return jnp.concatenate([text_dg, image_dg], axis=1)
+
+
+def gain_step(gains, bit):
+    return gains + dp_swap(gains, bit)
+
+
+def unpack_gains(gains, width):
+    return gains[:, :width], gains[:, width:]
+
+
+def late_start(side, states, grads):
     me = lax.axis_index("dp")
     far = (dp_swap(states, 1), dp_swap(grads, 1))
     flat = flat_grad(
@@ -654,8 +712,13 @@
     )
     blocks = flat.reshape(2, 2, 1280, LANES)
     y = (me >> 1) & 1
+    return plus(pick(blocks, 1 - y, 1), dp_swap(pick(blocks, y, 1), 2))
+
+
+def late_end(total):
+    me = lax.axis_index("dp")
+    y = (me >> 1) & 1
     odd = (me >> 2) & 1
-    total = plus(pick(blocks, 1 - y, 1), dp_swap(pick(blocks, y, 1), 2))
     own = jnp.where(y == 1, odd, 1 - odd)
     total = plus(pick(total, own), dp_swap(pick(total, 1 - own), 4))
     route = []

time: 464 us -> 384 us (0.83)
  the two profiles are of different devices: /device:TPU:1 before, /device:TPU:3 now
where the time goes in v3:
time: 384 us; the launch traced here: 377 us
  waiting for transfers between devices  117 us (30%)
  matrix products  75.3 us (20%)
  Pallas kernels  70.8 us (18%)
  starting transfers between devices  48.8 us (13%)
  other arithmetic  35.7 us (9%)
  local copies, waits for them, and re-layouts  26.2 us (7%)
    ppermute x52, waiting for transfers between devices, dp_swap(): return lax.ppermute(block, 'dp', [(i, i ^ bit) for i in range(count)])  111 us
    dot_general x20, matrix products, mm(): return jnp.dot(a, b, preferred_element_type=F32)  43.3 us
    ppermute x52, starting transfers between devices, dp_swap(): return lax.ppermute(block, 'dp', [(i, i ^ bit) for i in range(count)])  39.6 us
    dot_general x13, matrix products, mm_nt(): lax.dot_general(a, b, (((1,), (1,)), ((), ())), preferred_element_type=F32)  32.1 us
    pallas_call x8, Pallas kernels, flat_grad(): pl.pallas_call(functools.partial(flat_kernel, place=place, bm=bm, low=(lo...  29.1 us
    pallas_call x4, Pallas kernels, attend_back(): pl.pallas_call(functools.partial(body, pairs=pairs, blocks=blocks, cols=c...  22.8 us
    pallas_call x4, Pallas kernels, attend(): pl.pallas_call(functools.partial(body, pairs=pairs, blocks=blocks, cols=c...  19 us
    convert_element_type x15, other arithmetic, plus(): return (a.astype(F32) + b.astype(F32)).astype(BF16)  9.6 us
  transfers between devices with their start and end apart: 59, of which 21 were waited for; matrix products, arithmetic and copies ran while one was open for 34% of the time, Pallas kernels for 14%

profile of v3, /device:TPU:3, one launch (start us, length us, event | category | flops | bytes accessed | tf_op | source)
XLA Modules:
  0.0 377.2 jit_solution(17654807249974331237)
XLA Ops:
  7.2 3.8 collective-permute-done.1
  11.0 3.1 collective-permute-done.3
  15.1 2.7 collective-permute-start.11
  20.2 2.9 convolution_convert_fusion.2.refs_1_
  23.1 4.6 %attend.5 = bf16[192,1024]{1,0:T(8,128)(2,1)S(1)} custom-call(s32[4]{0:T(128)S(1)} %pad_add_fusion.lens_ref, bf16[192,1024]{1,0:T(8,128)(2,1)S(1)} %convolution_convert_fusion.9.refs_0_, bf16[512,2048]{1,0:T(8,128)(2,1)S(1)} %convolution_convert_fusion.2.refs_1_), custom_call_target="tpu_custom_call" | custom-call | flops 402653184 | bytes 2883584 | tf_op jit(solution)/shard_map/attend/pallas_call | solution.py:107
  35.4 4.2 %attend.6 = bf16[192,1024]{1,0:T(8,128)(2,1)S(1)} custom-call(s32[4]{0:T(128)S(1)} %pad_add_fusion.lens_ref, bf16[192,3072]{1,0:T(8,128)(2,1)S(1)} %convolution_convert_fusion.1.refs_0_), custom_call_target="tpu_custom_call" | custom-call | flops 150994944 | bytes 1572864 | tf_op jit(solution)/shard_map/attend/pallas_call | solution.py:107
  42.9 5.3 %attend_back.4 = bf16[192,3072]{1,0:T(8,128)(2,1)} custom-call(s32[4]{0:T(128)S(1)} %pad_add_fusion.lens_ref, bf16[192,3072]{1,0:T(8,128)(2,1)S(1)} %convolution_convert_fusion.1.refs_0_, bf16[192,1024]{1,0:T(8,128)(2,1)S(1)} %convolution_convert_fusion.8.refs_1_), custom_call_target="tpu_custom_call" | custom-call | flops 377487360 | bytes 3145728 | tf_op jit(solution)/shard_map/attend_back/pallas_call | solution.py:219
  48.3 4.5 %multiply_reduce_fusion.12 = (f32[1024]{0:T(1024)}, f32[192]{0:T(256)S(1)}, f32[192]{0:T(256)S(1)}, f32[192,1024]{1,0:T(8,128)S(1)}) fusion(f32[192,1024]{1,0:T(8,128)S(1)} %get-tuple-element.300, f32[192]{0:T(256)S(1)} %add_rsqrt_fusion.4, f32[192]{0:T(256)S(1)} %broadcast_multiply_fusion.15, f32[1024]{0:T(1024)S(1)} %bitcast.235, ...), kind=kOutput, calls=%fused_computation.103 | convolution fusion | flops 1209727488 | bytes 9841664 | tf_op jit(solution)/shard_map/dot_general | solution.py:26
  58.5 6.7 %attend_back.5 = (bf16[192,1024]{1,0:T(8,128)(2,1)}, bf16[512,2048]{1,0:T(8,128)(2,1)}) custom-call(s32[4]{0:T(128)S(1)} %pad_add_fusion.lens_ref, bf16[192,1024]{1,0:T(8,128)(2,1)S(1)} %convolution_convert_fusion.9.refs_0_, bf16[512,2048]{1,0:T(8,128)(2,1)S(1)} %convolution_convert_fusion.2.refs_1_, bf16[192,1024]{1,0:T(8,128)(2,1)S(1)} %convolution_convert_fusion.7.refs_2_), custom_call_target="tpu_custom_call" | custom-call | flops 1006632960 | bytes 5767168 | tf_op jit(solution)/shard_map/attend_back/pallas_call | solution.py:219
  71.6 3.3 convolution_convert_fusion.3.refs_1_
  77.4 5.5 %attend.4 = bf16[512,1024]{1,0:T(8,128)(2,1)} custom-call(s32[4]{0:T(128)S(1)} %pad_add_fusion.lens_ref, bf16[512,1024]{1,0:T(8,128)(2,1)S(1)} %convolution_convert_fusion.5.refs_0_, bf16[192,2048]{1,0:T(8,128)(2,1)S(1)} %convolution_convert_fusion.3.refs_1_), custom_call_target="tpu_custom_call" | custom-call | flops 402653184 | bytes 2883584 | tf_op jit(solution)/shard_map/attend/pallas_call | solution.py:107
  83.6 10.2 %conditional.2 = (bf16[20480,128]{1,0:T(8,128)(2,1)}) conditional(s32[]{:T(128)} %convert_element_type.373, (s32[2]{0:T(128)S(1)}, bf16[192,1024]{1,0:T(8,128)(2,1)}, bf16[192,1024]{1,0:T(8,128)(2,1)}, bf16[192,1024]{1,0:T(8,128)(2,1)S(1)}, bf16[192,1024]{1,0:T(8,128)(2,1)S(1)}, /*index=5*/bf16[192,1024]{1,0:T(8,128)(2,1)S(1)}, ...), branch_computations={%region_13.14_spmd, %region_14.15_spmd} | conditional | flops 2013265920 | bytes 14155896 | solution.py:592
  83.6 2.9 flat_grad.15.rest_0_
  86.5 4.9 %flat_grad.16.rest_0_ = bf16[20480,128]{1,0:T(8,128)(2,1)} custom-call(s32[2]{0:T(128)S(1)} %get-tuple-element.101.side_ref, bf16[192,1024]{1,0:T(8,128)(2,1)S(1)} %get-tuple-element.128.a0_ref, bf16[192,1024]{1,0:T(8,128)(2,1)S(1)} %get-tuple-element.129.a1_ref, bf16[192,3072]{1,0:T(8,128)(2,1)} %get-tuple-element.130.b0_ref, ...), custom_call_target="tpu_custom_call", output_to_operand_aliasing={{}: (5, {})} | custom-call | flops 1207959552 | bytes 6291456 | tf_op jit(solution)/shard_map/cond/branch_0_fun/flat_grad/pallas_call | solution.py:302
  93.8 3.0 fusion.59
  98.5 6.9 %multiply_convert_fusion = (bf16[512,3072]{1,0:T(8,128)(2,1)S(1)}, f32[512,3072]{1,0:T(8,128)}) fusion(bf16[512,768]{1,0:T(8,128)(2,1)} %multiply_convert_fusion.2, bf16[768,3072]{1,0:T(8,128)(2,1)} %param.31), kind=kOutput, calls=%fused_computation.7 | convolution fusion | flops 2423783424 | bytes 14942208 | tf_op jit(solution)/shard_map/dot_general | solution.py:22
  105.4 2.8 fusion.69
  110.0 3.1 convolution_convert_fusion.refs_0_
  113.1 4.6 %attend.7 = bf16[512,768]{1,0:T(8,128)(2,1)S(1)} custom-call(s32[4]{0:T(128)S(1)} %pad_add_fusion.lens_ref, bf16[512,2304]{1,0:T(8,128)(2,1)S(1)} %convolution_convert_fusion.refs_0_), custom_call_target="tpu_custom_call" | custom-call | flops 1610612736 | bytes 3145728 | tf_op jit(solution)/shard_map/attend/pallas_call | solution.py:107
  118.7 3.0 fusion.64
  128.2 2.9 fusion.27
  132.9 5.2 %attend_back.6 = bf16[512,2304]{1,0:T(8,128)(2,1)S(1)} custom-call(s32[4]{0:T(128)S(1)} %pad_add_fusion.lens_ref, bf16[512,2304]{1,0:T(8,128)(2,1)S(1)} %convolution_convert_fusion.refs_0_, bf16[512,768]{1,0:T(8,128)(2,1)S(1)} %convolution_convert_fusion.6.refs_1_), custom_call_target="tpu_custom_call" | custom-call | flops 4026531840 | bytes 6291456 | tf_op jit(solution)/shard_map/attend_back/pallas_call | solution.py:219
  138.1 14.8 %collective-permute-done.17 = bf16[2,2,1280,128]{3,2,0,1:T(8,128)(2,1)S(1)} collective-permute-done((bf16[2,2,1280,128]{3,2,0,1:T(8,128)(2,1)S(1)}, bf16[2,2,1280,128]{3,2,0,1:T(8,128)(2,1)S(1)}, u32[]{:S(2)}, u32[]{:S(2)}) %collective-permute-start.17) | collective-permute-done | bytes 1310752 | tf_op jit(solution)/shard_map/ppermute | solution.py:339
  153.3 3.7 collective-permute-done.18
  157.3 3.9 %multiply_reduce_fusion.1 = (f32[768]{0:T(1024)S(1)}, f32[512]{0:T(512)S(1)}, f32[512]{0:T(512)S(1)}, f32[512,768]{1,0:T(8,128)S(1)}) fusion(f32[512,768]{1,0:T(8,128)S(1)} %get-tuple-element.309, f32[512]{0:T(512)S(1)} %add_rsqrt_fusion.1, f32[512]{0:T(512)S(1)} %broadcast_multiply_fusion.6, f32[768]{0:T(1024)S(1)} %copy-done.66, ...), kind=kOutput, calls=%fused_computation.18 | convolution fusion | flops 1820195072 | bytes 11430912 | tf_op jit(solution)/shard_map/dot_general | solution.py:26
  161.7 6.7 %fusion.5 = bf16[512,3072]{1,0:T(8,128)(2,1)S(1)} fusion(f32[512,3072]{1,0:T(8,128)} %get-tuple-element.307, bf16[512,768]{1,0:T(8,128)(2,1)S(1)} %get-tuple-element.258, bf16[3072,768]{1,0:T(8,128)(2,1)S(1)} %bitcast.251), kind=kOutput, calls=%fused_computation.6 | convolution fusion | flops 2431647744 | bytes 14942208 | tf_op jit(solution)/shard_map/dot_general | solution.py:26
  168.5 3.1 multiply_reduce_fusion.2
  177.3 9.5 %collective-permute-done.28 = bf16[2,1280,128]{2,1,0:T(8,128)(2,1)S(1)} collective-permute-done((bf16[2,1280,128]{2,1,0:T(8,128)(2,1)S(1)}, bf16[2,1280,128]{2,1,0:T(8,128)(2,1)S(1)}, u32[]{:S(2)}, u32[]{:S(2)}) %collective-permute-start.28) | collective-permute-done | bytes 655392 | tf_op jit(solution)/shard_map/ppermute | solution.py:339
  189.1 3.7 collective-permute-done.29
  201.3 5.5 %attend_back.7 = (bf16[512,1024]{1,0:T(8,128)(2,1)S(1)}, bf16[192,2048]{1,0:T(8,128)(2,1)S(1)}) custom-call(s32[4]{0:T(128)S(1)} %pad_add_fusion.lens_ref, bf16[512,1024]{1,0:T(8,128)(2,1)S(1)} %copy-done.5, bf16[192,2048]{1,0:T(8,128)(2,1)S(1)} %copy-done.3, bf16[512,1024]{1,0:T(8,128)(2,1)S(1)} %convolution_convert_fusion.4.refs_2_), custom_call_target="tpu_custom_call" | custom-call | flops 1006632960 | bytes 5767168 | tf_op jit(solution)/shard_map/attend_back/pallas_call | solution.py:219
  208.0 4.3 %fusion.25 = f32[256,768]{1,0:T(8,128)} fusion(bf16[768,2048]{1,0:T(8,128)(2,1)} %param.29, bf16[512,2048]{1,0:T(8,128)(2,1)} %get-tuple-element.224), kind=kOutput, calls=%fused_computation.93 | convolution fusion | flops 805306368 | bytes 4980736 | tf_op jit(solution)/shard_map/dot_general | solution.py:26
  216.6 15.0 %collective-permute-done.58 = f32[3,1792]{1,0:T(4,128)S(1)} collective-permute-done((f32[3,1792]{1,0:T(4,128)S(1)}, f32[3,1792]{1,0:T(4,128)S(1)}, u32[]{:S(2)}, u32[]{:S(2)}) %collective-permute-start.58) | collective-permute-done | bytes 21536 | tf_op jit(solution)/shard_map/ppermute | solution.py:339
  238.4 11.0 %collective-permute-done.54 = bf16[1280,128]{1,0:T(8,128)(2,1)S(1)} collective-permute-done((bf16[1280,128]{1,0:T(8,128)(2,1)S(1)}, bf16[1280,128]{1,0:T(8,128)(2,1)S(1)}, u32[]{:S(2)}, u32[]{:S(2)}) %collective-permute-start.54) | collective-permute-done | bytes 327712 | tf_op jit(solution)/shard_map/ppermute | solution.py:339
  253.3 13.9 %collective-permute-done.37 = bf16[2,1280,128]{2,1,0:T(8,128)(2,1)S(1)} collective-permute-done((bf16[2,1280,128]{2,1,0:T(8,128)(2,1)S(1)}, bf16[2,1280,128]{2,1,0:T(8,128)(2,1)S(1)}, u32[]{:S(2)}, u32[]{:S(2)}) %collective-permute-start.37) | collective-permute-done | bytes 655392 | tf_op jit(solution)/shard_map/ppermute | solution.py:339
  271.0 16.8 %conditional.3 = (bf16[19968,128]{1,0:T(8,128)(2,1)}) conditional(s32[]{:T(128)} %convert_element_type.373, (s32[2]{0:T(128)S(1)}, bf16[512,768]{1,0:T(8,128)(2,1)}, bf16[512,768]{1,0:T(8,128)(2,1)}, bf16[512,3072]{1,0:T(8,128)(2,1)S(1)}, bf16[512,3072]{1,0:T(8,128)(2,1)S(1)}, /*index=5*/bf16[512,3072]{1,0:T(8,128)(2,1)S(1)}, ...), branch_computations={%region_32.33_spmd, %region_33.34_spmd} | conditional | flops 5234491392 | bytes 34209856 | solution.py:592
  271.0 3.7 flat_grad.21.rest_0_
  274.7 5.6 %flat_grad.22.rest_0_ = bf16[19968,128]{1,0:T(8,128)(2,1)} custom-call(s32[2]{0:T(128)S(1)} %get-tuple-element.149.side_ref, bf16[512,3072]{1,0:T(8,128)(2,1)S(1)} %get-tuple-element.158.a0_ref, bf16[512,3072]{1,0:T(8,128)(2,1)S(1)} %get-tuple-element.159.a1_ref, bf16[512,768]{1,0:T(8,128)(2,1)S(1)} %get-tuple-element.160.b0_ref, ...), custom_call_target="tpu_custom_call", output_to_operand_aliasing={{}: (5, {})} | custom-call | flops 2415919104 | bytes 10223616 | tf_op jit(solution)/shard_map/cond/branch_0_fun/flat_grad/pallas_call | solution.py:302
  280.3 4.8 %flat_grad.23.rest_0_ = bf16[19968,128]{1,0:T(8,128)(2,1)} custom-call(s32[2]{0:T(128)S(1)} %get-tuple-element.149.side_ref, bf16[512,768]{1,0:T(8,128)(2,1)} %get-tuple-element.154.a0_ref, bf16[512,768]{1,0:T(8,128)(2,1)} %get-tuple-element.155.a1_ref, bf16[512,2304]{1,0:T(8,128)(2,1)S(1)} %get-tuple-element.156.b0_ref, ...), custom_call_target="tpu_custom_call", output_to_operand_aliasing={{}: (5, {})} | custom-call | flops 1811939328 | bytes 8060928 | tf_op jit(solution)/shard_map/cond/branch_0_fun/flat_grad/pallas_call | solution.py:302
  287.8 2.9 fusion.65
  302.5 2.8 convolution_convert_fusion.10
  309.2 9.9 %collective-permute-done.51 = bf16[1280,128]{1,0:T(8,128)(2,1)} collective-permute-done((bf16[1280,128]{1,0:T(8,128)(2,1)}, bf16[1280,128]{1,0:T(8,128)(2,1)}, u32[]{:S(2)}, u32[]{:S(2)}) %collective-permute-start.51) | collective-permute-done | bytes 327712 | tf_op jit(solution)/shard_map/ppermute | solution.py:339
  327.8 7.2 %collective-permute-done.38 = bf16[2,2,624,128]{3,2,0,1:T(8,128)(2,1)} collective-permute-done((bf16[2,2,624,128]{3,2,0,1:T(8,128)(2,1)}, bf16[2,2,624,128]{3,2,0,1:T(8,128)(2,1)}, u32[]{:S(2)}, u32[]{:S(2)}) %collective-permute-start.38) | collective-permute-done | bytes 639008 | tf_op jit(solution)/shard_map/ppermute | solution.py:339
  336.5 4.3 %collective-permute-start.53 = (bf16[1280,128]{1,0:T(8,128)(2,1)S(1)}, bf16[1280,128]{1,0:T(8,128)(2,1)S(1)}, u32[]{:S(2)}, u32[]{:S(2)}) collective-permute-start(bf16[1280,128]{1,0:T(8,128)(2,1)S(1)} %add_convert_fusion), channel_id=1, source_target_pairs={{16,0},{17,1},{18,2},{19,3},{20,4},{21,5},{22,6},{23,7},{24,8},{25... | collective-permute-start | bytes 983048 | tf_op jit(solution)/shard_map/ppermute | solution.py:731
  342.2 2.8 collective-permute-start.46
  345.2 7.8 %collective-permute-done.39 = bf16[2,624,128]{2,1,0:T(8,128)(2,1)S(1)} collective-permute-done((bf16[2,624,128]{2,1,0:T(8,128)(2,1)S(1)}, bf16[2,624,128]{2,1,0:T(8,128)(2,1)S(1)}, u32[]{:S(2)}, u32[]{:S(2)}) %collective-permute-start.39) | collective-permute-done | bytes 319520 | tf_op jit(solution)/shard_map/ppermute | solution.py:339
  353.3 4.8 %copy.59 = f32[1280,2,128]{2,1,0:T(2,128)S(1)} copy(f32[1280,2,128]{2,0,1:T(8,128)S(1)} %maximum_convert_fusion) | data formatting | bytes 2621440 | tf_op jit(solution)/shard_map/convert_element_type | solution.py:741
  358.7 3.4 collective-permute-start.56
  362.2 8.4 %collective-permute-done.40 = bf16[624,128]{1,0:T(8,128)(2,1)S(1)} collective-permute-done((bf16[624,128]{1,0:T(8,128)(2,1)S(1)}, bf16[624,128]{1,0:T(8,128)(2,1)S(1)}, u32[]{:S(2)}, u32[]{:S(2)}) %collective-permute-start.40) | collective-permute-done | bytes 159776 | tf_op jit(solution)/shard_map/ppermute | solution.py:339
  (442 shorter events, 125.1 us)
Async XLA Ops:
  0.7 18.7 %collective-permute-start.2 = (bf16[256,768]{1,0:T(8,128)(2,1)}, bf16[256,768]{1,0:T(8,128)(2,1)S(1)}, u32[]{:S(2)}, u32[]{:S(2)}) collective-permute-start(bf16[256,768]{1,0:T(8,128)(2,1)} %param.25), channel_id=1, source_target_pairs={{0,16},{16,0},{1,17},{17,1},{2,18},{18,2},{3,19},{19,3},{4,20},{20... | collective-permute-start | bytes 1179656 | tf_op jit(solution)/shard_map/ppermute | solution.py:343
  0.8 10.2 %collective-permute-start.1 = (s32[2]{0:T(128)}, s32[2]{0:T(128)S(1)}, u32[]{:S(2)}, u32[]{:S(2)}) collective-permute-start(s32[2]{0:T(128)} %param.27), channel_id=1, source_target_pairs={{0,16},{16,0},{1,17},{17,1},{2,18},{18,2},{3,19},{19,3},{4,20},{20... | collective-permute-start | bytes 32 | tf_op jit(solution)/shard_map/ppermute | solution.py:343
  2.2 11.9 %collective-permute-start.3 = (bf16[72,1024]{1,0:T(8,128)(2,1)}, bf16[72,1024]{1,0:T(8,128)(2,1)S(1)}, u32[]{:S(2)}, u32[]{:S(2)}) collective-permute-start(bf16[72,1024]{1,0:T(8,128)(2,1)} %param.26), channel_id=1, source_target_pairs={{0,16},{16,0},{1,17},{17,1},{2,18},{18,2},{3,19},{19,3},{4,20},{20... | collective-permute-start | bytes 442376 | tf_op jit(solution)/shard_map/ppermute | solution.py:343
  2.3 38.4 %collective-permute-start.5 = (bf16[72,1024]{1,0:T(8,128)(2,1)}, bf16[72,1024]{1,0:T(8,128)(2,1)S(1)}, u32[]{:S(2)}, u32[]{:S(2)}) collective-permute-start(bf16[72,1024]{1,0:T(8,128)(2,1)} %param.45), channel_id=1, source_target_pairs={{0,16},{16,0},{1,17},{17,1},{2,18},{18,2},{3,19},{19,3},{4,20},{20... | collective-permute-start | bytes 442376 | tf_op jit(solution)/shard_map/ppermute | solution.py:343
  15.1 51.0 %collective-permute-start.11 = (bf16[192,1024]{1,0:T(8,128)(2,1)}, bf16[192,1024]{1,0:T(8,128)(2,1)}, u32[]{:S(2)}, u32[]{:S(2)}) collective-permute-start(bf16[192,1024]{1,0:T(8,128)(2,1)} %fusion.18.a0_ref), channel_id=1, source_target_pairs={{0,1},{1,0},{2,3},{3,2},{4,5},{5,4},{6,7},{7,6},{8,9},{9,8},{10,11... | collective-permute-start | bytes 1179656 | tf_op jit(solution)/shard_map/ppermute | solution.py:339
  31.5 34.7 %collective-permute-start.4 = (bf16[192,1024]{1,0:T(8,128)(2,1)}, bf16[192,1024]{1,0:T(8,128)(2,1)}, u32[]{:S(2)}, u32[]{:S(2)}) collective-permute-start(bf16[192,1024]{1,0:T(8,128)(2,1)} %get-tuple-element.297), channel_id=1, source_target_pairs={{0,1},{1,0},{2,3},{3,2},{4,5},{5,4},{6,7},{7,6},{8,9},{9,8},{10,11... | collective-permute-start | bytes 1179656 | tf_op jit(solution)/shard_map/ppermute | solution.py:339
  65.6 17.9 %collective-permute-start.8 = (bf16[192,3072]{1,0:T(8,128)(2,1)}, bf16[192,3072]{1,0:T(8,128)(2,1)}, u32[]{:S(2)}, u32[]{:S(2)}) collective-permute-start(bf16[192,3072]{1,0:T(8,128)(2,1)} %attend_back.4), channel_id=1, source_target_pairs={{0,1},{1,0},{2,3},{3,2},{4,5},{5,4},{6,7},{7,6},{8,9},{9,8},{10,11... | collective-permute-start | bytes 3538952 | tf_op jit(solution)/shard_map/ppermute | solution.py:339
  69.9 13.1 %collective-permute-start.6 = (bf16[192,1024]{1,0:T(8,128)(2,1)}, bf16[192,1024]{1,0:T(8,128)(2,1)S(1)}, u32[]{:S(2)}, u32[]{:S(2)}) collective-permute-start(bf16[192,1024]{1,0:T(8,128)(2,1)} %copy-done.56), channel_id=1, source_target_pairs={{0,1},{1,0},{2,3},{3,2},{4,5},{5,4},{6,7},{7,6},{8,9},{9,8},{10,11... | collective-permute-start | bytes 1179656 | tf_op jit(solution)/shard_map/ppermute | solution.py:339
  70.1 12.8 %collective-permute-start.7 = (bf16[192,1024]{1,0:T(8,128)(2,1)}, bf16[192,1024]{1,0:T(8,128)(2,1)S(1)}, u32[]{:S(2)}, u32[]{:S(2)}) collective-permute-start(bf16[192,1024]{1,0:T(8,128)(2,1)} %copy-done.54), channel_id=1, source_target_pairs={{0,1},{1,0},{2,3},{3,2},{4,5},{5,4},{6,7},{7,6},{8,9},{9,8},{10,11... | collective-permute-start | bytes 1179656 | tf_op jit(solution)/shard_map/ppermute | solution.py:339
  70.7 12.5 %collective-permute-start.9 = (bf16[192,1024]{1,0:T(8,128)(2,1)}, bf16[192,1024]{1,0:T(8,128)(2,1)S(1)}, u32[]{:S(2)}, u32[]{:S(2)}) collective-permute-start(bf16[192,1024]{1,0:T(8,128)(2,1)} %copy-done.21), channel_id=1, source_target_pairs={{0,1},{1,0},{2,3},{3,2},{4,5},{5,4},{6,7},{7,6},{8,9},{9,8},{10,11... | collective-permute-start | bytes 1179656 | tf_op jit(solution)/shard_map/ppermute | solution.py:339
  71.3 12.3 %collective-permute-start.10 = (bf16[192,1024]{1,0:T(8,128)(2,1)}, bf16[192,1024]{1,0:T(8,128)(2,1)S(1)}, u32[]{:S(2)}, u32[]{:S(2)}) collective-permute-start(bf16[192,1024]{1,0:T(8,128)(2,1)} %copy-done.25), channel_id=1, source_target_pairs={{0,1},{1,0},{2,3},{3,2},{4,5},{5,4},{6,7},{7,6},{8,9},{9,8},{10,11... | collective-permute-start | bytes 1179656 | tf_op jit(solution)/shard_map/ppermute | solution.py:339
  83.0 41.4 %collective-permute-start = (bf16[256,768]{1,0:T(8,128)(2,1)}, bf16[256,768]{1,0:T(8,128)(2,1)}, u32[]{:S(2)}, u32[]{:S(2)}) collective-permute-start(bf16[256,768]{1,0:T(8,128)(2,1)} %param.44), channel_id=1, source_target_pairs={{0,16},{16,0},{1,17},{17,1},{2,18},{18,2},{3,19},{19,3},{4,20},{20... | collective-permute-start | bytes 1179656 | tf_op jit(solution)/shard_map/ppermute | solution.py:343
  83.0 113.0 %collective-permute-start.27 = (bf16[512,768]{1,0:T(8,128)(2,1)}, bf16[512,768]{1,0:T(8,128)(2,1)}, u32[]{:S(2)}, u32[]{:S(2)}) collective-permute-start(bf16[512,768]{1,0:T(8,128)(2,1)} %constant_dynamic-update-slice_fusion), channel_id=1, source_target_pairs={{0,1},{1,0},{2,3},{3,2},{4,5},{5,4},{6,7},{7,6},{8,9},{9,8},{10,11... | collective-permute-start | bytes 2359304 | tf_op jit(solution)/shard_map/ppermute | solution.py:339
  83.2 129.8 %collective-permute-start.33 = (bf16[512,2048]{1,0:T(8,128)(2,1)}, bf16[512,2048]{1,0:T(8,128)(2,1)}, u32[]{:S(2)}, u32[]{:S(2)}) collective-permute-start(bf16[512,2048]{1,0:T(8,128)(2,1)} %get-tuple-element.224), channel_id=1, source_target_pairs={{0,1},{1,0},{2,3},{3,2},{4,5},{5,4},{6,7},{7,6},{8,9},{9,8},{10,11... | collective-permute-start | bytes 6291464 | tf_op jit(solution)/shard_map/ppermute | solution.py:339
  98.3 109.3 %collective-permute-start.19 = (bf16[512,768]{1,0:T(8,128)(2,1)}, bf16[512,768]{1,0:T(8,128)(2,1)}, u32[]{:S(2)}, u32[]{:S(2)}) collective-permute-start(bf16[512,768]{1,0:T(8,128)(2,1)} %multiply_convert_fusion.2), channel_id=1, source_target_pairs={{0,1},{1,0},{2,3},{3,2},{4,5},{5,4},{6,7},{7,6},{8,9},{9,8},{10,11... | collective-permute-start | bytes 2359304 | tf_op jit(solution)/shard_map/ppermute | solution.py:339
  122.3 30.6 %collective-permute-start.17 = (bf16[2,2,1280,128]{3,2,0,1:T(8,128)(2,1)S(1)}, bf16[2,2,1280,128]{3,2,0,1:T(8,128)(2,1)S(1)}, u32[]{:S(2)}, u32[]{:S(2)}) collective-permute-start(bf16[2,2,1280,128]{3,2,0,1:T(8,128)(2,1)S(1)} %bitcast.228), channel_id=1, source_target_pairs={{0,2},{1,3},{2,0},{3,1},{4,6},{5,7},{6,4},{7,5},{8,10},{9,11},{10,... | collective-permute-start | bytes 3932168 | tf_op jit(solution)/shard_map/ppermute | solution.py:339
  126.8 30.1 %collective-permute-start.18 = (bf16[2,2,1280,128]{3,2,0,1:T(8,128)(2,1)S(1)}, bf16[2,2,1280,128]{3,2,0,1:T(8,128)(2,1)S(1)}, u32[]{:S(2)}, u32[]{:S(2)}) collective-permute-start(bf16[2,2,1280,128]{3,2,0,1:T(8,128)(2,1)S(1)} %bitcast.229), channel_id=1, source_target_pairs={{0,4},{1,5},{2,6},{3,7},{4,0},{5,1},{6,2},{7,3},{8,12},{9,13},{10,... | collective-permute-start | bytes 3932168 | tf_op jit(solution)/shard_map/ppermute | solution.py:339
  171.7 15.1 %collective-permute-start.28 = (bf16[2,1280,128]{2,1,0:T(8,128)(2,1)S(1)}, bf16[2,1280,128]{2,1,0:T(8,128)(2,1)S(1)}, u32[]{:S(2)}, u32[]{:S(2)}) collective-permute-start(bf16[2,1280,128]{2,1,0:T(8,128)(2,1)S(1)} %dynamic-slice_bitcast_fusion.3), channel_id=1, source_target_pairs={{0,4},{1,5},{2,6},{3,7},{4,0},{5,1},{6,2},{7,3},{8,12},{9,13},{10,... | collective-permute-start | bytes 1966088 | tf_op jit(solution)/shard_map/ppermute | solution.py:339
  176.4 16.4 %collective-permute-start.29 = (bf16[2,1280,128]{2,1,0:T(8,128)(2,1)S(1)}, bf16[2,1280,128]{2,1,0:T(8,128)(2,1)S(1)}, u32[]{:S(2)}, u32[]{:S(2)}) collective-permute-start(bf16[2,1280,128]{2,1,0:T(8,128)(2,1)S(1)} %dynamic-slice_bitcast_fusion.2), channel_id=1, source_target_pairs={{0,2},{1,3},{2,0},{3,1},{4,6},{5,7},{6,4},{7,5},{8,10},{9,11},{10,... | collective-permute-start | bytes 1966088 | tf_op jit(solution)/shard_map/ppermute | solution.py:339
  186.8 21.0 %collective-permute-start.23 = (bf16[512,768]{1,0:T(8,128)(2,1)}, bf16[512,768]{1,0:T(8,128)(2,1)}, u32[]{:S(2)}, u32[]{:S(2)}) collective-permute-start(bf16[512,768]{1,0:T(8,128)(2,1)} %multiply_convert_fusion.1), channel_id=1, source_target_pairs={{0,1},{1,0},{2,3},{3,2},{4,5},{5,4},{6,7},{7,6},{8,9},{9,8},{10,11... | collective-permute-start | bytes 2359304 | tf_op jit(solution)/shard_map/ppermute | solution.py:339
  195.9 19.4 %collective-permute-start.34 = (bf16[512,1024]{1,0:T(8,128)(2,1)}, bf16[512,1024]{1,0:T(8,128)(2,1)S(1)}, u32[]{:S(2)}, u32[]{:S(2)}) collective-permute-start(bf16[512,1024]{1,0:T(8,128)(2,1)} %attend.4), channel_id=1, source_target_pairs={{0,1},{1,0},{2,3},{3,2},{4,5},{5,4},{6,7},{7,6},{8,9},{9,8},{10,11... | collective-permute-start | bytes 3145736 | tf_op jit(solution)/shard_map/ppermute | solution.py:339
  198.0 69.9 %collective-permute-start.20 = (bf16[512,3072]{1,0:T(8,128)(2,1)}, bf16[512,3072]{1,0:T(8,128)(2,1)S(1)}, u32[]{:S(2)}, u32[]{:S(2)}) collective-permute-start(bf16[512,3072]{1,0:T(8,128)(2,1)} %copy-done.9), channel_id=1, source_target_pairs={{0,1},{1,0},{2,3},{3,2},{4,5},{5,4},{6,7},{7,6},{8,9},{9,8},{10,11... | collective-permute-start | bytes 9437192 | tf_op jit(solution)/shard_map/ppermute | solution.py:339
  207.7 24.8 %collective-permute-start.36 = (bf16[192,2048]{1,0:T(8,128)(2,1)S(1)}, bf16[192,2048]{1,0:T(8,128)(2,1)S(1)}, u32[]{:S(2)}, u32[]{:S(2)}) collective-permute-start(bf16[192,2048]{1,0:T(8,128)(2,1)S(1)} %get-tuple-element.225.b0_ref), channel_id=1, source_target_pairs={{0,1},{1,0},{2,3},{3,2},{4,5},{5,4},{6,7},{7,6},{8,9},{9,8},{10,11... | collective-permute-start | bytes 2359304 | tf_op jit(solution)/shard_map/ppermute | solution.py:339
  207.8 4.5 %collective-permute-start.57 = (f32[3,1792]{1,0:T(4,128)S(1)}, f32[3,1792]{1,0:T(4,128)S(1)}, u32[]{:S(2)}, u32[]{:S(2)}) collective-permute-start(f32[3,1792]{1,0:T(4,128)S(1)} %add.341), channel_id=1, source_target_pairs={{0,4},{1,5},{2,6},{3,7},{4,0},{5,1},{6,2},{7,3},{8,12},{9,13},{10,... | collective-permute-start | bytes 64520 | tf_op jit(solution)/shard_map/ppermute | solution.py:339
  212.3 58.7 %collective-permute-start.21 = (bf16[512,3072]{1,0:T(8,128)(2,1)S(1)}, bf16[512,3072]{1,0:T(8,128)(2,1)S(1)}, u32[]{:S(2)}, u32[]{:S(2)}) collective-permute-start(bf16[512,3072]{1,0:T(8,128)(2,1)S(1)} %copy-done.31), channel_id=1, source_target_pairs={{0,1},{1,0},{2,3},{3,2},{4,5},{5,4},{6,7},{7,6},{8,9},{9,8},{10,11... | collective-permute-start | bytes 9437192 | tf_op jit(solution)/shard_map/ppermute | solution.py:339
  213.0 19.4 %collective-permute-start.55 = (bf16[1280,128]{1,0:T(8,128)(2,1)S(1)}, bf16[1280,128]{1,0:T(8,128)(2,1)S(1)}, u32[]{:S(2)}, u32[]{:S(2)}) collective-permute-start(bf16[1280,128]{1,0:T(8,128)(2,1)S(1)} %dynamic-slice_bitcast_fusion.6), channel_id=1, source_target_pairs={{0,8},{1,9},{2,10},{3,11},{4,12},{5,13},{6,14},{7,15},{8,0},{9,1},... | collective-permute-start | bytes 983048 | tf_op jit(solution)/shard_map/ppermute | solution.py:339
  215.4 16.1 %collective-permute-start.58 = (f32[3,1792]{1,0:T(4,128)S(1)}, f32[3,1792]{1,0:T(4,128)S(1)}, u32[]{:S(2)}, u32[]{:S(2)}) collective-permute-start(f32[3,1792]{1,0:T(4,128)S(1)} %add.369), channel_id=1, source_target_pairs={{0,8},{1,9},{2,10},{3,11},{4,12},{5,13},{6,14},{7,15},{8,0},{9,1},... | collective-permute-start | bytes 64520 | tf_op jit(solution)/shard_map/ppermute | solution.py:339
  231.5 19.2 %collective-permute-start.35 = (bf16[512,768]{1,0:T(8,128)(2,1)S(1)}, bf16[512,768]{1,0:T(8,128)(2,1)S(1)}, u32[]{:S(2)}, u32[]{:S(2)}) collective-permute-start(bf16[512,768]{1,0:T(8,128)(2,1)S(1)} %copy-done.37), channel_id=1, source_target_pairs={{0,1},{1,0},{2,3},{3,2},{4,5},{5,4},{6,7},{7,6},{8,9},{9,8},{10,11... | collective-permute-start | bytes 2359304 | tf_op jit(solution)/shard_map/ppermute | solution.py:339
  232.4 38.6 %collective-permute-start.24 = (bf16[512,2304]{1,0:T(8,128)(2,1)S(1)}, bf16[512,2304]{1,0:T(8,128)(2,1)S(1)}, u32[]{:S(2)}, u32[]{:S(2)}) collective-permute-start(bf16[512,2304]{1,0:T(8,128)(2,1)S(1)} %copy-done.46), channel_id=1, source_target_pairs={{0,1},{1,0},{2,3},{3,2},{4,5},{5,4},{6,7},{7,6},{8,9},{9,8},{10,11... | collective-permute-start | bytes 7077896 | tf_op jit(solution)/shard_map/ppermute | solution.py:339
  232.5 16.9 %collective-permute-start.54 = (bf16[1280,128]{1,0:T(8,128)(2,1)S(1)}, bf16[1280,128]{1,0:T(8,128)(2,1)S(1)}, u32[]{:S(2)}, u32[]{:S(2)}) collective-permute-start(bf16[1280,128]{1,0:T(8,128)(2,1)S(1)} %dynamic-slice_bitcast_fusion.7), channel_id=1, source_target_pairs={{0,8},{1,9},{2,10},{3,11},{4,12},{5,13},{6,14},{7,15},{8,0},{9,1},... | collective-permute-start | bytes 983048 | tf_op jit(solution)/shard_map/ppermute | solution.py:339
  250.7 16.4 %collective-permute-start.37 = (bf16[2,1280,128]{2,1,0:T(8,128)(2,1)S(1)}, bf16[2,1280,128]{2,1,0:T(8,128)(2,1)S(1)}, u32[]{:S(2)}, u32[]{:S(2)}) collective-permute-start(bf16[2,1280,128]{2,1,0:T(8,128)(2,1)S(1)} %dynamic-slice_bitcast_fusion.1), channel_id=1, source_target_pairs={{0,2},{1,3},{2,0},{3,1},{4,6},{5,7},{6,4},{7,5},{8,10},{9,11},{10,... | collective-permute-start | bytes 1966088 | tf_op jit(solution)/shard_map/ppermute | solution.py:339
  252.9 16.3 %collective-permute-start.25 = (bf16[512,768]{1,0:T(8,128)(2,1)S(1)}, bf16[512,768]{1,0:T(8,128)(2,1)S(1)}, u32[]{:S(2)}, u32[]{:S(2)}) collective-permute-start(bf16[512,768]{1,0:T(8,128)(2,1)S(1)} %copy-done.63), channel_id=1, source_target_pairs={{0,1},{1,0},{2,3},{3,2},{4,5},{5,4},{6,7},{7,6},{8,9},{9,8},{10,11... | collective-permute-start | bytes 2359304 | tf_op jit(solution)/shard_map/ppermute | solution.py:339
  291.7 30.6 %collective-permute-start.47 = (bf16[2,2,624,128]{3,2,1,0:T(8,128)(2,1)}, bf16[2,2,624,128]{3,2,1,0:T(8,128)(2,1)}, u32[]{:S(2)}, u32[]{:S(2)}) collective-permute-start(bf16[2,2,624,128]{3,2,1,0:T(8,128)(2,1)} %dynamic-slice_bitcast_fusion.5), channel_id=1, source_target_pairs={{0,2},{1,3},{2,0},{3,1},{4,6},{5,7},{6,4},{7,5},{8,10},{9,11},{10,... | collective-permute-start | bytes 1916936 | tf_op jit(solution)/shard_map/ppermute | solution.py:339
  293.6 30.0 %collective-permute-start.44 = (bf16[2,2,624,128]{3,2,0,1:T(8,128)(2,1)}, bf16[2,2,624,128]{3,2,0,1:T(8,128)(2,1)}, u32[]{:S(2)}, u32[]{:S(2)}) collective-permute-start(bf16[2,2,624,128]{3,2,0,1:T(8,128)(2,1)} %bitcast.211), channel_id=1, source_target_pairs={{0,2},{1,3},{2,0},{3,1},{4,6},{5,7},{6,4},{7,5},{8,10},{9,11},{10,... | collective-permute-start | bytes 1916936 | tf_op jit(solution)/shard_map/ppermute | solution.py:339
  296.8 29.7 %collective-permute-start.41 = (bf16[2,2,624,128]{3,2,0,1:T(8,128)(2,1)}, bf16[2,2,624,128]{3,2,0,1:T(8,128)(2,1)}, u32[]{:S(2)}, u32[]{:S(2)}) collective-permute-start(bf16[2,2,624,128]{3,2,0,1:T(8,128)(2,1)} %bitcast.212), channel_id=1, source_target_pairs={{0,4},{1,5},{2,6},{3,7},{4,0},{5,1},{6,2},{7,3},{8,12},{9,13},{10,... | collective-permute-start | bytes 1916936 | tf_op jit(solution)/shard_map/ppermute | solution.py:339
  298.6 36.4 %collective-permute-start.38 = (bf16[2,2,624,128]{3,2,0,1:T(8,128)(2,1)}, bf16[2,2,624,128]{3,2,0,1:T(8,128)(2,1)}, u32[]{:S(2)}, u32[]{:S(2)}) collective-permute-start(bf16[2,2,624,128]{3,2,0,1:T(8,128)(2,1)} %bitcast.213), channel_id=1, source_target_pairs={{0,2},{1,3},{2,0},{3,1},{4,6},{5,7},{6,4},{7,5},{8,10},{9,11},{10,... | collective-permute-start | bytes 1916936 | tf_op jit(solution)/shard_map/ppermute | solution.py:339
  299.6 19.5 %collective-permute-start.51 = (bf16[1280,128]{1,0:T(8,128)(2,1)}, bf16[1280,128]{1,0:T(8,128)(2,1)}, u32[]{:S(2)}, u32[]{:S(2)}) collective-permute-start(bf16[1280,128]{1,0:T(8,128)(2,1)} %dynamic-slice_bitcast_fusion.8), channel_id=1, source_target_pairs={{0,4},{1,5},{2,6},{3,7},{4,0},{5,1},{6,2},{7,3},{8,12},{9,13},{10,... | collective-permute-start | bytes 983048 | tf_op jit(solution)/shard_map/ppermute | solution.py:339
  320.3 16.1 %collective-permute-start.52 = (bf16[1280,128]{1,0:T(8,128)(2,1)S(1)}, bf16[1280,128]{1,0:T(8,128)(2,1)S(1)}, u32[]{:S(2)}, u32[]{:S(2)}) collective-permute-start(bf16[1280,128]{1,0:T(8,128)(2,1)S(1)} %fusion.32), channel_id=1, source_target_pairs={{0,8},{1,9},{10,2},{11,3},{12,4},{13,5},{14,6},{15,7},{16,24},{17,... | collective-permute-start | bytes 983048 | tf_op jit(solution)/shard_map/ppermute | solution.py:730
  323.6 17.2 %collective-permute-start.48 = (bf16[2,624,128]{2,1,0:T(8,128)(2,1)S(1)}, bf16[2,624,128]{2,1,0:T(8,128)(2,1)S(1)}, u32[]{:S(2)}, u32[]{:S(2)}) collective-permute-start(bf16[2,624,128]{2,1,0:T(8,128)(2,1)S(1)} %dynamic-slice_bitcast_fusion.9), channel_id=1, source_target_pairs={{0,4},{1,5},{2,6},{3,7},{4,0},{5,1},{6,2},{7,3},{8,12},{9,13},{10,... | collective-permute-start | bytes 958472 | tf_op jit(solution)/shard_map/ppermute | solution.py:339
  325.0 17.1 %collective-permute-start.45 = (bf16[2,624,128]{2,1,0:T(8,128)(2,1)S(1)}, bf16[2,624,128]{2,1,0:T(8,128)(2,1)S(1)}, u32[]{:S(2)}, u32[]{:S(2)}) collective-permute-start(bf16[2,624,128]{2,1,0:T(8,128)(2,1)S(1)} %dynamic-slice_bitcast_fusion.10), channel_id=1, source_target_pairs={{0,4},{1,5},{2,6},{3,7},{4,0},{5,1},{6,2},{7,3},{8,12},{9,13},{10,... | collective-permute-start | bytes 958472 | tf_op jit(solution)/shard_map/ppermute | solution.py:339
  327.8 17.2 %collective-permute-start.42 = (bf16[2,624,128]{2,1,0:T(8,128)(2,1)S(1)}, bf16[2,624,128]{2,1,0:T(8,128)(2,1)S(1)}, u32[]{:S(2)}, u32[]{:S(2)}) collective-permute-start(bf16[2,624,128]{2,1,0:T(8,128)(2,1)S(1)} %dynamic-slice_bitcast_fusion.11), channel_id=1, source_target_pairs={{0,2},{1,3},{2,0},{3,1},{4,6},{5,7},{6,4},{7,5},{8,10},{9,11},{10,... | collective-permute-start | bytes 958472 | tf_op jit(solution)/shard_map/ppermute | solution.py:339
  336.3 16.7 %collective-permute-start.39 = (bf16[2,624,128]{2,1,0:T(8,128)(2,1)S(1)}, bf16[2,624,128]{2,1,0:T(8,128)(2,1)S(1)}, u32[]{:S(2)}, u32[]{:S(2)}) collective-permute-start(bf16[2,624,128]{2,1,0:T(8,128)(2,1)S(1)} %dynamic-slice_bitcast_fusion.12), channel_id=1, source_target_pairs={{0,4},{1,5},{2,6},{3,7},{4,0},{5,1},{6,2},{7,3},{8,12},{9,13},{10,... | collective-permute-start | bytes 958472 | tf_op jit(solution)/shard_map/ppermute | solution.py:339
  336.5 16.7 %collective-permute-start.53 = (bf16[1280,128]{1,0:T(8,128)(2,1)S(1)}, bf16[1280,128]{1,0:T(8,128)(2,1)S(1)}, u32[]{:S(2)}, u32[]{:S(2)}) collective-permute-start(bf16[1280,128]{1,0:T(8,128)(2,1)S(1)} %add_convert_fusion), channel_id=1, source_target_pairs={{16,0},{17,1},{18,2},{19,3},{20,4},{21,5},{22,6},{23,7},{24,8},{25... | collective-permute-start | bytes 983048 | tf_op jit(solution)/shard_map/ppermute | solution.py:731
  340.9 21.2 %collective-permute-start.49 = (bf16[624,128]{1,0:T(8,128)(2,1)S(1)}, bf16[624,128]{1,0:T(8,128)(2,1)S(1)}, u32[]{:S(2)}, u32[]{:S(2)}) collective-permute-start(bf16[624,128]{1,0:T(8,128)(2,1)S(1)} %dynamic-slice_bitcast_fusion.13), channel_id=1, source_target_pairs={{0,8},{1,9},{2,10},{3,11},{4,12},{5,13},{6,14},{7,15},{8,0},{9,1},... | collective-permute-start | bytes 479240 | tf_op jit(solution)/shard_map/ppermute | solution.py:339
  342.2 19.9 %collective-permute-start.46 = (bf16[624,128]{1,0:T(8,128)(2,1)S(1)}, bf16[624,128]{1,0:T(8,128)(2,1)S(1)}, u32[]{:S(2)}, u32[]{:S(2)}) collective-permute-start(bf16[624,128]{1,0:T(8,128)(2,1)S(1)} %dynamic-slice_bitcast_fusion.14), channel_id=1, source_target_pairs={{0,8},{1,9},{2,10},{3,11},{4,12},{5,13},{6,14},{7,15},{8,0},{9,1},... | collective-permute-start | bytes 479240 | tf_op jit(solution)/shard_map/ppermute | solution.py:339
  345.1 17.0 %collective-permute-start.43 = (bf16[624,128]{1,0:T(8,128)(2,1)S(1)}, bf16[624,128]{1,0:T(8,128)(2,1)S(1)}, u32[]{:S(2)}, u32[]{:S(2)}) collective-permute-start(bf16[624,128]{1,0:T(8,128)(2,1)S(1)} %dynamic-slice_bitcast_fusion.15), channel_id=1, source_target_pairs={{0,8},{1,9},{2,10},{3,11},{4,12},{5,13},{6,14},{7,15},{8,0},{9,1},... | collective-permute-start | bytes 479240 | tf_op jit(solution)/shard_map/ppermute | solution.py:339
  353.1 17.6 %collective-permute-start.40 = (bf16[624,128]{1,0:T(8,128)(2,1)S(1)}, bf16[624,128]{1,0:T(8,128)(2,1)S(1)}, u32[]{:S(2)}, u32[]{:S(2)}) collective-permute-start(bf16[624,128]{1,0:T(8,128)(2,1)S(1)} %dynamic-slice_bitcast_fusion.16), channel_id=1, source_target_pairs={{0,8},{1,9},{2,10},{3,11},{4,12},{5,13},{6,14},{7,15},{8,0},{9,1},... | collective-permute-start | bytes 479240 | tf_op jit(solution)/shard_map/ppermute | solution.py:339
  358.7 14.0 %collective-permute-start.56 = (f32[1280,128]{1,0:T(8,128)S(1)}, f32[1280,128]{1,0:T(8,128)S(1)}, u32[]{:S(2)}, u32[]{:S(2)}) collective-permute-start(f32[1280,128]{1,0:T(8,128)S(1)} %dynamic-slice_bitcast_fusion), channel_id=1, source_target_pairs={{0,1},{1,0},{2,3},{3,2},{4,5},{5,4},{6,7},{7,6},{8,9},{9,8},{10,11... | collective-permute-start | bytes 1966088 | tf_op jit(solution)/shard_map/ppermute | solution.py:339
  (107 other events, 1041.0 us)
